TPU v7x, 256 devices: a whole 4x4x8 slice. The times are simulated.
256 devices in a mesh: rep: 2 (over x_hi), fsdp: 128 (over x_lo, y, z, core).
Axes of the slice: x: 4 (x_hi: 2, x_lo: 2; x = x_hi * 2 + x_lo), y: 4, z: 8, core: 2. Of those that a mesh axis runs over, the one named last changes fastest.
Arguments:
- inputs: bfloat16 [163840, 8192], P(('rep', 'fsdp')), may hold values from -6 to 6
- cotangent: bfloat16 [163840, 512], P(('rep', 'fsdp')), may hold values from -0.01953125 to 0.01953125
- weight: float32 [2, 8192, 512], P('rep', 'fsdp'), may hold values from -0.0625 to 0.0625
- first: float32 [2, 8192, 512], P('rep', 'fsdp'), may hold values from -3 to 3
- second: float32 [2, 8192, 512], P('rep', 'fsdp'), may hold values from 0.05 to 2
- roster_step: int32 [2], P('rep'), may hold values from 1 to 64
- anchor: float32 [8192, 512], P('fsdp'), may hold values from -0.0625 to 0.0625
- drift: float32 [2, 8192, 512], P('rep', 'fsdp'), may hold values from -3 to 3
- momentum: float32 [8192, 512], P('fsdp'), may hold values from -3 to 3
Outputs:
- new_weight: float32 [2, 8192, 512], P('rep', 'fsdp')
- new_first: float32 [2, 8192, 512], P('rep', 'fsdp')
- new_second: float32 [2, 8192, 512], P('rep', 'fsdp')
- adam_step: float32 [2, 8192, 512], P('rep', 'fsdp')
- new_anchor: float32 [8192, 512], P('fsdp')
- new_momentum: float32 [8192, 512], P('fsdp')
All inputs are finite; a program needn't handle non-finite values.
Results may differ from a plain program's by a relative error of at most 0.00085.
Values may be sent and summed in bfloat16 or wider, within the bound.
No kernel may reach another device: no remote copies, remote signals or barrier semaphores. Data moves between devices by JAX's collectives and lax.ppermute only.
A program may use at most 128 MiB of HBM per device.

v0:
```python
import jax
import jax.numpy as jnp
from jax import lax
from jax.sharding import PartitionSpec as P


def inner_update(inputs, cotangent, weight, first, second, roster_step):
    master = weight[0]
    cast = master.astype(jnp.bfloat16)
    columns = inputs
    pre = jnp.dot(
        columns,
        lax.all_gather(cast, "fsdp", axis=0, tiled=True),
        preferred_element_type=jnp.float32,
    )
    sig = jax.nn.sigmoid(pre)
    slope = sig * (1.0 + pre * (1.0 - sig))
    error = (cotangent.astype(jnp.float32) * slope).astype(jnp.bfloat16)
    columns = inputs
    grad = lax.psum_scatter(
        lax.dot_general(
            columns, error, (((0,), (0,)), ((), ())), preferred_element_type=jnp.float32
        ),
        "fsdp",
        scatter_dimension=0,
        tiled=True,
    )
    step_f = roster_step[0].astype(jnp.float32)
    new_first = 0.9 * first[0] + 0.1 * grad
    new_second = 0.95 * second[0] + 0.05 * grad * grad
    corr_one = 1.0 - jnp.power(jnp.float32(0.9), step_f)
    corr_two = 1.0 - jnp.power(jnp.float32(0.95), step_f)
    adam_step = new_first / corr_one / (jnp.sqrt(new_second / corr_two) + 1e-08)
    new_weight = master - 0.0003 * (adam_step + 0.1 * master)
    return (new_weight[None], new_first[None], new_second[None], adam_step[None])


def nesterov(anchor_part, momentum_part, delta):
    new_momentum = 0.9 * momentum_part + delta
    new_anchor = anchor_part - 0.7 * (delta + 0.9 * new_momentum)
    return (new_anchor, new_momentum)


def outer_update(anchor, drift, momentum):
    replicas = lax.axis_size("rep")
    term = -drift[0]
    summed = lax.psum(term, "rep")
    new_anchor, new_momentum = nesterov(anchor, momentum, summed / replicas)
    return (new_anchor, new_momentum)


def on_device(inputs, cotangent, weight, first, second, roster_step, anchor, drift, momentum):
    new_weight, new_first, new_second, adam_step = inner_update(
        inputs, cotangent, weight, first, second, roster_step
    )
    new_anchor, new_momentum = outer_update(anchor, drift, momentum)
    return (new_weight, new_first, new_second, adam_step, new_anchor, new_momentum)


def solution(mesh):
    return jax.shard_map(
        on_device,
        mesh=mesh,
        in_specs=(
            P(("rep", "fsdp"), None),
            P(("rep", "fsdp"), None),
            P("rep", "fsdp", None),
            P("rep", "fsdp", None),
            P("rep", "fsdp", None),
            P("rep"),
            P("fsdp", None),
            P("rep", "fsdp", None),
            P("fsdp", None),
        ),
        out_specs=(
            P("rep", "fsdp", None),
            P("rep", "fsdp", None),
            P("rep", "fsdp", None),
            P("rep", "fsdp", None),
            P("fsdp", None),
            P("fsdp", None),
        ),
        check_vma=False,
    )
```

profile of v0, /device:TPU:4, one launch (start us, length us, event | category | flops | bytes accessed | tf_op | source)
XLA Modules:
  0.0 871.8 jit_solution(4087980806876960859)
XLA Ops:
  8.0 0.0 all-gather.2.cloned.1.call-start
  8.0 1.5 bitcast_convert_fusion
  9.6 0.0 all-gather.2.cloned.1.call-update
  9.6 0.0 all-reduce.2.cloned.1.call-start
  9.7 1.6 negate_bitcast_fusion
  11.2 0.0 all-reduce.2.cloned.1.call-update
  11.3 0.0 copy-start.1
  11.3 0.0 reduce-scatter.4.cloned.1.call-start
  11.3 222.7 %all-gather.2.cloned.1.call-done = bf16[8192,512]{1,0:T(8,128)(2,1)} async-done(((bf16[64,512]{1,0:T(8,128)(2,1)}), bf16[8192,512]{1,0:T(8,128)(2,1)}) %all-gather.2.cloned.1.call-update) | async-done | bytes 8388624 | tf_op jit(solution)/shard_map/all_gather | solution.py:13
  234.0 0.0 copy-start
  234.0 10.8 %fusion.8 = f32[640,512]{1,0:T(8,128)S(1)} fusion(bf16[640,8192]{1,0:T(8,128)(2,1)} %param.9, bf16[8192,512]{1,0:T(8,128)(2,1)} %all-gather.2.cloned.1.call-done), kind=kOutput, calls=%fused_computation.19 | convolution fusion | flops 5368709120 | bytes 20185088 | tf_op jit(solution)/shard_map/dot_general | solution.py:11
  244.8 0.0 copy-done.1
  244.8 0.0 copy-done
  244.8 10.6 %convolution_bitcast_fusion = f32[8192,512]{0,1:T(8,128)} fusion(bf16[640,8192]{1,0:T(8,128)(2,1)S(1)} %copy-done, f32[640,512]{1,0:T(8,128)S(1)} %fusion.8, bf16[640,512]{1,0:T(8,128)(2,1)S(1)} %copy-done.1), kind=kOutput, calls=%fused_computation | convolution fusion | flops 5371985920 | bytes 29229056 | tf_op jit(solution)/shard_map/dot_general | solution.py:21
  255.4 17.4 %copy.25 = f32[8192,512]{1,0:T(8,128)} copy(f32[8192,512]{0,1:T(8,128)} %convolution_bitcast_fusion) | data formatting | bytes 33554432
  272.9 0.0 copy-start.3
  272.9 0.0 copy-start.4
  272.9 0.0 copy-start.2
  272.9 0.0 copy-start.5
  272.9 0.0 copy-start.6
  272.9 0.0 reduce-scatter.4.cloned.1.call-update
  273.7 0.0 all-reduce.2.cloned.1.call-done
  273.8 0.0 copy-done.3
  273.8 0.1 copy-done.4
  273.9 1.6 multiply_subtract_fusion
  275.5 587.1 %reduce-scatter.4.cloned.1.call-done = f32[64,512]{1,0:T(8,128)} async-done(((f32[8192,512]{1,0:T(8,128)}), f32[64,512]{1,0:T(8,128)}) %reduce-scatter.4.cloned.1.call-update) | async-done | bytes 131088 | tf_op jit(solution)/shard_map/reduce_scatter | solution.py:20
  862.6 0.0 copy-done.2
  862.6 0.0 copy-done.5
  862.6 0.0 copy-done.6
  862.6 1.8 fusion.4
Async XLA Ops:
  8.0 226.0 %all-gather.2.cloned.1.call-start = ((), (), s32[]{:S(2)}) async-start(), calls=%async_computation.1 | async-start | bytes 8454144 | tf_op jit(solution)/shard_map/all_gather | solution.py:13
  9.6 264.1 %all-reduce.2.cloned.1.call-start = ((), (), s32[]{:S(2)}) async-start(), calls=%async_computation.2 | async-start | bytes 262144 | tf_op jit(solution)/shard_map/psum | solution.py:47
  11.3 233.6 %copy-start.1 = (bf16[640,512]{1,0:T(8,128)(2,1)S(1)}, bf16[640,512]{1,0:T(8,128)(2,1)}, u32[]{:S(2)}) copy-start(bf16[640,512]{1,0:T(8,128)(2,1)} %param.10) | copy-start | bytes 1966084
  11.3 851.3 %reduce-scatter.4.cloned.1.call-start = ((), (), s32[]{:S(2)}) async-start(), calls=%async_computation.3 | async-start | bytes 16908288 | tf_op jit(solution)/shard_map/reduce_scatter | solution.py:20
  234.0 10.8 %copy-start = (bf16[640,8192]{1,0:T(8,128)(2,1)S(1)}, bf16[640,8192]{1,0:T(8,128)(2,1)}, u32[]{:S(2)}) copy-start(bf16[640,8192]{1,0:T(8,128)(2,1)} %param.9) | copy-start | bytes 31457284
  272.9 0.9 copy-start.3
  272.9 1.0 copy-start.4
  272.9 589.7 %copy-start.2 = (f32[1,64,512]{2,1,0:T(8,128)S(1)}, f32[1,64,512]{2,1,0:T(8,128)}, u32[]{:S(2)}) copy-start(f32[1,64,512]{2,1,0:T(8,128)} %param.11) | copy-start | bytes 393220
  272.9 589.7 %copy-start.5 = (f32[1,64,512]{2,1,0:T(8,128)S(1)}, f32[1,64,512]{2,1,0:T(8,128)}, u32[]{:S(2)}) copy-start(f32[1,64,512]{2,1,0:T(8,128)} %param.13) | copy-start | bytes 393220
  272.9 589.7 %copy-start.6 = (f32[1,64,512]{2,1,0:T(8,128)S(1)}, f32[1,64,512]{2,1,0:T(8,128)}, u32[]{:S(2)}) copy-start(f32[1,64,512]{2,1,0:T(8,128)} %param.12) | copy-start | bytes 393220
Sparse Core Ops, SparseCore 0:
  11.3 222.6 all-gather.1
  273.1 589.4 reduce-scatter.3
Sparse Core Ops, SparseCore 1:
  13.2 35.3 all-reduce.1
where the time goes:
time: 872 us
  waiting for transfers between devices  810 us (93%)
  matrix products  21.4 us (2%)
  local copies, waits for them, and re-layouts  17.6 us (2%)
  between operations  16.3 us (2%)
    reduce_scatter x1, waiting for transfers between devices, inner_update(): lax.psum_scatter(lax.dot_general(columns, error, (((0,), (0,)), ((), ()))...  587 us
    all_gather x1, waiting for transfers between devices, inner_update(): lax.all_gather(cast, 'fsdp', axis=0, tiled=True)  223 us
    unnamed x15, local copies, waits for them, and re-layouts  17.6 us
  transfers between devices with their start and end apart: 3, of which 2 were waited for; matrix products, arithmetic and copies ran while one was open for 5% of the time, Pallas kernels for 0%

commit v1 on v0

v1 whole, which is shorter than its diff:
```python
import jax
import jax.numpy as jnp
from jax import lax
from jax.experimental import pallas as pl
from jax.experimental.pallas import tpu as pltpu
from jax.sharding import Mesh, PartitionSpec as P

AXES = ("r", "x", "y", "z", "c")
SIZES = (2, 2, 4, 8, 2)
D = 8192
HALF = 4096
KV = 512
PART = 256
LINE = 1024
TOK = 640
PART_SCALE = 256.0
PLANE_SCALE = 64.0


def swap(value, axis):
    return lax.ppermute(value, axis, [(0, 1), (1, 0)])


def corner(value, flip):
    pairs = []
    for x in range(2):
        for c in range(2):
            pairs.append((2 * x + c, 2 * ((1 - c) if flip else c) + x))
    return lax.ppermute(value, ("x", "c"), pairs)


def corner_back(value, flip):
    pairs = []
    for x in range(2):
        for c in range(2):
            pairs.append((2 * ((1 - c) if flip else c) + x, 2 * x + c))
    return lax.ppermute(value, ("x", "c"), pairs)


def shift(value, axis, size, step):
    return lax.ppermute(value, axis, [(i, (i + step) % size) for i in range(size)])


def pre_kernel(place_ref, *refs):
    columns, weights, o_ref = refs[:4], refs[4:8], refs[8]
    total = jnp.dot(columns[0][...], weights[0][...], preferred_element_type=jnp.float32)
    for column, part in zip(columns[1:], weights[1:]):
        total = total + jnp.dot(column[...], part[...], preferred_element_type=jnp.float32)
    o_ref[...] = total


def project(place, columns, weights):
    rows = 320

    def column_spec(step):
        return pl.BlockSpec((rows, LINE), lambda i, p: (i, p[0] + lax.rem(p[1] + step, 4)))

    return pl.pallas_call(
        pre_kernel,
        grid_spec=pltpu.PrefetchScalarGridSpec(
            num_scalar_prefetch=1,
            grid=(TOK // rows,),
            in_specs=[column_spec(step) for step in range(4)] + [pl.BlockSpec((LINE, PART), lambda i, p: (0, 0))] * 4,
            out_specs=pl.BlockSpec((rows, PART), lambda i, p: (i, 0)),
        ),
        out_shape=jax.ShapeDtypeStruct((TOK, PART), jnp.float32),
        compiler_params=pltpu.CompilerParams(vmem_limit_bytes=16 * 1024 * 1024),
        cost_estimate=pl.CostEstimate(
            flops=2 * TOK * HALF * PART, bytes_accessed=2 * TOK * HALF + 2 * HALF * PART + 4 * TOK * PART, transcendentals=0
        ),
    )(place, *[columns] * 4, *weights)


def error_kernel(own_ref, got_ref, cot_ref, o_ref):
    pre = own_ref[...] + got_ref[...]
    sig = jax.nn.sigmoid(pre)
    slope = sig * (1.0 + pre * (1.0 - sig))
    error = cot_ref[...].astype(jnp.float32) * slope
    o_ref[...] = error.T.astype(jnp.bfloat16)


def error_of(own, got, cotangent, part):
    return pl.pallas_call(
        error_kernel,
        grid=(1,),
        in_specs=[
            pl.BlockSpec((TOK, PART), lambda i: (0, 0)),
            pl.BlockSpec((TOK, PART), lambda i: (0, 0)),
            pl.BlockSpec((TOK, PART), lambda i: (0, part)),
        ],
        out_specs=pl.BlockSpec((PART, TOK), lambda i: (0, 0)),
        out_shape=jax.ShapeDtypeStruct((PART, TOK), jnp.bfloat16),
        compiler_params=pltpu.CompilerParams(vmem_limit_bytes=16 * 1024 * 1024),
        cost_estimate=pl.CostEstimate(flops=8 * TOK * PART, bytes_accessed=12 * TOK * PART, transcendentals=TOK * PART),
    )(own, got, cotangent)


def grad_kernel(own_ref, other_ref, xo_ref, xr_ref, eo_ref, er_ref, o_ref):
    part = jnp.dot(eo_ref[...], xo_ref[...], preferred_element_type=jnp.float32)
    part = part + jnp.dot(er_ref[...], xr_ref[...], preferred_element_type=jnp.float32)
    for k in range(o_ref.shape[0]):
        o_ref[k] = part[:, 128 * k : 128 * (k + 1)]


def gradient(own_place, other_place, own, other, err_own, err_other, step):
    width = 512
    count = LINE // width

    def column_spec(which):
        def index(i, a, b):
            p = (a, b)[which]
            return (0, (p[0] + lax.rem(p[1] + step, 4)) * count + i)

        return pl.BlockSpec((TOK, width), index)

    e_spec = pl.BlockSpec((PART, TOK), lambda i, a, b: (0, 0))
    return pl.pallas_call(
        grad_kernel,
        grid_spec=pltpu.PrefetchScalarGridSpec(
            num_scalar_prefetch=2,
            grid=(count,),
            in_specs=[column_spec(0), column_spec(1), e_spec, e_spec],
            out_specs=pl.BlockSpec((width // 128, PART, 128), lambda i, a, b: (i, 0, 0)),
        ),
        out_shape=jax.ShapeDtypeStruct((LINE // 128, PART, 128), jnp.float32),
        compiler_params=pltpu.CompilerParams(vmem_limit_bytes=16 * 1024 * 1024),
        cost_estimate=pl.CostEstimate(
            flops=4 * TOK * LINE * PART, bytes_accessed=4 * TOK * LINE + 4 * LINE * PART, transcendentals=0
        ),
    )(own_place, other_place, own, other, err_own, err_other)


def turn_kernel(x_ref, i_ref, a_ref, b_ref):
    total = i_ref[...].T * (1.0 / PLANE_SCALE)
    low, high = total[:64], total[64:]
    flag = jnp.full(low.shape, x_ref[0], jnp.int32) == 0
    a_ref[...] = jnp.where(flag, low, high)
    b_ref[...] = jnp.where(flag, high, low)


def turn(place, value):
    vmem = pl.BlockSpec(memory_space=pltpu.VMEM)
    return pl.pallas_call(
        turn_kernel,
        in_specs=[pl.BlockSpec(memory_space=pltpu.SMEM), vmem],
        out_specs=[vmem] * 2,
        out_shape=[jax.ShapeDtypeStruct((64, PART), jnp.float32)] * 2,
    )(place, value)


def adam_kernel(s_ref, a0_ref, b0_ref, a1_ref, b1_ref, w_ref, m_ref, v_ref, nw_ref, nm_ref, nv_ref, st_ref):
    grad = jnp.concatenate([a0_ref[...] + b0_ref[...], a1_ref[...] + b1_ref[...]], axis=1)
    master = w_ref[...]
    new_first = 0.9 * m_ref[...] + 0.1 * grad
    new_second = 0.95 * v_ref[...] + 0.05 * grad * grad
    step = new_first / s_ref[0] / (jnp.sqrt(new_second / s_ref[1]) + 1e-08)
    nw_ref[...] = master - 0.0003 * (step + 0.1 * master)
    nm_ref[...] = new_first
    nv_ref[...] = new_second
    st_ref[...] = step


def adam(corr, pieces, master, first, second):
    shape = jax.ShapeDtypeStruct(master.shape, jnp.float32)
    vmem = pl.BlockSpec(memory_space=pltpu.VMEM)
    return pl.pallas_call(
        adam_kernel,
        in_specs=[pl.BlockSpec(memory_space=pltpu.SMEM)] + [vmem] * 7,
        out_specs=[vmem] * 4,
        out_shape=[shape] * 4,
    )(corr, *pieces, master, first, second)


def gather_line(block):
    column = lax.all_to_all(jnp.broadcast_to(block[None], (8, 128, PART)), "z", 0, 0, tiled=True)
    return column.reshape(1024, PART)


def gather_plane(column):
    return [column] + [shift(column, "y", 4, -step) for step in (1, 2, 3)]


def scatter_plane(pieces):
    got = []
    for step in (2, 1, 3):
        got.append(shift((pieces[step] * PART_SCALE).astype(jnp.float16), "y", 4, step))
    return pieces[0] * PLANE_SCALE + sum(g.astype(jnp.float32) for g in got) * (PLANE_SCALE / PART_SCALE)


def scatter_line(line):
    return lax.all_to_all(line.astype(jnp.float16), "z", 0, 0, tiled=True)


def finish(place, got):
    a, b = turn(place, jnp.sum(got.astype(jnp.float32), axis=0))
    return corner_back(a, False), corner_back(b, True)


def on_device(inputs, cotangent, weight, first, second, roster_step, anchor, drift, momentum):
    q = lax.axis_index("c").astype(jnp.int32)
    y = lax.axis_index("y").astype(jnp.int32)
    x = lax.axis_index("x").astype(jnp.int32)
    own_place = jnp.stack([q * 4, y])
    other_place = jnp.stack([y * 0, y])
    x_place = x.reshape(1)
    at_zero = x == 0
    master = weight[0]
    cast = master.astype(jnp.bfloat16)
    a = corner(cast, False)
    b = corner(cast, True)
    send = lax.dynamic_slice(inputs, (0, (1 - q) * HALF), (TOK, HALF))
    block = jnp.concatenate([jnp.where(at_zero, a, b), jnp.where(at_zero, b, a)], axis=0)
    block, send = lax.optimization_barrier((block, send))
    other = swap(send, "c")
    drift_other = swap(drift[0], "r")

    line0 = gather_line(block[:, :PART])
    line0, block, drift_other = lax.optimization_barrier((line0, block, drift_other))
    line1 = gather_line(block[:, PART:])

    def compute(line, part):
        half = gather_plane(line)
        pre_other = project(other_place, other, half)
        got = swap(pre_other, "c")
        pre = project(own_place, inputs, half)
        error = error_of(pre, got, cotangent, part)
        error_other = swap(error, "c")
        return [gradient(own_place, other_place, inputs, other, error, error_other, step) for step in range(4)]

    g0 = scatter_plane(compute(line0, 0))
    g1 = scatter_plane(compute(line1, 1))
    t0 = finish(x_place, scatter_line(g0))
    t1 = finish(x_place, scatter_line(g1))

    step_f = roster_step[0].astype(jnp.float32)
    corr = jnp.stack([1.0 - jnp.power(jnp.float32(0.9), step_f), 1.0 - jnp.power(jnp.float32(0.95), step_f)])
    new_weight, new_first, new_second, adam_step = adam(corr, t0 + t1, master, first[0], second[0])

    delta = -(drift[0] + drift_other) / 2
    new_momentum = 0.9 * momentum + delta
    new_anchor = anchor - 0.7 * (delta + 0.9 * new_momentum)
    return (new_weight[None], new_first[None], new_second[None], adam_step[None], new_anchor, new_momentum)


def solution(mesh):
    fine = Mesh(mesh.devices.reshape(SIZES), AXES)
    every = ("r", "x", "y", "z", "c")
    fsdp = ("x", "y", "z", "c")
    return jax.shard_map(
        on_device,
        mesh=fine,
        in_specs=(
            P(every, None),
            P(every, None),
            P("r", fsdp, None),
            P("r", fsdp, None),
            P("r", fsdp, None),
            P("r"),
            P(fsdp, None),
            P("r", fsdp, None),
            P(fsdp, None),
        ),
        out_specs=(
            P("r", fsdp, None),
            P("r", fsdp, None),
            P("r", fsdp, None),
            P("r", fsdp, None),
            P(fsdp, None),
            P(fsdp, None),
        ),
        check_vma=False,
    )
```

time: 872 us -> 211 us (0.24)
  waiting for transfers between devices: 810 us -> 74.2 us
  starting transfers between devices: 0.12 us -> 56.1 us
  Pallas kernels: 0 us -> 48.2 us
  matrix products: 21.4 us -> 0 us
  between operations: 16.3 us -> 1.7 us
    reduce_scatter x1 -> x0, waiting for transfers between devices: 587 us -> none  [inner_update(): lax.psum_scatter(lax.dot_general(columns, error, (((0,), (0,)), ((), ()))...]
    all_gather x1 -> x0, waiting for transfers between devices: 223 us -> none  [inner_update(): lax.all_gather(cast, 'fsdp', axis=0, tiled=True)]
    pallas_call x0 -> x17, Pallas kernels: none -> 48.2 us  [the longest x8 23.1 us: gradient(): pl.pallas_call(grad_kernel, grid_spec=pltpu.PrefetchScalarGridSpec(num_sc...]
    ppermute x0 -> x24, waiting for transfers between devices: none -> 42.5 us  [the longest x12 34.7 us: shift(): lax.ppermute(value, axis, [(i, (i + step) % size) for i in range(size)])]
    all_to_all x0 -> x4, waiting for transfers between devices: none -> 31.6 us  [the longest x2 24.1 us: gather_line(): lax.all_to_all(jnp.broadcast_to(block[None], (8, 128, PART)), 'z', 0, 0,...]
    ppermute x0 -> x24, starting transfers between devices: none -> 30.7 us  [the longest x12 19.2 us: shift(): lax.ppermute(value, axis, [(i, (i + step) % size) for i in range(size)])]
    all_to_all x0 -> x4, starting transfers between devices: none -> 25.4 us  [the longest x2 13.4 us: scatter_line(): return lax.all_to_all(line.astype(jnp.float16), 'z', 0, 0, tiled=True)]
    dot_general x2 -> x0, matrix products: 21.4 us -> none  [the longest x1 10.8 us: inner_update(): jnp.dot(columns, lax.all_gather(cast, 'fsdp', axis=0, tiled=True), prefer...]
  transfers between devices with their start and end apart: 3 -> 28, of which waited for: 2 -> 10; matrix products, arithmetic and copies ran while one was open for 5% -> 7% of each run, Pallas kernels for 0% -> 22%
where the time goes in v1:
time: 211 us; the launch traced here: 209 us
  waiting for transfers between devices  74.2 us (35%)
  starting transfers between devices  56.1 us (27%)
  Pallas kernels  48.2 us (23%)
  local copies, waits for them, and re-layouts  19.9 us (9%)
  other arithmetic  9.04 us (4%)
    ppermute x12, waiting for transfers between devices, shift(): lax.ppermute(value, axis, [(i, (i + step) % size) for i in range(size)])  34.7 us
    all_to_all x2, waiting for transfers between devices, gather_line(): lax.all_to_all(jnp.broadcast_to(block[None], (8, 128, PART)), 'z', 0, 0,...  24.1 us
    pallas_call x8, Pallas kernels, gradient(): pl.pallas_call(grad_kernel, grid_spec=pltpu.PrefetchScalarGridSpec(num_sc...  23.1 us
    ppermute x12, starting transfers between devices, shift(): lax.ppermute(value, axis, [(i, (i + step) % size) for i in range(size)])  19.2 us
    pallas_call x4, Pallas kernels, project(): pl.pallas_call(pre_kernel, grid_spec=pltpu.PrefetchScalarGridSpec(num_sca...  17 us
    all_to_all x2, starting transfers between devices, scatter_line(): return lax.all_to_all(line.astype(jnp.float16), 'z', 0, 0, tiled=True)  13.4 us
    unnamed x26, local copies, waits for them, and re-layouts  12.7 us
    all_to_all x2, starting transfers between devices, gather_line(): lax.all_to_all(jnp.broadcast_to(block[None], (8, 128, PART)), 'z', 0, 0,...  12 us
  transfers between devices with their start and end apart: 28, of which 10 were waited for; matrix products, arithmetic and copies ran while one was open for 7% of the time, Pallas kernels for 22%

profile of v1, /device:TPU:4, one launch (start us, length us, event | category | flops | bytes accessed | tf_op | source)
XLA Modules:
  0.0 209.1 jit_solution(17659981307760020349)
XLA Ops:
  0.6 0.9 bitcast_convert_fusion
  1.6 0.7 collective-permute-start
  2.2 2.8 %collective-permute-start.1 = (bf16[64,512]{1,0:T(8,128)(2,1)S(1)}, bf16[64,512]{1,0:T(8,128)(2,1)S(1)}, u32[]{:S(2)}, u32[]{:S(2)}) collective-permute-start(bf16[64,512]{1,0:T(8,128)(2,1)S(1)} %bitcast_convert_fusion), channel_id=1, source_target_pairs={{0,64},{1,0},{64,65},{65,1},{2,66},{3,2},{66,67},{67,3},{4,68},{5,... | collective-permute-start | bytes 196616 | tf_op jit(solution)/shard_map/ppermute | solution.py:29
  5.0 5.5 %constant_dynamic-slice_fusion = bf16[640,4096]{1,0:T(8,128)(2,1)} fusion(bf16[640,8192]{1,0:T(8,128)(2,1)} %xo_ref.15, s32[]{:T(128)S(6)} %select_n.18), kind=kLoop, calls=%fused_computation.19 | loop fusion | bytes 10485764 | tf_op jit(solution)/shard_map/dynamic_slice | solution.py:211
  10.7 0.8 broadcast_in_dim.24
  11.6 8.5 %all-to-all-start = ((bf16[8,128,256]{2,1,0:T(8,128)(2,1)}), bf16[8,128,256]{2,1,0:T(8,128)(2,1)S(1)}, u32[]{:S(2)}, u32[]{:S(2)}) async-start(bf16[8,128,256]{2,1,0:T(8,128)(2,1)} %broadcast_in_dim.24), calls=%async_computation | async-start | bytes 1048576 | tf_op jit(solution)/shard_map/all_to_all | solution.py:175
  20.0 0.8 collective-permute-start.3
  20.8 6.5 %collective-permute-done.3 = f32[64,512]{1,0:T(8,128)} collective-permute-done((f32[64,512]{1,0:T(8,128)S(1)}, f32[64,512]{1,0:T(8,128)}, u32[]{:S(2)}, u32[]{:S(2)}) %collective-permute-start.3) | collective-permute-done | bytes 131104 | tf_op jit(solution)/shard_map/ppermute | solution.py:21
  27.3 10.9 %all-to-all-done = bf16[8,128,256]{2,1,0:T(8,128)(2,1)S(1)} async-done(((bf16[8,128,256]{2,1,0:T(8,128)(2,1)}), bf16[8,128,256]{2,1,0:T(8,128)(2,1)S(1)}, u32[]{:S(2)}, u32[]{:S(2)}) %all-to-all-start) | async-done | bytes 524320 | tf_op jit(solution)/shard_map/all_to_all | solution.py:175
  38.2 0.8 broadcast_in_dim.25
  39.0 3.5 %all-to-all-start.2 = ((bf16[8,128,256]{2,1,0:T(8,128)(2,1)}), bf16[8,128,256]{2,1,0:T(8,128)(2,1)S(1)}, u32[]{:S(2)}, u32[]{:S(2)}) async-start(bf16[8,128,256]{2,1,0:T(8,128)(2,1)} %broadcast_in_dim.25), calls=%async_computation.2 | async-start | bytes 1048576 | tf_op jit(solution)/shard_map/all_to_all | solution.py:175
  42.5 3.1 %collective-permute-start.4 = (bf16[1024,256]{1,0:T(8,128)(2,1)S(1)}, bf16[1024,256]{1,0:T(8,128)(2,1)S(1)}, u32[]{:S(2)}, u32[]{:S(2)}) collective-permute-start(bf16[1024,256]{1,0:T(8,128)(2,1)S(1)} %bitcast.17), channel_id=1, source_target_pairs={{0,48},{16,0},{32,16},{48,32},{1,49},{17,1},{33,17},{49,33},{2,50}... | collective-permute-start | bytes 1572872 | tf_op jit(solution)/shard_map/ppermute | solution.py:41
  45.6 0.6 collective-permute-start.5
  46.3 1.0 collective-permute-start.6
  47.2 13.2 %all-to-all-done.2 = bf16[8,128,256]{2,1,0:T(8,128)(2,1)S(1)} async-done(((bf16[8,128,256]{2,1,0:T(8,128)(2,1)}), bf16[8,128,256]{2,1,0:T(8,128)(2,1)S(1)}, u32[]{:S(2)}, u32[]{:S(2)}) %all-to-all-start.2) | async-done | bytes 524320 | tf_op jit(solution)/shard_map/all_to_all | solution.py:175
  60.4 3.0 %collective-permute-start.14 = (bf16[1024,256]{1,0:T(8,128)(2,1)S(1)}, bf16[1024,256]{1,0:T(8,128)(2,1)S(1)}, u32[]{:S(2)}, u32[]{:S(2)}) collective-permute-start(bf16[1024,256]{1,0:T(8,128)(2,1)S(1)} %bitcast.22), channel_id=1, source_target_pairs={{0,48},{16,0},{32,16},{48,32},{1,49},{17,1},{33,17},{49,33},{2,50}... | collective-permute-start | bytes 1572872 | tf_op jit(solution)/shard_map/ppermute | solution.py:41
  63.5 5.7 %collective-permute-done.4.refs_5_ = bf16[1024,256]{1,0:T(8,128)(2,1)S(1)} collective-permute-done((bf16[1024,256]{1,0:T(8,128)(2,1)S(1)}, bf16[1024,256]{1,0:T(8,128)(2,1)S(1)}, u32[]{:S(2)}, u32[]{:S(2)}) %collective-permute-start.4) | collective-permute-done | bytes 524320 | tf_op jit(solution)/shard_map/ppermute | solution.py:41
  69.2 4.5 %collective-permute-start.16 = (bf16[1024,256]{1,0:T(8,128)(2,1)S(1)}, bf16[1024,256]{1,0:T(8,128)(2,1)}, u32[]{:S(2)}, u32[]{:S(2)}) collective-permute-start(bf16[1024,256]{1,0:T(8,128)(2,1)S(1)} %bitcast.24), channel_id=1, source_target_pairs={{0,16},{16,32},{32,48},{48,0},{1,17},{17,33},{33,49},{49,1},{2,18}... | collective-permute-start | bytes 1572872 | tf_op jit(solution)/shard_map/ppermute | solution.py:41
  73.8 4.8 %shard_map.137 = f32[640,256]{1,0:T(8,128)} custom-call(s32[2]{0:T(128)S(1)} %pad_add_fusion.1.place_ref.other_ref, bf16[640,4096]{1,0:T(8,128)(2,1)} %collective-permute-done.2.refs_0_.refs_1_.refs_2_.refs_3_.xr_ref, bf16[640,4096]{1,0:T(8,128)(2,1)} %collective-permute-done.2.refs_0_.refs_1_.refs_2_.refs_3_.xr_ref, ...), custom_call_target="tpu_custom_call" | custom-call | flops 1342177280 | bytes 7995392 | tf_op jit(solution)/shard_map/pallas_call | solution.py:58
  78.6 12.1 %collective-permute-done.14.refs_5_ = bf16[1024,256]{1,0:T(8,128)(2,1)S(1)} collective-permute-done((bf16[1024,256]{1,0:T(8,128)(2,1)S(1)}, bf16[1024,256]{1,0:T(8,128)(2,1)S(1)}, u32[]{:S(2)}, u32[]{:S(2)}) %collective-permute-start.14) | collective-permute-done | bytes 524320 | tf_op jit(solution)/shard_map/ppermute | solution.py:41
  90.7 3.8 %collective-permute-done.16.refs_7_ = bf16[1024,256]{1,0:T(8,128)(2,1)} collective-permute-done((bf16[1024,256]{1,0:T(8,128)(2,1)S(1)}, bf16[1024,256]{1,0:T(8,128)(2,1)}, u32[]{:S(2)}, u32[]{:S(2)}) %collective-permute-start.16) | collective-permute-done | bytes 524320 | tf_op jit(solution)/shard_map/ppermute | solution.py:41
  94.5 5.3 %shard_map.145 = f32[640,256]{1,0:T(8,128)} custom-call(s32[2]{0:T(128)S(1)} %pad_add_fusion.1.place_ref.other_ref, bf16[640,4096]{1,0:T(8,128)(2,1)} %collective-permute-done.2.refs_0_.refs_1_.refs_2_.refs_3_.xr_ref, bf16[640,4096]{1,0:T(8,128)(2,1)} %collective-permute-done.2.refs_0_.refs_1_.refs_2_.refs_3_.xr_ref, ...), custom_call_target="tpu_custom_call" | custom-call | flops 1342177280 | bytes 7995392 | tf_op jit(solution)/shard_map/pallas_call | solution.py:58
  100.0 4.0 %copy-done = bf16[640,8192]{1,0:T(8,128)(2,1)S(1)} copy-done((bf16[640,8192]{1,0:T(8,128)(2,1)S(1)}, bf16[640,8192]{1,0:T(8,128)(2,1)}, u32[]{:S(2)}) %copy-start) | copy-done | bytes 10485784
  104.0 2.8 %shard_map.136.own_ref = f32[640,256]{1,0:T(8,128)S(1)} custom-call(s32[2]{0:T(128)S(1)} %pad_add_fusion.place_ref.own_ref, bf16[640,8192]{1,0:T(8,128)(2,1)S(1)} %copy-done, bf16[640,8192]{1,0:T(8,128)(2,1)S(1)} %copy-done, bf16[640,8192]{1,0:T(8,128)(2,1)S(1)} %copy-done, bf16[640,8192]{1,0:T(8,128)(2,1)S(1)} %copy-done, bf16[1024,256]{1,0:T(8,128)(2,1)S(1)} %bitcast.21, ...), custom_call_target="tpu_custom_call" | custom-call | flops 1342177280 | bytes 7995392 | tf_op jit(solution)/shard_map/pallas_call | solution.py:58
  106.8 1.4 shard_map.138.eo_ref
  108.1 0.8 collective-permute-start.8
  108.9 4.0 %copy-done.1 = bf16[640,8192]{1,0:T(8,128)(2,1)S(1)} copy-done((bf16[640,8192]{1,0:T(8,128)(2,1)S(1)}, bf16[640,8192]{1,0:T(8,128)(2,1)}, u32[]{:S(2)}) %copy-start.1) | copy-done | bytes 10485784
  112.9 4.1 %shard_map.144.own_ref = f32[640,256]{1,0:T(8,128)S(1)} custom-call(s32[2]{0:T(128)S(1)} %pad_add_fusion.place_ref.own_ref, bf16[640,8192]{1,0:T(8,128)(2,1)S(1)} %copy-done.1, bf16[640,8192]{1,0:T(8,128)(2,1)S(1)} %copy-done.1, bf16[640,8192]{1,0:T(8,128)(2,1)S(1)} %copy-done.1, bf16[640,8192]{1,0:T(8,128)(2,1)S(1)} %copy-done.1, ...), custom_call_target="tpu_custom_call" | custom-call | flops 1342177280 | bytes 7995392 | tf_op jit(solution)/shard_map/pallas_call | solution.py:58
  117.1 1.4 shard_map.146.eo_ref
  118.6 2.9 %shard_map.142 = f32[8,256,128]{2,1,0:T(8,128)S(1)} custom-call(s32[2]{0:T(128)S(1)} %pad_add_fusion.place_ref.own_ref, s32[2]{0:T(128)S(1)} %pad_add_fusion.1.place_ref.other_ref, bf16[640,8192]{1,0:T(8,128)(2,1)S(1)} %copy-done.2, bf16[640,4096]{1,0:T(8,128)(2,1)} %collective-permute-done.2.refs_0_.refs_1_.refs_2_.refs_3_.xr_ref, ...), custom_call_target="tpu_custom_call" | custom-call | flops 671088640 | bytes 3670016 | tf_op jit(solution)/shard_map/pallas_call | solution.py:117
  121.6 0.7 collective-permute-start.11
  122.3 2.9 %shard_map.141 = f32[8,256,128]{2,1,0:T(8,128)S(1)} custom-call(s32[2]{0:T(128)S(1)} %pad_add_fusion.place_ref.own_ref, s32[2]{0:T(128)S(1)} %pad_add_fusion.1.place_ref.other_ref, bf16[640,8192]{1,0:T(8,128)(2,1)S(1)} %copy-done.2, bf16[640,4096]{1,0:T(8,128)(2,1)} %collective-permute-done.2.refs_0_.refs_1_.refs_2_.refs_3_.xr_ref, ...), custom_call_target="tpu_custom_call" | custom-call | flops 671088640 | bytes 3670016 | tf_op jit(solution)/shard_map/pallas_call | solution.py:117
  125.3 1.5 collective-permute-start.10
  126.8 2.9 %shard_map.140 = f32[8,256,128]{2,1,0:T(8,128)S(1)} custom-call(s32[2]{0:T(128)S(1)} %pad_add_fusion.place_ref.own_ref, s32[2]{0:T(128)S(1)} %pad_add_fusion.1.place_ref.other_ref, bf16[640,8192]{1,0:T(8,128)(2,1)S(1)} %copy-done.2, bf16[640,4096]{1,0:T(8,128)(2,1)} %collective-permute-done.2.refs_0_.refs_1_.refs_2_.refs_3_.xr_ref, ...), custom_call_target="tpu_custom_call" | custom-call | flops 671088640 | bytes 3670016 | tf_op jit(solution)/shard_map/pallas_call | solution.py:117
  129.8 0.8 collective-permute-start.9
  130.6 2.9 %shard_map.150 = f32[8,256,128]{2,1,0:T(8,128)S(1)} custom-call(s32[2]{0:T(128)S(1)} %pad_add_fusion.place_ref.own_ref, s32[2]{0:T(128)S(1)} %pad_add_fusion.1.place_ref.other_ref, bf16[640,8192]{1,0:T(8,128)(2,1)S(1)} %copy-done.2, bf16[640,4096]{1,0:T(8,128)(2,1)} %collective-permute-done.2.refs_0_.refs_1_.refs_2_.refs_3_.xr_ref, ...), custom_call_target="tpu_custom_call" | custom-call | flops 671088640 | bytes 3670016 | tf_op jit(solution)/shard_map/pallas_call | solution.py:117
  133.6 2.1 %collective-permute-start.21 = (f16[8,256,128]{2,1,0:T(8,128)(2,1)S(1)}, f16[8,256,128]{2,1,0:T(8,128)(2,1)}, u32[]{:S(2)}, u32[]{:S(2)}) collective-permute-start(f16[8,256,128]{2,1,0:T(8,128)(2,1)S(1)} %multiply_convert_fusion), channel_id=1, source_target_pairs={{0,48},{16,0},{32,16},{48,32},{1,49},{17,1},{33,17},{49,33},{2,50}... | collective-permute-start | bytes 1572872 | tf_op jit(solution)/shard_map/ppermute | solution.py:41
  135.7 2.9 %shard_map.149 = f32[8,256,128]{2,1,0:T(8,128)S(1)} custom-call(s32[2]{0:T(128)S(1)} %pad_add_fusion.place_ref.own_ref, s32[2]{0:T(128)S(1)} %pad_add_fusion.1.place_ref.other_ref, bf16[640,8192]{1,0:T(8,128)(2,1)S(1)} %copy-done.2, bf16[640,4096]{1,0:T(8,128)(2,1)} %collective-permute-done.2.refs_0_.refs_1_.refs_2_.refs_3_.xr_ref, ...), custom_call_target="tpu_custom_call" | custom-call | flops 671088640 | bytes 3670016 | tf_op jit(solution)/shard_map/pallas_call | solution.py:117
  138.7 0.1 collective-permute-start.20
  138.8 2.9 %shard_map.139 = f32[8,256,128]{2,1,0:T(8,128)S(1)} custom-call(s32[2]{0:T(128)S(1)} %pad_add_fusion.place_ref.own_ref, s32[2]{0:T(128)S(1)} %pad_add_fusion.1.place_ref.other_ref, bf16[640,8192]{1,0:T(8,128)(2,1)S(1)} %copy-done.2, bf16[640,4096]{1,0:T(8,128)(2,1)} %collective-permute-done.2.refs_0_.refs_1_.refs_2_.refs_3_.xr_ref, ...), custom_call_target="tpu_custom_call" | custom-call | flops 671088640 | bytes 3670016 | tf_op jit(solution)/shard_map/pallas_call | solution.py:117
  141.7 2.9 %shard_map.148 = f32[8,256,128]{2,1,0:T(8,128)S(1)} custom-call(s32[2]{0:T(128)S(1)} %pad_add_fusion.place_ref.own_ref, s32[2]{0:T(128)S(1)} %pad_add_fusion.1.place_ref.other_ref, bf16[640,8192]{1,0:T(8,128)(2,1)S(1)} %copy-done.2, bf16[640,4096]{1,0:T(8,128)(2,1)} %collective-permute-done.2.refs_0_.refs_1_.refs_2_.refs_3_.xr_ref, ...), custom_call_target="tpu_custom_call" | custom-call | flops 671088640 | bytes 3670016 | tf_op jit(solution)/shard_map/pallas_call | solution.py:117
  144.6 8.0 %collective-permute-done.10 = f16[8,256,128]{2,1,0:T(8,128)(2,1)S(1)} collective-permute-done((f16[8,256,128]{2,1,0:T(8,128)(2,1)S(1)}, f16[8,256,128]{2,1,0:T(8,128)(2,1)S(1)}, u32[]{:S(2)}, u32[]{:S(2)}) %collective-permute-start.10) | collective-permute-done | bytes 524320 | tf_op jit(solution)/shard_map/ppermute | solution.py:41
  152.6 1.1 add_convert_fusion.1
  153.8 6.8 %all-to-all-start.1 = ((f16[8,256,128]{2,1,0:T(8,128)(2,1)}), f16[8,256,128]{2,1,0:T(8,128)(2,1)S(1)}, u32[]{:S(2)}, u32[]{:S(2)}) async-start(f16[8,256,128]{2,1,0:T(8,128)(2,1)} %add_convert_fusion.1), calls=%async_computation.1 | async-start | bytes 1048576 | tf_op jit(solution)/shard_map/all_to_all | solution.py:191
  160.7 1.8 collective-permute-start.19
  162.5 4.0 %copy-done.3 = bf16[640,8192]{1,0:T(8,128)(2,1)S(1)} copy-done((bf16[640,8192]{1,0:T(8,128)(2,1)S(1)}, bf16[640,8192]{1,0:T(8,128)(2,1)}, u32[]{:S(2)}) %copy-start.3) | copy-done | bytes 10485784
  166.5 2.9 %shard_map.147 = f32[8,256,128]{2,1,0:T(8,128)S(1)} custom-call(s32[2]{0:T(128)S(1)} %pad_add_fusion.place_ref.own_ref, s32[2]{0:T(128)S(1)} %pad_add_fusion.1.place_ref.other_ref, bf16[640,8192]{1,0:T(8,128)(2,1)S(1)} %copy-done.3, bf16[640,4096]{1,0:T(8,128)(2,1)} %collective-permute-done.2.refs_0_.refs_1_.refs_2_.refs_3_.xr_ref, ...), custom_call_target="tpu_custom_call" | custom-call | flops 671088640 | bytes 3670016 | tf_op jit(solution)/shard_map/pallas_call | solution.py:117
  169.4 5.1 %collective-permute-done.20 = f16[8,256,128]{2,1,0:T(8,128)(2,1)} collective-permute-done((f16[8,256,128]{2,1,0:T(8,128)(2,1)S(1)}, f16[8,256,128]{2,1,0:T(8,128)(2,1)}, u32[]{:S(2)}, u32[]{:S(2)}) %collective-permute-start.20) | collective-permute-done | bytes 524320 | tf_op jit(solution)/shard_map/ppermute | solution.py:41
  174.5 2.4 %add_convert_fusion = f16[8,256,128]{2,1,0:T(8,128)(2,1)} fusion(f16[8,256,128]{2,1,0:T(8,128)(2,1)} %collective-permute-done.21, f16[8,256,128]{2,1,0:T(8,128)(2,1)} %collective-permute-done.20, f16[8,256,128]{2,1,0:T(8,128)(2,1)S(1)} %collective-permute-done.19, f32[8,256,128]{2,1,0:T(8,128)S(1)} %shard_map.147), kind=kLoop, calls=%fused_computation.1 | loop fusion | flops 2359296 | bytes 3145728 | tf_op jit(solution)/shard_map/convert_element_type | solution.py:191
  176.9 6.7 %all-to-all-start.3 = ((f16[8,256,128]{2,1,0:T(8,128)(2,1)}), f16[8,256,128]{2,1,0:T(8,128)(2,1)S(1)}, u32[]{:S(2)}, u32[]{:S(2)}) async-start(f16[8,256,128]{2,1,0:T(8,128)(2,1)} %add_convert_fusion), calls=%async_computation.3 | async-start | bytes 1048576 | tf_op jit(solution)/shard_map/all_to_all | solution.py:191
  184.2 0.7 pad_maximum_fusion.1.s_ref
  184.9 0.7 convert_reduce_fusion.1.i_ref
  185.6 1.7 shard_map.143
  187.3 1.5 collective-permute-start.12
  188.8 1.7 collective-permute-start.13
  190.4 7.5 %all-to-all-done.3 = f16[8,256,128]{2,1,0:T(8,128)(2,1)S(1)} async-done(((f16[8,256,128]{2,1,0:T(8,128)(2,1)}), f16[8,256,128]{2,1,0:T(8,128)(2,1)S(1)}, u32[]{:S(2)}, u32[]{:S(2)}) %all-to-all-start.3) | async-done | bytes 524320 | tf_op jit(solution)/shard_map/all_to_all | solution.py:191
  198.0 0.7 convert_reduce_fusion.i_ref
  198.7 1.7 shard_map.151
  200.4 1.5 collective-permute-start.22
  201.8 1.7 collective-permute-start.23
  203.5 1.6 multiply_subtract_fusion
  205.2 1.2 collective-permute-done.23.b1_ref
  206.4 0.6 copy-done.12
  207.1 2.0 shard_map.152
  (57 shorter events, 1.1 us)
Async XLA Ops:
  1.6 9.0 %collective-permute-start = (bf16[64,512]{1,0:T(8,128)(2,1)S(1)}, bf16[64,512]{1,0:T(8,128)(2,1)S(1)}, u32[]{:S(2)}, u32[]{:S(2)}) collective-permute-start(bf16[64,512]{1,0:T(8,128)(2,1)S(1)} %bitcast_convert_fusion), channel_id=1, source_target_pairs={{0,0},{1,64},{64,1},{65,65},{2,2},{3,66},{66,3},{67,67},{4,4},{5,6... | collective-permute-start | bytes 196616 | tf_op jit(solution)/shard_map/ppermute | solution.py:29
  2.2 8.4 %collective-permute-start.1 = (bf16[64,512]{1,0:T(8,128)(2,1)S(1)}, bf16[64,512]{1,0:T(8,128)(2,1)S(1)}, u32[]{:S(2)}, u32[]{:S(2)}) collective-permute-start(bf16[64,512]{1,0:T(8,128)(2,1)S(1)} %bitcast_convert_fusion), channel_id=1, source_target_pairs={{0,64},{1,0},{64,65},{65,1},{2,66},{3,2},{66,67},{67,3},{4,68},{5,... | collective-permute-start | bytes 196616 | tf_op jit(solution)/shard_map/ppermute | solution.py:29
  5.0 15.0 %copy-start.6 = (f32[1,64,512]{2,1,0:T(8,128)S(1)}, f32[1,64,512]{2,1,0:T(8,128)}, u32[]{:S(2)}) copy-start(f32[1,64,512]{2,1,0:T(8,128)} %param.16) | copy-start | bytes 393220
  10.6 63.2 %collective-permute-start.2 = (bf16[640,4096]{1,0:T(8,128)(2,1)}, bf16[640,4096]{1,0:T(8,128)(2,1)}, u32[]{:S(2)}, u32[]{:S(2)}) collective-permute-start(bf16[640,4096]{1,0:T(8,128)(2,1)} %constant_dynamic-slice_fusion), channel_id=1, source_target_pairs={{0,1},{1,0},{2,3},{3,2},{4,5},{5,4},{6,7},{7,6},{8,9},{9,8},{10,11... | collective-permute-start | bytes 15728648 | tf_op jit(solution)/shard_map/ppermute | solution.py:21
  11.6 26.7 %all-to-all-start = ((bf16[8,128,256]{2,1,0:T(8,128)(2,1)}), bf16[8,128,256]{2,1,0:T(8,128)(2,1)S(1)}, u32[]{:S(2)}, u32[]{:S(2)}) async-start(bf16[8,128,256]{2,1,0:T(8,128)(2,1)} %broadcast_in_dim.24), calls=%async_computation | async-start | bytes 1048576 | tf_op jit(solution)/shard_map/all_to_all | solution.py:175
  20.0 7.3 %collective-permute-start.3 = (f32[64,512]{1,0:T(8,128)S(1)}, f32[64,512]{1,0:T(8,128)}, u32[]{:S(2)}, u32[]{:S(2)}) collective-permute-start(f32[64,512]{1,0:T(8,128)S(1)} %bitcast.28), channel_id=1, source_target_pairs={{0,128},{128,0},{1,129},{129,1},{2,130},{130,2},{3,131},{131,3},{4... | collective-permute-start | bytes 393224 | tf_op jit(solution)/shard_map/ppermute | solution.py:21
  39.0 21.4 %all-to-all-start.2 = ((bf16[8,128,256]{2,1,0:T(8,128)(2,1)}), bf16[8,128,256]{2,1,0:T(8,128)(2,1)S(1)}, u32[]{:S(2)}, u32[]{:S(2)}) async-start(bf16[8,128,256]{2,1,0:T(8,128)(2,1)} %broadcast_in_dim.25), calls=%async_computation.2 | async-start | bytes 1048576 | tf_op jit(solution)/shard_map/all_to_all | solution.py:175
  42.5 26.6 %collective-permute-start.4 = (bf16[1024,256]{1,0:T(8,128)(2,1)S(1)}, bf16[1024,256]{1,0:T(8,128)(2,1)S(1)}, u32[]{:S(2)}, u32[]{:S(2)}) collective-permute-start(bf16[1024,256]{1,0:T(8,128)(2,1)S(1)} %bitcast.17), channel_id=1, source_target_pairs={{0,48},{16,0},{32,16},{48,32},{1,49},{17,1},{33,17},{49,33},{2,50}... | collective-permute-start | bytes 1572872 | tf_op jit(solution)/shard_map/ppermute | solution.py:41
  45.6 23.5 %collective-permute-start.5 = (bf16[1024,256]{1,0:T(8,128)(2,1)S(1)}, bf16[1024,256]{1,0:T(8,128)(2,1)S(1)}, u32[]{:S(2)}, u32[]{:S(2)}) collective-permute-start(bf16[1024,256]{1,0:T(8,128)(2,1)S(1)} %bitcast.18), channel_id=1, source_target_pairs={{0,32},{16,48},{32,0},{48,16},{1,33},{17,49},{33,1},{49,17},{2,34}... | collective-permute-start | bytes 1572872 | tf_op jit(solution)/shard_map/ppermute | solution.py:41
  46.3 27.5 %collective-permute-start.6 = (bf16[1024,256]{1,0:T(8,128)(2,1)S(1)}, bf16[1024,256]{1,0:T(8,128)(2,1)S(1)}, u32[]{:S(2)}, u32[]{:S(2)}) collective-permute-start(bf16[1024,256]{1,0:T(8,128)(2,1)S(1)} %bitcast.19), channel_id=1, source_target_pairs={{0,16},{16,32},{32,48},{48,0},{1,17},{17,33},{33,49},{49,1},{2,18}... | collective-permute-start | bytes 1572872 | tf_op jit(solution)/shard_map/ppermute | solution.py:41
  60.4 30.3 %collective-permute-start.14 = (bf16[1024,256]{1,0:T(8,128)(2,1)S(1)}, bf16[1024,256]{1,0:T(8,128)(2,1)S(1)}, u32[]{:S(2)}, u32[]{:S(2)}) collective-permute-start(bf16[1024,256]{1,0:T(8,128)(2,1)S(1)} %bitcast.22), channel_id=1, source_target_pairs={{0,48},{16,0},{32,16},{48,32},{1,49},{17,1},{33,17},{49,33},{2,50}... | collective-permute-start | bytes 1572872 | tf_op jit(solution)/shard_map/ppermute | solution.py:41
  69.2 21.6 %collective-permute-start.15 = (bf16[1024,256]{1,0:T(8,128)(2,1)S(1)}, bf16[1024,256]{1,0:T(8,128)(2,1)}, u32[]{:S(2)}, u32[]{:S(2)}) collective-permute-start(bf16[1024,256]{1,0:T(8,128)(2,1)S(1)} %bitcast.23), channel_id=1, source_target_pairs={{0,32},{16,48},{32,0},{48,16},{1,33},{17,49},{33,1},{49,17},{2,34}... | collective-permute-start | bytes 1572872 | tf_op jit(solution)/shard_map/ppermute | solution.py:41
  69.2 25.4 %collective-permute-start.16 = (bf16[1024,256]{1,0:T(8,128)(2,1)S(1)}, bf16[1024,256]{1,0:T(8,128)(2,1)}, u32[]{:S(2)}, u32[]{:S(2)}) collective-permute-start(bf16[1024,256]{1,0:T(8,128)(2,1)S(1)} %bitcast.24), channel_id=1, source_target_pairs={{0,16},{16,32},{32,48},{48,0},{1,17},{17,33},{33,49},{49,1},{2,18}... | collective-permute-start | bytes 1572872 | tf_op jit(solution)/shard_map/ppermute | solution.py:41
  78.6 28.1 %collective-permute-start.7 = (f32[640,256]{1,0:T(8,128)}, f32[640,256]{1,0:T(8,128)}, u32[]{:S(2)}, u32[]{:S(2)}) collective-permute-start(f32[640,256]{1,0:T(8,128)} %shard_map.137), channel_id=1, source_target_pairs={{0,1},{1,0},{2,3},{3,2},{4,5},{5,4},{6,7},{7,6},{8,9},{9,8},{10,11... | collective-permute-start | bytes 1966088 | tf_op jit(solution)/shard_map/ppermute | solution.py:21
  99.9 17.2 %collective-permute-start.17 = (f32[640,256]{1,0:T(8,128)}, f32[640,256]{1,0:T(8,128)}, u32[]{:S(2)}, u32[]{:S(2)}) collective-permute-start(f32[640,256]{1,0:T(8,128)} %shard_map.145), channel_id=1, source_target_pairs={{0,1},{1,0},{2,3},{3,2},{4,5},{5,4},{6,7},{7,6},{8,9},{9,8},{10,11... | collective-permute-start | bytes 1966088 | tf_op jit(solution)/shard_map/ppermute | solution.py:21
  99.9 4.0 %copy-start = (bf16[640,8192]{1,0:T(8,128)(2,1)S(1)}, bf16[640,8192]{1,0:T(8,128)(2,1)}, u32[]{:S(2)}) copy-start(bf16[640,8192]{1,0:T(8,128)(2,1)} %xo_ref.15) | copy-start | bytes 31457284
  103.9 2.8 %copy-start.4 = (bf16[640,512]{1,0:T(8,128)(2,1)S(1)}, bf16[640,512]{1,0:T(8,128)(2,1)}, u32[]{:S(2)}) copy-start(bf16[640,512]{1,0:T(8,128)(2,1)} %cot_ref.3) | copy-start | bytes 1966084
  108.1 10.4 %collective-permute-start.8 = (bf16[256,640]{1,0:T(8,128)(2,1)S(1)}, bf16[256,640]{1,0:T(8,128)(2,1)S(1)}, u32[]{:S(2)}, u32[]{:S(2)}) collective-permute-start(bf16[256,640]{1,0:T(8,128)(2,1)S(1)} %shard_map.138.eo_ref), channel_id=1, source_target_pairs={{0,1},{1,0},{2,3},{3,2},{4,5},{5,4},{6,7},{7,6},{8,9},{9,8},{10,11... | collective-permute-start | bytes 983048 | tf_op jit(solution)/shard_map/ppermute | solution.py:21
  108.9 4.0 %copy-start.1 = (bf16[640,8192]{1,0:T(8,128)(2,1)S(1)}, bf16[640,8192]{1,0:T(8,128)(2,1)}, u32[]{:S(2)}) copy-start(bf16[640,8192]{1,0:T(8,128)(2,1)} %xo_ref.15) | copy-start | bytes 31457284
  112.9 5.6 %copy-start.2 = (bf16[640,8192]{1,0:T(8,128)(2,1)S(1)}, bf16[640,8192]{1,0:T(8,128)(2,1)}, u32[]{:S(2)}) copy-start(bf16[640,8192]{1,0:T(8,128)(2,1)} %xo_ref.15) | copy-start | bytes 31457284
  118.5 12.1 %collective-permute-start.18 = (bf16[256,640]{1,0:T(8,128)(2,1)S(1)}, bf16[256,640]{1,0:T(8,128)(2,1)S(1)}, u32[]{:S(2)}, u32[]{:S(2)}) collective-permute-start(bf16[256,640]{1,0:T(8,128)(2,1)S(1)} %shard_map.146.eo_ref), channel_id=1, source_target_pairs={{0,1},{1,0},{2,3},{3,2},{4,5},{5,4},{6,7},{7,6},{8,9},{9,8},{10,11... | collective-permute-start | bytes 983048 | tf_op jit(solution)/shard_map/ppermute | solution.py:21
  121.6 23.0 %collective-permute-start.11 = (f16[8,256,128]{2,1,0:T(8,128)(2,1)S(1)}, f16[8,256,128]{2,1,0:T(8,128)(2,1)S(1)}, u32[]{:S(2)}, u32[]{:S(2)}) collective-permute-start(f16[8,256,128]{2,1,0:T(8,128)(2,1)S(1)} %multiply_convert_fusion.3), channel_id=1, source_target_pairs={{0,48},{16,0},{32,16},{48,32},{1,49},{17,1},{33,17},{49,33},{2,50}... | collective-permute-start | bytes 1572872 | tf_op jit(solution)/shard_map/ppermute | solution.py:41
  125.3 27.3 %collective-permute-start.10 = (f16[8,256,128]{2,1,0:T(8,128)(2,1)S(1)}, f16[8,256,128]{2,1,0:T(8,128)(2,1)S(1)}, u32[]{:S(2)}, u32[]{:S(2)}) collective-permute-start(f16[8,256,128]{2,1,0:T(8,128)(2,1)S(1)} %multiply_convert_fusion.4), channel_id=1, source_target_pairs={{0,16},{16,32},{32,48},{48,0},{1,17},{17,33},{33,49},{49,1},{2,18}... | collective-permute-start | bytes 1572872 | tf_op jit(solution)/shard_map/ppermute | solution.py:41
  129.8 22.8 %collective-permute-start.9 = (f16[8,256,128]{2,1,0:T(8,128)(2,1)S(1)}, f16[8,256,128]{2,1,0:T(8,128)(2,1)S(1)}, u32[]{:S(2)}, u32[]{:S(2)}) collective-permute-start(f16[8,256,128]{2,1,0:T(8,128)(2,1)S(1)} %multiply_convert_fusion.5), channel_id=1, source_target_pairs={{0,32},{16,48},{32,0},{48,16},{1,33},{17,49},{33,1},{49,17},{2,34}... | collective-permute-start | bytes 1572872 | tf_op jit(solution)/shard_map/ppermute | solution.py:41
  133.6 35.8 %collective-permute-start.21 = (f16[8,256,128]{2,1,0:T(8,128)(2,1)S(1)}, f16[8,256,128]{2,1,0:T(8,128)(2,1)}, u32[]{:S(2)}, u32[]{:S(2)}) collective-permute-start(f16[8,256,128]{2,1,0:T(8,128)(2,1)S(1)} %multiply_convert_fusion), channel_id=1, source_target_pairs={{0,48},{16,0},{32,16},{48,32},{1,49},{17,1},{33,17},{49,33},{2,50}... | collective-permute-start | bytes 1572872 | tf_op jit(solution)/shard_map/ppermute | solution.py:41
  138.7 35.8 %collective-permute-start.20 = (f16[8,256,128]{2,1,0:T(8,128)(2,1)S(1)}, f16[8,256,128]{2,1,0:T(8,128)(2,1)}, u32[]{:S(2)}, u32[]{:S(2)}) collective-permute-start(f16[8,256,128]{2,1,0:T(8,128)(2,1)S(1)} %multiply_convert_fusion.1), channel_id=1, source_target_pairs={{0,16},{16,32},{32,48},{48,0},{1,17},{17,33},{33,49},{49,1},{2,18}... | collective-permute-start | bytes 1572872 | tf_op jit(solution)/shard_map/ppermute | solution.py:41
  153.8 23.1 %all-to-all-start.1 = ((f16[8,256,128]{2,1,0:T(8,128)(2,1)}), f16[8,256,128]{2,1,0:T(8,128)(2,1)S(1)}, u32[]{:S(2)}, u32[]{:S(2)}) async-start(f16[8,256,128]{2,1,0:T(8,128)(2,1)} %add_convert_fusion.1), calls=%async_computation.1 | async-start | bytes 1048576 | tf_op jit(solution)/shard_map/all_to_all | solution.py:191
  160.7 13.8 %collective-permute-start.19 = (f16[8,256,128]{2,1,0:T(8,128)(2,1)S(1)}, f16[8,256,128]{2,1,0:T(8,128)(2,1)S(1)}, u32[]{:S(2)}, u32[]{:S(2)}) collective-permute-start(f16[8,256,128]{2,1,0:T(8,128)(2,1)S(1)} %multiply_convert_fusion.2), channel_id=1, source_target_pairs={{0,32},{16,48},{32,0},{48,16},{1,33},{17,49},{33,1},{49,17},{2,34}... | collective-permute-start | bytes 1572872 | tf_op jit(solution)/shard_map/ppermute | solution.py:41
  162.5 4.0 %copy-start.3 = (bf16[640,8192]{1,0:T(8,128)(2,1)S(1)}, bf16[640,8192]{1,0:T(8,128)(2,1)}, u32[]{:S(2)}) copy-start(bf16[640,8192]{1,0:T(8,128)(2,1)} %xo_ref.15) | copy-start | bytes 31457284
  169.3 34.1 %copy-start.5 = (f32[64,512]{1,0:T(8,128)S(1)}, f32[64,512]{1,0:T(8,128)}, u32[]{:S(2)}) copy-start(f32[64,512]{1,0:T(8,128)} %param.15) | copy-start | bytes 393220
  169.4 34.1 %copy-start.7 = (f32[1,64,512]{2,1,0:T(8,128)S(1)}, f32[1,64,512]{2,1,0:T(8,128)}, u32[]{:S(2)}) copy-start(f32[1,64,512]{2,1,0:T(8,128)} %param.16) | copy-start | bytes 393220
  169.4 34.1 %copy-start.8 = (f32[64,512]{1,0:T(8,128)S(1)}, f32[64,512]{1,0:T(8,128)}, u32[]{:S(2)}) copy-start(f32[64,512]{1,0:T(8,128)} %param.17) | copy-start | bytes 393220
  176.9 21.1 %all-to-all-start.3 = ((f16[8,256,128]{2,1,0:T(8,128)(2,1)}), f16[8,256,128]{2,1,0:T(8,128)(2,1)S(1)}, u32[]{:S(2)}, u32[]{:S(2)}) async-start(f16[8,256,128]{2,1,0:T(8,128)(2,1)} %add_convert_fusion), calls=%async_computation.3 | async-start | bytes 1048576 | tf_op jit(solution)/shard_map/all_to_all | solution.py:191
  187.3 17.9 %collective-permute-start.12 = (f32[64,256]{1,0:T(8,128)}, f32[64,256]{1,0:T(8,128)S(1)}, u32[]{:S(2)}, u32[]{:S(2)}) collective-permute-start(f32[64,256]{1,0:T(8,128)} %get-tuple-element.22), channel_id=1, source_target_pairs={{0,0},{64,1},{1,64},{65,65},{2,2},{66,3},{3,66},{67,67},{4,4},{68,... | collective-permute-start | bytes 196616 | tf_op jit(solution)/shard_map/ppermute | solution.py:37
  188.8 16.4 %collective-permute-start.13 = (f32[64,256]{1,0:T(8,128)}, f32[64,256]{1,0:T(8,128)S(1)}, u32[]{:S(2)}, u32[]{:S(2)}) collective-permute-start(f32[64,256]{1,0:T(8,128)} %get-tuple-element.23), channel_id=1, source_target_pairs={{64,0},{0,1},{65,64},{1,65},{66,2},{2,3},{67,66},{3,67},{68,4},{4,... | collective-permute-start | bytes 196616 | tf_op jit(solution)/shard_map/ppermute | solution.py:37
  200.4 4.8 %collective-permute-start.22 = (f32[64,256]{1,0:T(8,128)}, f32[64,256]{1,0:T(8,128)S(1)}, u32[]{:S(2)}, u32[]{:S(2)}) collective-permute-start(f32[64,256]{1,0:T(8,128)} %get-tuple-element.25), channel_id=1, source_target_pairs={{0,0},{64,1},{1,64},{65,65},{2,2},{66,3},{3,66},{67,67},{4,4},{68,... | collective-permute-start | bytes 196616 | tf_op jit(solution)/shard_map/ppermute | solution.py:37
  201.8 4.6 %collective-permute-start.23 = (f32[64,256]{1,0:T(8,128)}, f32[64,256]{1,0:T(8,128)S(1)}, u32[]{:S(2)}, u32[]{:S(2)}) collective-permute-start(f32[64,256]{1,0:T(8,128)} %get-tuple-element.26), channel_id=1, source_target_pairs={{64,0},{0,1},{65,64},{1,65},{66,2},{2,3},{67,66},{3,67},{68,4},{4,... | collective-permute-start | bytes 196616 | tf_op jit(solution)/shard_map/ppermute | solution.py:37
  205.2 1.3 copy-start.9
  205.2 1.3 copy-start.10
  205.2 1.3 copy-start.11
  206.4 0.6 copy-start.12

commit v2 on v1

v2 whole, which is shorter than its diff:
```python
import jax
import jax.numpy as jnp
from jax import lax
from jax.experimental import pallas as pl
from jax.experimental.pallas import tpu as pltpu
from jax.sharding import Mesh, PartitionSpec as P

AXES = ("r", "x", "y", "z", "c")
SIZES = (2, 2, 4, 8, 2)
D = 8192
HALF = 4096
KV = 512
PART = 256
LINE = 1024
TOK = 640
PART_SCALE = 256.0
PAIR_SCALE = 128.0
PLANE_SCALE = 64.0
WHOLE_SCALE = 32.0
WIDE = 55 * 1024 * 1024
LIGHT = pl.CostEstimate(flops=1000, bytes_accessed=1000, transcendentals=0)


def swap(value, axis):
    return lax.ppermute(value, axis, [(0, 1), (1, 0)])


SIDE = [(1, 0), (2, 3), (0, 2), (3, 1)]
CROSS = [(1, 2), (2, 1)]


def spread(value):
    return lax.ppermute(value, ("x", "c"), SIDE), lax.ppermute(value, ("x", "c"), CROSS)


def collect(side, cross):
    return (
        lax.ppermute(side, ("x", "c"), [(d, s) for s, d in SIDE]),
        lax.ppermute(cross, ("x", "c"), [(d, s) for s, d in CROSS]),
    )


def shift(value, axis, size, step):
    return lax.ppermute(value, axis, [(i, (i + step) % size) for i in range(size)])


def round_kernel(a_ref, b_ref, c_ref, d_ref, line_ref, other_ref, rows_ref, next_ref):
    for i, ref in enumerate((a_ref, b_ref, c_ref, d_ref)):
        rows_ref[i] = ref[...]


def next_round(pieces, line, other):
    vmem = pl.BlockSpec(memory_space=pltpu.VMEM)
    anywhere = pl.BlockSpec(memory_space=pl.ANY)
    return pl.pallas_call(
        round_kernel,
        in_specs=[vmem] * 4 + [anywhere] * 2,
        out_specs=[vmem, anywhere],
        out_shape=[
            jax.ShapeDtypeStruct((4,) + pieces[0].shape, pieces[0].dtype),
            jax.ShapeDtypeStruct(line.shape, line.dtype),
        ],
        input_output_aliases={4: 1},
        cost_estimate=LIGHT,
    )(*pieces, line, other)


def gate_kernel(value_ref, after_ref, o_ref):
    o_ref[0] = value_ref[0]


def gate(value, after):
    smem = pl.BlockSpec(memory_space=pltpu.SMEM)
    return pl.pallas_call(
        gate_kernel,
        in_specs=[smem, pl.BlockSpec(memory_space=pl.ANY)],
        out_specs=smem,
        out_shape=jax.ShapeDtypeStruct((1,), jnp.float32),
        cost_estimate=LIGHT,
    )(jnp.full((1,), value, jnp.float32), after)[0]


def put_in_order(place_ref, own_ref, side_ref, cross_ref, put):
    x, q = place_ref[0], place_ref[1]

    @pl.when(jnp.logical_and(x == 0, q == 0))
    def _():
        put(own_ref, side_ref)

    @pl.when(jnp.logical_and(x == 1, q == 1))
    def _():
        put(side_ref, own_ref)

    @pl.when(jnp.logical_and(x == 1, q == 0))
    def _():
        put(side_ref, cross_ref)

    @pl.when(jnp.logical_and(x == 0, q == 1))
    def _():
        put(cross_ref, side_ref)


def weave_kernel(place_ref, own_ref, side_ref, cross_ref, o_ref):
    def put(low, high):
        o_ref[:, :, :64] = low[...]
        o_ref[:, :, 64:] = high[...]

    put_in_order(place_ref, own_ref, side_ref, cross_ref, put)


def weave(place, own, side, cross):
    vmem = pl.BlockSpec(memory_space=pltpu.VMEM)
    return pl.pallas_call(
        weave_kernel,
        in_specs=[pl.BlockSpec(memory_space=pltpu.SMEM)] + [vmem] * 3,
        out_specs=vmem,
        out_shape=jax.ShapeDtypeStruct((4, 8, 128, PART), jnp.bfloat16),
        compiler_params=pltpu.CompilerParams(vmem_limit_bytes=16 * 1024 * 1024),
        cost_estimate=LIGHT,
    )(place, own, side, cross)


def join_kernel(place_ref, own_ref, side_ref, cross_ref, start_ref, drift_ref, o_ref):
    def put(low, high):
        o_ref[:64] = low[...]
        o_ref[64:] = high[...]

    put_in_order(place_ref, own_ref, side_ref, cross_ref, put)


def join(place, own, side, cross, *after):
    vmem = pl.BlockSpec(memory_space=pltpu.VMEM)
    return pl.pallas_call(
        join_kernel,
        in_specs=[pl.BlockSpec(memory_space=pltpu.SMEM)] + [vmem] * 3 + [pl.BlockSpec(memory_space=pl.ANY)] * 2,
        out_specs=vmem,
        out_shape=jax.ShapeDtypeStruct((128, PART), jnp.bfloat16),
        cost_estimate=LIGHT,
    )(place, own, side, cross, *after)


def pre_kernel(place_ref, *refs):
    columns, first, second, o_ref = refs[:4], refs[4:8], refs[8:12], refs[13]
    for k, weights in enumerate((first, second)):
        total = None
        for column, part in zip(columns, weights):
            term = jnp.dot(column[...], part[...].reshape(LINE, PART), preferred_element_type=jnp.float32)
            total = term if total is None else total + term
        o_ref[:, k * PART : (k + 1) * PART] = total


def project(place, columns, first, second, after):
    rows = 320

    def column_spec(step):
        return pl.BlockSpec((rows, LINE), lambda i, p: (i, p[0] + lax.rem(p[1] + step, 4)))

    weight_specs = [pl.BlockSpec((LINE, PART), lambda i, p: (0, 0))] * 4
    weight_specs += [pl.BlockSpec((1, 8, 128, PART), lambda i, p, s=step: (s, 0, 0, 0)) for step in range(4)]
    return pl.pallas_call(
        pre_kernel,
        grid_spec=pltpu.PrefetchScalarGridSpec(
            num_scalar_prefetch=1,
            grid=(TOK // rows,),
            in_specs=[column_spec(step) for step in range(4)] + weight_specs + [pl.BlockSpec(memory_space=pl.ANY)],
            out_specs=pl.BlockSpec((rows, KV), lambda i, p: (i, 0)),
        ),
        out_shape=jax.ShapeDtypeStruct((TOK, KV), jnp.float32),
        compiler_params=pltpu.CompilerParams(vmem_limit_bytes=WIDE),
        cost_estimate=LIGHT,
    )(place, *[columns] * 4, *first, *[second] * 4, after)


def error_kernel(own_ref, got_ref, cot_ref, o_ref):
    pre = own_ref[...] + got_ref[...]
    sig = jax.nn.sigmoid(pre)
    slope = sig * (1.0 + pre * (1.0 - sig))
    o_ref[...] = (cot_ref[...].astype(jnp.float32) * slope).astype(jnp.bfloat16)


def error_of(own, got, cotangent):
    rows = 160
    block = pl.BlockSpec((rows, KV), lambda i: (i, 0))
    return pl.pallas_call(
        error_kernel,
        grid=(TOK // rows,),
        in_specs=[block] * 3,
        out_specs=block,
        out_shape=jax.ShapeDtypeStruct((TOK, KV), jnp.bfloat16),
        compiler_params=pltpu.CompilerParams(vmem_limit_bytes=16 * 1024 * 1024),
        cost_estimate=LIGHT,
    )(own, got, cotangent)


def grad_kernel(place_ref, xo_ref, xr_ref, eo_ref, er_ref, first_ref, second_ref):
    dims = (((0,), (0,)), ((), ()))
    part = lax.dot_general(xo_ref[...], eo_ref[...], dims, preferred_element_type=jnp.float32)
    part = part + lax.dot_general(xr_ref[...], er_ref[...], dims, preferred_element_type=jnp.float32)
    first_ref[...] = part[:, :PART]
    second_ref[...] = part[:, PART:]


def gradient(place, own, other, err_own, err_other):
    width = 1024
    each = LINE // width
    x_spec = pl.BlockSpec((TOK, width), lambda i, p: (0, p[0] * each + i))
    e_spec = pl.BlockSpec((TOK, KV), lambda i, p: (0, 0))
    shape = jax.ShapeDtypeStruct((HALF, PART), jnp.float32)
    first, second = pl.pallas_call(
        grad_kernel,
        grid_spec=pltpu.PrefetchScalarGridSpec(
            num_scalar_prefetch=1,
            grid=(4 * each,),
            in_specs=[x_spec, x_spec, e_spec, e_spec],
            out_specs=[
                pl.BlockSpec((width, PART), lambda i, p: (i, 0)),
                pl.BlockSpec((width, PART), lambda i, p: (lax.rem(i // each + 4 - p[1], 4) * each + lax.rem(i, each), 0)),
            ],
        ),
        out_shape=[shape, shape],
        compiler_params=pltpu.CompilerParams(vmem_limit_bytes=WIDE),
        cost_estimate=LIGHT,
    )(place, own, other, err_own, err_other)
    return first.reshape(4, 8, 128, PART), second.reshape(4, 8, 128, PART)


def adam_kernel(s_ref, g0_ref, g1_ref, w_ref, m_ref, v_ref, nw_ref, nm_ref, nv_ref, st_ref):
    grad = jnp.concatenate([g0_ref[...], g1_ref[...]], axis=1)
    master = w_ref[...]
    new_first = 0.9 * m_ref[...] + 0.1 * grad
    new_second = 0.95 * v_ref[...] + 0.05 * grad * grad
    step = new_first / s_ref[0] / (jnp.sqrt(new_second / s_ref[1]) + 1e-08)
    nw_ref[...] = master - 0.0003 * (step + 0.1 * master)
    nm_ref[...] = new_first
    nv_ref[...] = new_second
    st_ref[...] = step


def adam(corr, pieces, master, first, second):
    shape = jax.ShapeDtypeStruct(master.shape, jnp.float32)
    vmem = pl.BlockSpec(memory_space=pltpu.VMEM)
    return pl.pallas_call(
        adam_kernel,
        in_specs=[pl.BlockSpec(memory_space=pltpu.SMEM)] + [vmem] * 5,
        out_specs=[vmem] * 4,
        out_shape=[shape] * 4,
    )(corr, *pieces, master, first, second)


def gather_line(block):
    rows = block.shape[0]
    column = lax.all_to_all(jnp.broadcast_to(block[None], (8, rows, PART)), "z", 0, 0, tiled=True)
    return column.reshape(8 * rows, PART)


def gather_plane(column):
    got = {step: shift(column, "y", 4, -step) for step in (2, 1, 3)}
    return [column, got[1], got[2], got[3]]


def send_plane(pieces, scale):
    return [shift((pieces[step - 1] * scale).astype(jnp.float16), "y", 4, step) for step in (2, 1, 3)]


def total_of(own, got, scale):
    return own + sum(g.astype(jnp.float32) for g in got) * (1.0 / scale)


def scatter_line(total, scale, applied=None):
    total = total * (scale if applied is None else applied)
    got = lax.all_to_all(total.astype(jnp.float16), "z", 0, 0, tiled=True)
    return jnp.sum(got.astype(jnp.float32), axis=0) * (1.0 / scale)


def on_device(inputs, cotangent, weight, first, second, roster_step, anchor, drift, momentum):
    q = lax.axis_index("c").astype(jnp.int32).reshape(1)
    y = lax.axis_index("y").astype(jnp.int32).reshape(1)
    x = lax.axis_index("x").astype(jnp.int32).reshape(1)
    place = jnp.concatenate([x, q])
    level = (x == q)[0]
    first_core = (q == 0)[0]
    master = weight[0]
    cast = master.astype(jnp.bfloat16)
    start = gather_line(cast[:, PART:])
    side, cross = spread(cast[:, :PART])
    drift_other = swap(drift[0], "r")
    other = swap(inputs, "c")
    block = join(place, cast[:, :PART], side, cross, start, drift_other)
    column = gather_plane(start)
    rows, line = next_round(column, gather_line(block), other)
    half0 = gather_plane(line)
    rows = rows.reshape(4, 8, 64, PART)
    half1 = weave(place, rows, *spread(rows))

    delta = -(drift[0] + drift_other) / 2
    new_momentum = 0.9 * momentum + delta
    new_anchor = anchor - 0.7 * (delta + 0.9 * new_momentum)

    at = jnp.concatenate([4 * q, y])
    pre_other = project(at, other, half0, half1, q)
    got = swap(pre_other, "c")
    pre = project(at, inputs, half0, half1, pre_other)
    error = error_of(pre, got, cotangent)
    error_other = swap(error, "c")
    whole0, whole1 = gradient(at, inputs, other, error, error_other)
    got0 = lax.all_to_all((whole0 * PART_SCALE).astype(jnp.float16), "y", 0, 0, tiled=True)
    low, high = whole1[:, :, :64], whole1[:, :, 64:]
    same, else_ = jnp.where(first_core, low, high), jnp.where(first_core, high, low)
    side_out = (jnp.where(level, else_, same) * PART_SCALE).astype(jnp.float16)
    cross_out = (else_ * PART_SCALE).astype(jnp.float16)
    side, cross = collect(side_out, cross_out)
    met1 = jnp.where(level, same, cross.astype(jnp.float32) * (1.0 / PART_SCALE)) + side.astype(jnp.float32) * (
        1.0 / PART_SCALE
    )
    sent1 = send_plane(met1[1:], PAIR_SCALE)

    total0 = jnp.sum(got0.astype(jnp.float32), axis=0) * (1.0 / PART_SCALE)
    total0 = scatter_line(total0, PLANE_SCALE)
    low, high = total0[:64], total0[64:]
    same, else_ = jnp.where(first_core, low, high), jnp.where(first_core, high, low)
    side, cross = collect(jnp.where(level, else_, same), else_)
    first0 = side + jnp.where(level, same, cross)
    total1 = scatter_line(total_of(met1[0], sent1, PAIR_SCALE), WHOLE_SCALE, gate(WHOLE_SCALE, total0))

    step_f = roster_step[0].astype(jnp.float32)
    corr = jnp.stack([1.0 - jnp.power(jnp.float32(0.9), step_f), 1.0 - jnp.power(jnp.float32(0.95), step_f)])
    new_weight, new_first, new_second, adam_step = adam(corr, (first0, total1), master, first[0], second[0])
    return (new_weight[None], new_first[None], new_second[None], adam_step[None], new_anchor, new_momentum)


def solution(mesh):
    fine = Mesh(mesh.devices.reshape(SIZES), AXES)
    every = ("r", "x", "y", "z", "c")
    fsdp = ("x", "y", "z", "c")
    return jax.shard_map(
        on_device,
        mesh=fine,
        in_specs=(
            P(every, None),
            P(every, None),
            P("r", fsdp, None),
            P("r", fsdp, None),
            P("r", fsdp, None),
            P("r"),
            P(fsdp, None),
            P("r", fsdp, None),
            P(fsdp, None),
        ),
        out_specs=(
            P("r", fsdp, None),
            P("r", fsdp, None),
            P("r", fsdp, None),
            P("r", fsdp, None),
            P(fsdp, None),
            P(fsdp, None),
        ),
        check_vma=False,
    )
```

time: 211 us -> 204 us (0.967)
  other arithmetic: 9.04 us -> 23.3 us
  Pallas kernels: 48.2 us -> 35.3 us
  local copies, waits for them, and re-layouts: 19.9 us -> 8.82 us
  waiting for transfers between devices: 74.2 us -> 84.6 us
  starting transfers between devices: 56.1 us -> 49.3 us
    ppermute x6 -> x8, waiting for transfers between devices: 1.26 us -> 22 us  [the longest x2 19.2 us: spread(): lax.ppermute(value, ('x', 'c'), SIDE)]
    ppermute x12 -> x9, waiting for transfers between devices: 34.7 us -> 18.9 us  [shift(): lax.ppermute(value, axis, [(i, (i + step) % size) for i in range(size)])]
    pallas_call x8 -> x1, Pallas kernels: 23.1 us -> 12.2 us  [gradient(): pl.pallas_call(grad_kernel, grid_spec=pltpu.PrefetchScalarGridSpec(num_sc...]
    all_to_all x4 -> x5, waiting for transfers between devices: 31.6 us -> 40.3 us  [the longest x1 20.4 us: on_device(): lax.all_to_all((whole0 * PART_SCALE).astype(jnp.float16), 'y', 0, 0, tile...]
    convert_element_type x8 -> x5, other arithmetic: 4.19 us -> 12.2 us  [the longest x1 4.31 us: on_device(): cross_out = (else_ * PART_SCALE).astype(jnp.float16)]
    ppermute x12 -> x9, starting transfers between devices: 19.2 us -> 13 us  [shift(): lax.ppermute(value, axis, [(i, (i + step) % size) for i in range(size)])]
    unnamed x26 -> x50, local copies, waits for them, and re-layouts: 12.7 us -> 6.42 us
    dynamic_slice x1 -> x0, local copies, waits for them, and re-layouts: 5.55 us -> none  [on_device(): send = lax.dynamic_slice(inputs, (0, (1 - q) * HALF), (TOK, HALF))]
  transfers between devices with their start and end apart: 28 -> 26, of which waited for: 10 -> 13; matrix products, arithmetic and copies ran while one was open for 7% -> 9% of each run, Pallas kernels for 22% -> 5%
where the time goes in v2:
time: 204 us; the launch traced here: 203 us
  waiting for transfers between devices  84.6 us (41%)
  starting transfers between devices  49.3 us (24%)
  Pallas kernels  35.3 us (17%)
  other arithmetic  23.3 us (11%)
  local copies, waits for them, and re-layouts  8.82 us (4%)
    all_to_all x1, waiting for transfers between devices, on_device(): lax.all_to_all((whole0 * PART_SCALE).astype(jnp.float16), 'y', 0, 0, tile...  20.4 us
    ppermute x2, waiting for transfers between devices, spread(): lax.ppermute(value, ('x', 'c'), SIDE)  19.2 us
    ppermute x9, waiting for transfers between devices, shift(): lax.ppermute(value, axis, [(i, (i + step) % size) for i in range(size)])  18.9 us
    pallas_call x2, Pallas kernels, project(): pl.pallas_call(pre_kernel, grid_spec=pltpu.PrefetchScalarGridSpec(num_sca...  15.8 us
    all_to_all x2, waiting for transfers between devices, scatter_line(): got = lax.all_to_all(total.astype(jnp.float16), 'z', 0, 0, tiled=True)  14.9 us
    ppermute x9, starting transfers between devices, shift(): lax.ppermute(value, axis, [(i, (i + step) % size) for i in range(size)])  13 us
    pallas_call x1, Pallas kernels, gradient(): pl.pallas_call(grad_kernel, grid_spec=pltpu.PrefetchScalarGridSpec(num_sc...  12.2 us
    all_to_all x2, starting transfers between devices, gather_line(): lax.all_to_all(jnp.broadcast_to(block[None], (8, rows, PART)), 'z', 0, 0,...  12 us
  transfers between devices with their start and end apart: 26, of which 13 were waited for; matrix products, arithmetic and copies ran while one was open for 9% of the time, Pallas kernels for 5%

profile of v2, /device:TPU:4, one launch (start us, length us, event | category | flops | bytes accessed | tf_op | source)
XLA Modules:
  0.0 203.0 jit_solution(16393220649271602145)
XLA Ops:
  0.7 0.9 bitcast_convert_fusion
  1.7 0.7 broadcast_in_dim.24
  2.4 8.5 %all-to-all-start = ((bf16[8,64,256]{2,1,0:T(8,128)(2,1)}), bf16[8,64,256]{2,1,0:T(8,128)(2,1)S(1)}, u32[]{:S(2)}, u32[]{:S(2)}) async-start(bf16[8,64,256]{2,1,0:T(8,128)(2,1)} %broadcast_in_dim.24), calls=%async_computation | async-start | bytes 524288 | tf_op jit(solution)/shard_map/all_to_all | solution.py:252
  11.4 2.1 %collective-permute-start.4 = (bf16[64,256]{1,0:T(8,128)(2,1)S(1)}, bf16[64,256]{1,0:T(8,128)(2,1)S(1)}, u32[]{:S(2)}, u32[]{:S(2)}) collective-permute-start(bf16[64,256]{1,0:T(8,128)(2,1)S(1)} %get-tuple-element.31.own_ref), channel_id=1, source_target_pairs={{1,0},{64,65},{0,64},{65,1},{3,2},{66,67},{2,66},{67,3},{5,4},{68,... | collective-permute-start | bytes 98312 | tf_op jit(solution)/shard_map/ppermute | solution.py:33
  13.5 0.7 collective-permute-start.5
  14.1 0.7 pad_add_fusion.1.place_ref
  14.8 2.1 %collective-permute-done.4.side_ref = bf16[64,256]{1,0:T(8,128)(2,1)S(1)} collective-permute-done((bf16[64,256]{1,0:T(8,128)(2,1)S(1)}, bf16[64,256]{1,0:T(8,128)(2,1)S(1)}, u32[]{:S(2)}, u32[]{:S(2)}) %collective-permute-start.4) | collective-permute-done | bytes 32800 | tf_op jit(solution)/shard_map/ppermute | solution.py:33
  16.9 1.6 collective-permute-done.6.drift_ref
  18.5 4.9 %all-to-all-done = bf16[8,64,256]{2,1,0:T(8,128)(2,1)S(1)} async-done(((bf16[8,64,256]{2,1,0:T(8,128)(2,1)}), bf16[8,64,256]{2,1,0:T(8,128)(2,1)S(1)}, u32[]{:S(2)}, u32[]{:S(2)}) %all-to-all-start) | async-done | bytes 262176 | tf_op jit(solution)/shard_map/all_to_all | solution.py:252
  23.4 0.7 copy-done.7
  24.1 1.5 shard_map.136
  25.6 1.7 broadcast_in_dim.25
  27.2 3.5 %all-to-all-start.1 = ((bf16[8,128,256]{2,1,0:T(8,128)(2,1)}), bf16[8,128,256]{2,1,0:T(8,128)(2,1)S(1)}, u32[]{:S(2)}, u32[]{:S(2)}) async-start(bf16[8,128,256]{2,1,0:T(8,128)(2,1)} %broadcast_in_dim.25), calls=%async_computation.1 | async-start | bytes 1048576 | tf_op jit(solution)/shard_map/all_to_all | solution.py:252
  30.7 3.1 %collective-permute-start.1 = (bf16[512,256]{1,0:T(8,128)(2,1)}, bf16[512,256]{1,0:T(8,128)(2,1)S(1)}, u32[]{:S(2)}, u32[]{:S(2)}) collective-permute-start(bf16[512,256]{1,0:T(8,128)(2,1)} %bitcast.44), channel_id=1, source_target_pairs={{0,48},{16,0},{32,16},{48,32},{1,49},{17,1},{33,17},{49,33},{2,50}... | collective-permute-start | bytes 786440 | tf_op jit(solution)/shard_map/ppermute | solution.py:44
  33.8 0.6 collective-permute-start.2
  34.5 1.0 collective-permute-start.3
  35.4 10.1 %collective-permute-done.1.b_ref = bf16[512,256]{1,0:T(8,128)(2,1)S(1)} collective-permute-done((bf16[512,256]{1,0:T(8,128)(2,1)}, bf16[512,256]{1,0:T(8,128)(2,1)S(1)}, u32[]{:S(2)}, u32[]{:S(2)}) %collective-permute-start.1) | collective-permute-done | bytes 262176 | tf_op jit(solution)/shard_map/ppermute | solution.py:44
  45.5 3.6 %collective-permute-done.3.d_ref = bf16[512,256]{1,0:T(8,128)(2,1)S(1)} collective-permute-done((bf16[512,256]{1,0:T(8,128)(2,1)}, bf16[512,256]{1,0:T(8,128)(2,1)S(1)}, u32[]{:S(2)}, u32[]{:S(2)}) %collective-permute-start.3) | collective-permute-done | bytes 262176 | tf_op jit(solution)/shard_map/ppermute | solution.py:44
  49.2 0.7 copy-done.16
  50.0 2.2 %shard_map.137 = (bf16[4,512,256]{2,1,0:T(8,128)(2,1)}, bf16[1024,256]{1,0:T(8,128)(2,1)}) custom-call(bf16[512,256]{1,0:T(8,128)(2,1)} %bitcast.47, bf16[512,256]{1,0:T(8,128)(2,1)} %copy-done.14, bf16[512,256]{1,0:T(8,128)(2,1)} %copy-done.15, bf16[512,256]{1,0:T(8,128)(2,1)} %copy-done.16, ...), custom_call_target="tpu_custom_call", output_to_operand_aliasing={{1}: (4, {})} | custom-call | flops 1000 | bytes 1000 | tf_op jit(solution)/shard_map/pallas_call | solution.py:55
  52.2 1.2 collective-permute-start.10
  53.4 0.7 collective-permute-start.11
  54.2 2.5 %collective-permute-start.7 = (bf16[1024,256]{1,0:T(8,128)(2,1)}, bf16[1024,256]{1,0:T(8,128)(2,1)S(1)}, u32[]{:S(2)}, u32[]{:S(2)}) collective-permute-start(bf16[1024,256]{1,0:T(8,128)(2,1)} %get-tuple-element.14.refs_4_), channel_id=1, source_target_pairs={{0,48},{16,0},{32,16},{48,32},{1,49},{17,1},{33,17},{49,33},{2,50}... | collective-permute-start | bytes 1572872 | tf_op jit(solution)/shard_map/ppermute | solution.py:44
  56.6 0.6 collective-permute-start.8
  57.3 1.0 collective-permute-start.9
  58.2 0.6 pad_add_fusion.place_ref
  58.8 17.1 %collective-permute-done.10.side_ref = bf16[4,8,64,256]{3,2,1,0:T(8,128)(2,1)S(1)} collective-permute-done((bf16[4,8,64,256]{3,2,1,0:T(8,128)(2,1)}, bf16[4,8,64,256]{3,2,1,0:T(8,128)(2,1)S(1)}, u32[]{:S(2)}, u32[]{:S(2)}) %collective-permute-start.10) | collective-permute-done | bytes 1048608 | tf_op jit(solution)/shard_map/ppermute | solution.py:33
  76.0 1.2 copy-done.3
  77.2 0.7 shard_map.138.refs_8_.refs_9_.refs_10_.refs_11_
  77.9 1.4 copy-done
  79.3 0.8 collective-permute-done.7.refs_5_
  80.1 4.4 %collective-permute-done.9.refs_7_ = bf16[1024,256]{1,0:T(8,128)(2,1)} collective-permute-done((bf16[1024,256]{1,0:T(8,128)(2,1)}, bf16[1024,256]{1,0:T(8,128)(2,1)}, u32[]{:S(2)}, u32[]{:S(2)}) %collective-permute-start.9) | collective-permute-done | bytes 524320 | tf_op jit(solution)/shard_map/ppermute | solution.py:44
  84.5 7.8 %shard_map.139.refs_12_ = f32[640,512]{1,0:T(8,128)} custom-call(s32[2]{0:T(128)} %pad_add_fusion.place_ref, bf16[640,8192]{1,0:T(8,128)(2,1)} %collective-permute-done.other_ref.refs_0_.refs_1_.refs_2_.refs_3_.xr_ref, bf16[640,8192]{1,0:T(8,128)(2,1)} %collective-permute-done.other_ref.refs_0_.refs_1_.refs_2_.refs_3_.xr_ref, ...), custom_call_target="tpu_custom_call" | custom-call | flops 1000 | bytes 1000 | tf_op jit(solution)/shard_map/pallas_call | solution.py:160
  92.5 8.0 %shard_map.140.own_ref = f32[640,512]{1,0:T(8,128)} custom-call(s32[2]{0:T(128)} %pad_add_fusion.place_ref, bf16[640,8192]{1,0:T(8,128)(2,1)} %xo_ref.1, bf16[640,8192]{1,0:T(8,128)(2,1)} %xo_ref.1, bf16[640,8192]{1,0:T(8,128)(2,1)} %xo_ref.1, bf16[640,8192]{1,0:T(8,128)(2,1)} %xo_ref.1, bf16[1024,256]{1,0:T(8,128)(2,1)} %get-tuple-element.14.refs_4_, ...), custom_call_target="tpu_custom_call" | custom-call | flops 1000 | bytes 1000 | tf_op jit(solution)/shard_map/pallas_call | solution.py:160
  100.5 1.3 copy-done.1
  102.3 0.6 collective-permute-start.13
  102.9 1.8 collective-permute-done.13.er_ref
  104.7 0.8 copy-done.11
  105.5 12.2 %shard_map.142 = (f32[4096,256]{1,0:T(8,128)}, f32[4096,256]{1,0:T(8,128)}) custom-call(s32[2]{0:T(128)} %pad_add_fusion.place_ref, bf16[640,8192]{1,0:T(8,128)(2,1)} %xo_ref.1, bf16[640,8192]{1,0:T(8,128)(2,1)} %collective-permute-done.other_ref.refs_0_.refs_1_.refs_2_.refs_3_.xr_ref, bf16[640,512]{1,0:T(8,128)(2,1)} %copy-done.2, bf16[640,512]{1,0:T(8,128)(2,1)} %copy-done.11), custom_call_target="tpu_custom_call" | custom-call | flops 1000 | bytes 1000 | tf_op jit(solution)/shard_map/pallas_call | solution.py:209
  117.7 4.1 %multiply_convert_fusion = f16[4096,256]{1,0:T(8,128)(2,1)} fusion(f32[4096,256]{1,0:T(8,128)} %get-tuple-element.16), kind=kLoop, calls=%fused_computation.1 | loop fusion | flops 2097152 | bytes 6291456 | tf_op jit(solution)/shard_map/convert_element_type | solution.py:306
  121.8 3.6 %all-to-all-start.2 = ((f16[4,8,128,256]{3,2,1,0:T(8,128)(2,1)}), f16[4,8,128,256]{3,2,1,0:T(8,128)(2,1)S(1)}, u32[]{:S(2)}, u32[]{:S(2)}) async-start(f16[4,8,128,256]{3,2,1,0:T(8,128)(2,1)} %bitcast.10), calls=%async_computation.2 | async-start | bytes 4194304 | tf_op jit(solution)/shard_map/all_to_all | solution.py:306
  125.4 4.3 %multiply_convert_fusion.2 = (f16[4,8,64,256]{3,2,1,0:T(8,128)(2,1)}, f16[4,8,64,256]{3,2,1,0:T(8,128)(2,1)}) fusion(f32[4,8,128,256]{3,2,1,0:T(8,128)} %bitcast.40, pred[]{:T(512)} %bitcast.3, pred[]{:T(512)} %bitcast.2), kind=kLoop, calls=%fused_computation.4 | loop fusion | flops 3670016 | bytes 6291458 | tf_op jit(solution)/shard_map/convert_element_type | solution.py:310
  129.7 1.6 collective-permute-start.16
  131.4 0.7 collective-permute-start.17
  132.0 20.4 %all-to-all-done.2 = f16[4,8,128,256]{3,2,1,0:T(8,128)(2,1)S(1)} async-done(((f16[4,8,128,256]{3,2,1,0:T(8,128)(2,1)}), f16[4,8,128,256]{3,2,1,0:T(8,128)(2,1)S(1)}, u32[]{:S(2)}, u32[]{:S(2)}) %all-to-all-start.2) | async-done | bytes 2097184 | tf_op jit(solution)/shard_map/all_to_all | solution.py:306
  152.9 0.9 multiply_convert_fusion.3
  153.8 5.0 %all-to-all-start.3 = ((f16[8,128,256]{2,1,0:T(8,128)(2,1)}), f16[8,128,256]{2,1,0:T(8,128)(2,1)S(1)}, u32[]{:S(2)}, u32[]{:S(2)}) async-start(f16[8,128,256]{2,1,0:T(8,128)(2,1)} %multiply_convert_fusion.3), calls=%async_computation.3 | async-start | bytes 1048576 | tf_op jit(solution)/shard_map/all_to_all | solution.py:271
  159.5 0.7 pad_maximum_fusion.s_ref
  160.2 3.5 %multiply_add_fusion = f32[4,8,64,256]{3,2,1,0:T(8,128)S(1)} fusion(f16[4,8,64,256]{3,2,1,0:T(8,128)(2,1)} %collective-permute-done.17, f16[4,8,64,256]{3,2,1,0:T(8,128)(2,1)} %collective-permute-done.16, pred[]{:T(512)} %bitcast.2, f32[4,8,128,256]{3,2,1,0:T(8,128)} %bitcast.41, pred[]{:T(512)} %bitcast.3), kind=kLoop, calls=%fused_computation.2 | loop fusion | flops 3670016 | bytes 8388610 | tf_op jit(solution)/shard_map/add | solution.py:312
  163.9 1.0 collective-permute-start.18
  164.9 1.1 collective-permute-start.19
  166.0 2.1 %collective-permute-start.20 = (f16[8,64,256]{2,1,0:T(8,128)(2,1)S(1)}, f16[8,64,256]{2,1,0:T(8,128)(2,1)}, u32[]{:S(2)}, u32[]{:S(2)}) collective-permute-start(f16[8,64,256]{2,1,0:T(8,128)(2,1)S(1)} %get-tuple-element.29), channel_id=1, source_target_pairs={{0,48},{16,0},{32,16},{48,32},{1,49},{17,1},{33,17},{49,33},{2,50}... | collective-permute-start | bytes 786440 | tf_op jit(solution)/shard_map/ppermute | solution.py:44
  168.1 7.9 %all-to-all-done.3 = f16[8,128,256]{2,1,0:T(8,128)(2,1)S(1)} async-done(((f16[8,128,256]{2,1,0:T(8,128)(2,1)}), f16[8,128,256]{2,1,0:T(8,128)(2,1)S(1)}, u32[]{:S(2)}, u32[]{:S(2)}) %all-to-all-start.3) | async-done | bytes 524320 | tf_op jit(solution)/shard_map/all_to_all | solution.py:271
  176.1 0.7 broadcast_multiply_fusion.after_ref
  177.3 1.5 broadcast_select_fusion
  178.9 2.7 %fusion.5 = f16[8,64,256]{2,1,0:T(8,128)(2,1)} fusion(f32[4,8,64,256]{3,2,1,0:T(8,128)S(1)} %multiply_add_fusion, f16[8,64,256]{2,1,0:T(8,128)(2,1)} %collective-permute-done.20, f16[8,64,256]{2,1,0:T(8,128)(2,1)} %collective-permute-done.19, f16[8,64,256]{2,1,0:T(8,128)(2,1)} %collective-permute-done.18, f32[]{:T(128)} %bitcast.16), kind=kLoop, calls=%fused_computation.18 | loop fusion | flops 1179648 | bytes 1572868 | tf_op jit(solution)/shard_map/convert_element_type | solution.py:271
  181.5 6.7 %all-to-all-start.4 = ((f16[8,64,256]{2,1,0:T(8,128)(2,1)}), f16[8,64,256]{2,1,0:T(8,128)(2,1)S(1)}, u32[]{:S(2)}, u32[]{:S(2)}) async-start(f16[8,64,256]{2,1,0:T(8,128)(2,1)} %fusion.5), calls=%async_computation.4 | async-start | bytes 524288 | tf_op jit(solution)/shard_map/all_to_all | solution.py:271
  188.4 0.7 collective-permute-start.15
  189.1 0.7 multiply_subtract_fusion
  189.9 2.8 %collective-permute-done.14 = f32[64,256]{1,0:T(8,128)S(1)} collective-permute-done((f32[64,256]{1,0:T(8,128)S(1)}, f32[64,256]{1,0:T(8,128)S(1)}, u32[]{:S(2)}, u32[]{:S(2)}) %collective-permute-start.14) | collective-permute-done | bytes 65568 | tf_op jit(solution)/shard_map/ppermute | solution.py:38
  192.7 0.6 select_add_fusion.g0_ref
  193.3 7.1 %all-to-all-done.4 = f16[8,64,256]{2,1,0:T(8,128)(2,1)S(1)} async-done(((f16[8,64,256]{2,1,0:T(8,128)(2,1)}), f16[8,64,256]{2,1,0:T(8,128)(2,1)S(1)}, u32[]{:S(2)}, u32[]{:S(2)}) %all-to-all-start.4) | async-done | bytes 262176 | tf_op jit(solution)/shard_map/all_to_all | solution.py:271
  200.4 0.6 broadcast_multiply_fusion.1.g1_ref
  201.0 1.9 shard_map.144
  (68 shorter events, 2.9 us)
Async XLA Ops:
  0.6 48.5 %collective-permute-start = (bf16[640,8192]{1,0:T(8,128)(2,1)}, bf16[640,8192]{1,0:T(8,128)(2,1)}, u32[]{:S(2)}, u32[]{:S(2)}) collective-permute-start(bf16[640,8192]{1,0:T(8,128)(2,1)} %xo_ref.1), channel_id=1, source_target_pairs={{0,1},{1,0},{2,3},{3,2},{4,5},{5,4},{6,7},{7,6},{8,9},{9,8},{10,11... | collective-permute-start | bytes 31457288 | tf_op jit(solution)/shard_map/ppermute | solution.py:25
  1.7 21.7 %copy-start.17 = (bf16[64,256]{1,0:T(8,128)(2,1)}, bf16[64,256]{1,0:T(8,128)(2,1)S(1)}, u32[]{:S(2)}) copy-start(bf16[64,256]{1,0:T(8,128)(2,1)S(1)} %get-tuple-element.31.own_ref) | copy-start | bytes 98308
  2.4 21.0 %all-to-all-start = ((bf16[8,64,256]{2,1,0:T(8,128)(2,1)}), bf16[8,64,256]{2,1,0:T(8,128)(2,1)S(1)}, u32[]{:S(2)}, u32[]{:S(2)}) async-start(bf16[8,64,256]{2,1,0:T(8,128)(2,1)} %broadcast_in_dim.24), calls=%async_computation | async-start | bytes 524288 | tf_op jit(solution)/shard_map/all_to_all | solution.py:252
  10.9 7.6 %collective-permute-start.6 = (f32[64,512]{1,0:T(8,128)}, f32[64,512]{1,0:T(8,128)S(1)}, u32[]{:S(2)}, u32[]{:S(2)}) collective-permute-start(f32[64,512]{1,0:T(8,128)} %bitcast.51), channel_id=1, source_target_pairs={{0,128},{128,0},{1,129},{129,1},{2,130},{130,2},{3,131},{131,3},{4... | collective-permute-start | bytes 393224 | tf_op jit(solution)/shard_map/ppermute | solution.py:25
  11.4 5.5 %collective-permute-start.4 = (bf16[64,256]{1,0:T(8,128)(2,1)S(1)}, bf16[64,256]{1,0:T(8,128)(2,1)S(1)}, u32[]{:S(2)}, u32[]{:S(2)}) collective-permute-start(bf16[64,256]{1,0:T(8,128)(2,1)S(1)} %get-tuple-element.31.own_ref), channel_id=1, source_target_pairs={{1,0},{64,65},{0,64},{65,1},{3,2},{66,67},{2,66},{67,3},{5,4},{68,... | collective-permute-start | bytes 98312 | tf_op jit(solution)/shard_map/ppermute | solution.py:33
  13.5 3.5 %collective-permute-start.5 = (bf16[64,256]{1,0:T(8,128)(2,1)S(1)}, bf16[64,256]{1,0:T(8,128)(2,1)S(1)}, u32[]{:S(2)}, u32[]{:S(2)}) collective-permute-start(bf16[64,256]{1,0:T(8,128)(2,1)S(1)} %get-tuple-element.31.own_ref), channel_id=1, source_target_pairs={{1,64},{64,1},{3,66},{66,3},{5,68},{68,5},{7,70},{70,7},{9,72},{72... | collective-permute-start | bytes 98312 | tf_op jit(solution)/shard_map/ppermute | solution.py:33
  16.9 6.5 %copy-start.23 = (bf16[64,256]{1,0:T(8,128)(2,1)}, bf16[64,256]{1,0:T(8,128)(2,1)S(1)}, u32[]{:S(2)}) copy-start(bf16[64,256]{1,0:T(8,128)(2,1)S(1)} %collective-permute-done.4.side_ref) | copy-start | bytes 98308
  16.9 6.5 %copy-start.24 = (bf16[64,256]{1,0:T(8,128)(2,1)}, bf16[64,256]{1,0:T(8,128)(2,1)S(1)}, u32[]{:S(2)}) copy-start(bf16[64,256]{1,0:T(8,128)(2,1)S(1)} %collective-permute-done.5.cross_ref) | copy-start | bytes 98308
  18.5 4.9 %copy-start.12 = (f32[64,512]{1,0:T(8,128)}, f32[64,512]{1,0:T(8,128)S(1)}, u32[]{:S(2)}) copy-start(f32[64,512]{1,0:T(8,128)S(1)} %collective-permute-done.6.drift_ref) | copy-start | bytes 393220
  23.4 0.7 copy-start.7
  27.2 21.9 %all-to-all-start.1 = ((bf16[8,128,256]{2,1,0:T(8,128)(2,1)}), bf16[8,128,256]{2,1,0:T(8,128)(2,1)S(1)}, u32[]{:S(2)}, u32[]{:S(2)}) async-start(bf16[8,128,256]{2,1,0:T(8,128)(2,1)} %broadcast_in_dim.25), calls=%async_computation.1 | async-start | bytes 1048576 | tf_op jit(solution)/shard_map/all_to_all | solution.py:252
  30.7 14.8 %collective-permute-start.1 = (bf16[512,256]{1,0:T(8,128)(2,1)}, bf16[512,256]{1,0:T(8,128)(2,1)S(1)}, u32[]{:S(2)}, u32[]{:S(2)}) collective-permute-start(bf16[512,256]{1,0:T(8,128)(2,1)} %bitcast.44), channel_id=1, source_target_pairs={{0,48},{16,0},{32,16},{48,32},{1,49},{17,1},{33,17},{49,33},{2,50}... | collective-permute-start | bytes 786440 | tf_op jit(solution)/shard_map/ppermute | solution.py:44
  33.8 11.7 %collective-permute-start.2 = (bf16[512,256]{1,0:T(8,128)(2,1)}, bf16[512,256]{1,0:T(8,128)(2,1)S(1)}, u32[]{:S(2)}, u32[]{:S(2)}) collective-permute-start(bf16[512,256]{1,0:T(8,128)(2,1)} %bitcast.45), channel_id=1, source_target_pairs={{0,32},{16,48},{32,0},{48,16},{1,33},{17,49},{33,1},{49,17},{2,34}... | collective-permute-start | bytes 786440 | tf_op jit(solution)/shard_map/ppermute | solution.py:44
  34.5 14.7 %collective-permute-start.3 = (bf16[512,256]{1,0:T(8,128)(2,1)}, bf16[512,256]{1,0:T(8,128)(2,1)S(1)}, u32[]{:S(2)}, u32[]{:S(2)}) collective-permute-start(bf16[512,256]{1,0:T(8,128)(2,1)} %bitcast.46), channel_id=1, source_target_pairs={{0,16},{16,32},{32,48},{48,0},{1,17},{17,33},{33,49},{49,1},{2,18}... | collective-permute-start | bytes 786440 | tf_op jit(solution)/shard_map/ppermute | solution.py:44
  45.5 3.6 %copy-start.14 = (bf16[512,256]{1,0:T(8,128)(2,1)}, bf16[512,256]{1,0:T(8,128)(2,1)S(1)}, u32[]{:S(2)}) copy-start(bf16[512,256]{1,0:T(8,128)(2,1)S(1)} %collective-permute-done.1.b_ref) | copy-start | bytes 786436
  45.5 3.6 %copy-start.15 = (bf16[512,256]{1,0:T(8,128)(2,1)}, bf16[512,256]{1,0:T(8,128)(2,1)S(1)}, u32[]{:S(2)}) copy-start(bf16[512,256]{1,0:T(8,128)(2,1)S(1)} %collective-permute-done.2.c_ref) | copy-start | bytes 786436
  49.1 0.7 copy-start.16
  49.1 0.9 copy-start.6
  50.0 25.9 %copy-start.5 = (s32[2]{0:T(128)S(1)}, s32[2]{0:T(128)}, u32[]{:S(2)}) copy-start(s32[2]{0:T(128)} %pad_add_fusion.1.place_ref) | copy-start | bytes 28
  52.2 23.7 %collective-permute-start.10 = (bf16[4,8,64,256]{3,2,1,0:T(8,128)(2,1)}, bf16[4,8,64,256]{3,2,1,0:T(8,128)(2,1)S(1)}, u32[]{:S(2)}, u32[]{:S(2)}) collective-permute-start(bf16[4,8,64,256]{3,2,1,0:T(8,128)(2,1)} %bitcast.37), channel_id=1, source_target_pairs={{1,0},{64,65},{0,64},{65,1},{3,2},{66,67},{2,66},{67,3},{5,4},{68,... | collective-permute-start | bytes 3145736 | tf_op jit(solution)/shard_map/ppermute | solution.py:33
  53.4 22.5 %collective-permute-start.11 = (bf16[4,8,64,256]{3,2,1,0:T(8,128)(2,1)}, bf16[4,8,64,256]{3,2,1,0:T(8,128)(2,1)S(1)}, u32[]{:S(2)}, u32[]{:S(2)}) collective-permute-start(bf16[4,8,64,256]{3,2,1,0:T(8,128)(2,1)} %bitcast.38), channel_id=1, source_target_pairs={{1,64},{64,1},{3,66},{66,3},{5,68},{68,5},{7,70},{70,7},{9,72},{72... | collective-permute-start | bytes 3145736 | tf_op jit(solution)/shard_map/ppermute | solution.py:33
  54.2 25.9 %collective-permute-start.7 = (bf16[1024,256]{1,0:T(8,128)(2,1)}, bf16[1024,256]{1,0:T(8,128)(2,1)S(1)}, u32[]{:S(2)}, u32[]{:S(2)}) collective-permute-start(bf16[1024,256]{1,0:T(8,128)(2,1)} %get-tuple-element.14.refs_4_), channel_id=1, source_target_pairs={{0,48},{16,0},{32,16},{48,32},{1,49},{17,1},{33,17},{49,33},{2,50}... | collective-permute-start | bytes 1572872 | tf_op jit(solution)/shard_map/ppermute | solution.py:44
  56.6 23.5 %collective-permute-start.8 = (bf16[1024,256]{1,0:T(8,128)(2,1)}, bf16[1024,256]{1,0:T(8,128)(2,1)S(1)}, u32[]{:S(2)}, u32[]{:S(2)}) collective-permute-start(bf16[1024,256]{1,0:T(8,128)(2,1)} %get-tuple-element.14.refs_4_), channel_id=1, source_target_pairs={{0,32},{16,48},{32,0},{48,16},{1,33},{17,49},{33,1},{49,17},{2,34}... | collective-permute-start | bytes 1572872 | tf_op jit(solution)/shard_map/ppermute | solution.py:44
  57.3 27.2 %collective-permute-start.9 = (bf16[1024,256]{1,0:T(8,128)(2,1)}, bf16[1024,256]{1,0:T(8,128)(2,1)}, u32[]{:S(2)}, u32[]{:S(2)}) collective-permute-start(bf16[1024,256]{1,0:T(8,128)(2,1)} %get-tuple-element.14.refs_4_), channel_id=1, source_target_pairs={{0,16},{16,32},{32,48},{48,0},{1,17},{17,33},{33,49},{49,1},{2,18}... | collective-permute-start | bytes 1572872 | tf_op jit(solution)/shard_map/ppermute | solution.py:44
  75.9 1.2 copy-start.3
  77.9 1.4 copy-start
  80.1 4.4 %copy-start.8 = (bf16[1024,256]{1,0:T(8,128)(2,1)}, bf16[1024,256]{1,0:T(8,128)(2,1)S(1)}, u32[]{:S(2)}) copy-start(bf16[1024,256]{1,0:T(8,128)(2,1)S(1)} %collective-permute-done.7.refs_5_) | copy-start | bytes 1572868
  80.1 4.4 %copy-start.9 = (bf16[1024,256]{1,0:T(8,128)(2,1)}, bf16[1024,256]{1,0:T(8,128)(2,1)S(1)}, u32[]{:S(2)}) copy-start(bf16[1024,256]{1,0:T(8,128)(2,1)S(1)} %collective-permute-done.8.refs_6_) | copy-start | bytes 1572868
  92.3 8.2 %copy-start.4 = (bf16[640,512]{1,0:T(8,128)(2,1)S(1)}, bf16[640,512]{1,0:T(8,128)(2,1)}, u32[]{:S(2)}) copy-start(bf16[640,512]{1,0:T(8,128)(2,1)} %cot_ref.1) | copy-start | bytes 1966084
  92.3 8.2 %collective-permute-start.12 = (f32[640,512]{1,0:T(8,128)}, f32[640,512]{1,0:T(8,128)S(1)}, u32[]{:S(2)}, u32[]{:S(2)}) collective-permute-start(f32[640,512]{1,0:T(8,128)} %shard_map.139.refs_12_), channel_id=1, source_target_pairs={{0,1},{1,0},{2,3},{3,2},{4,5},{5,4},{6,7},{7,6},{8,9},{9,8},{10,11... | collective-permute-start | bytes 3932168 | tf_op jit(solution)/shard_map/ppermute | solution.py:25
  100.5 1.3 copy-start.1
  102.3 2.4 %copy-start.2 = (bf16[640,512]{1,0:T(8,128)(2,1)}, bf16[640,512]{1,0:T(8,128)(2,1)S(1)}, u32[]{:S(2)}) copy-start(bf16[640,512]{1,0:T(8,128)(2,1)S(1)} %shard_map.141.eo_ref) | copy-start | bytes 1966084
  102.3 2.4 %collective-permute-start.13 = (bf16[640,512]{1,0:T(8,128)(2,1)S(1)}, bf16[640,512]{1,0:T(8,128)(2,1)S(1)}, u32[]{:S(2)}, u32[]{:S(2)}) collective-permute-start(bf16[640,512]{1,0:T(8,128)(2,1)S(1)} %shard_map.141.eo_ref), channel_id=1, source_target_pairs={{0,1},{1,0},{2,3},{3,2},{4,5},{5,4},{6,7},{7,6},{8,9},{9,8},{10,11... | collective-permute-start | bytes 1966088 | tf_op jit(solution)/shard_map/ppermute | solution.py:25
  104.7 0.8 copy-start.11
  121.8 30.6 %all-to-all-start.2 = ((f16[4,8,128,256]{3,2,1,0:T(8,128)(2,1)}), f16[4,8,128,256]{3,2,1,0:T(8,128)(2,1)S(1)}, u32[]{:S(2)}, u32[]{:S(2)}) async-start(f16[4,8,128,256]{3,2,1,0:T(8,128)(2,1)} %bitcast.10), calls=%async_computation.2 | async-start | bytes 4194304 | tf_op jit(solution)/shard_map/all_to_all | solution.py:306
  129.7 30.4 %collective-permute-start.16 = (f16[4,8,64,256]{3,2,1,0:T(8,128)(2,1)}, f16[4,8,64,256]{3,2,1,0:T(8,128)(2,1)}, u32[]{:S(2)}, u32[]{:S(2)}) collective-permute-start(f16[4,8,64,256]{3,2,1,0:T(8,128)(2,1)} %get-tuple-element.26), channel_id=1, source_target_pairs={{64,1},{1,64},{66,3},{3,66},{68,5},{5,68},{70,7},{7,70},{72,9},{9,... | collective-permute-start | bytes 3145736 | tf_op jit(solution)/shard_map/ppermute | solution.py:39
  131.4 28.8 %collective-permute-start.17 = (f16[4,8,64,256]{3,2,1,0:T(8,128)(2,1)}, f16[4,8,64,256]{3,2,1,0:T(8,128)(2,1)}, u32[]{:S(2)}, u32[]{:S(2)}) collective-permute-start(f16[4,8,64,256]{3,2,1,0:T(8,128)(2,1)} %get-tuple-element.27), channel_id=1, source_target_pairs={{0,1},{65,64},{64,0},{1,65},{2,3},{67,66},{66,2},{3,67},{4,5},{69,... | collective-permute-start | bytes 3145736 | tf_op jit(solution)/shard_map/ppermute | solution.py:38
  153.8 22.2 %all-to-all-start.3 = ((f16[8,128,256]{2,1,0:T(8,128)(2,1)}), f16[8,128,256]{2,1,0:T(8,128)(2,1)S(1)}, u32[]{:S(2)}, u32[]{:S(2)}) async-start(f16[8,128,256]{2,1,0:T(8,128)(2,1)} %multiply_convert_fusion.3), calls=%async_computation.3 | async-start | bytes 1048576 | tf_op jit(solution)/shard_map/all_to_all | solution.py:271
  163.9 25.2 %copy-start.13 = (f32[64,512]{1,0:T(8,128)S(1)}, f32[64,512]{1,0:T(8,128)}, u32[]{:S(2)}) copy-start(f32[64,512]{1,0:T(8,128)} %copy-done.12) | copy-start | bytes 393220
  163.9 14.9 %collective-permute-start.18 = (f16[8,64,256]{2,1,0:T(8,128)(2,1)S(1)}, f16[8,64,256]{2,1,0:T(8,128)(2,1)}, u32[]{:S(2)}, u32[]{:S(2)}) collective-permute-start(f16[8,64,256]{2,1,0:T(8,128)(2,1)S(1)} %get-tuple-element.28), channel_id=1, source_target_pairs={{0,32},{16,48},{32,0},{48,16},{1,33},{17,49},{33,1},{49,17},{2,34}... | collective-permute-start | bytes 786440 | tf_op jit(solution)/shard_map/ppermute | solution.py:44
  164.9 13.9 %collective-permute-start.19 = (f16[8,64,256]{2,1,0:T(8,128)(2,1)S(1)}, f16[8,64,256]{2,1,0:T(8,128)(2,1)}, u32[]{:S(2)}, u32[]{:S(2)}) collective-permute-start(f16[8,64,256]{2,1,0:T(8,128)(2,1)S(1)} %get-tuple-element.30), channel_id=1, source_target_pairs={{0,16},{16,32},{32,48},{48,0},{1,17},{17,33},{33,49},{49,1},{2,18}... | collective-permute-start | bytes 786440 | tf_op jit(solution)/shard_map/ppermute | solution.py:44
  166.0 12.8 %collective-permute-start.20 = (f16[8,64,256]{2,1,0:T(8,128)(2,1)S(1)}, f16[8,64,256]{2,1,0:T(8,128)(2,1)}, u32[]{:S(2)}, u32[]{:S(2)}) collective-permute-start(f16[8,64,256]{2,1,0:T(8,128)(2,1)S(1)} %get-tuple-element.29), channel_id=1, source_target_pairs={{0,48},{16,0},{32,16},{48,32},{1,49},{17,1},{33,17},{49,33},{2,50}... | collective-permute-start | bytes 786440 | tf_op jit(solution)/shard_map/ppermute | solution.py:44
  176.1 13.0 %copy-start.18 = (f32[1,64,512]{2,1,0:T(8,128)S(1)}, f32[1,64,512]{2,1,0:T(8,128)}, u32[]{:S(2)}) copy-start(f32[1,64,512]{2,1,0:T(8,128)} %param.16) | copy-start | bytes 393220
  176.8 15.9 %copy-start.10 = (f32[128,256]{1,0:T(8,128)S(1)}, f32[128,256]{1,0:T(8,128)}, u32[]{:S(2)}) copy-start(f32[128,256]{1,0:T(8,128)} %broadcast_multiply_fusion.after_ref) | copy-start | bytes 393220
  178.8 10.3 %copy-start.19 = (f32[64,512]{1,0:T(8,128)S(1)}, f32[64,512]{1,0:T(8,128)}, u32[]{:S(2)}) copy-start(f32[64,512]{1,0:T(8,128)} %param.15) | copy-start | bytes 393220
  178.8 10.3 %copy-start.20 = (f32[64,512]{1,0:T(8,128)S(1)}, f32[64,512]{1,0:T(8,128)}, u32[]{:S(2)}) copy-start(f32[64,512]{1,0:T(8,128)} %param.17) | copy-start | bytes 393220
  178.8 9.5 %copy-start.22 = (f32[64,256]{1,0:T(8,128)S(1)}, f32[64,256]{1,0:T(8,128)}, u32[]{:S(2)}) copy-start(f32[64,256]{1,0:T(8,128)} %get-tuple-element.24) | copy-start | bytes 196612
  178.9 9.5 %copy-start.21 = (f32[64,256]{1,0:T(8,128)S(1)}, f32[64,256]{1,0:T(8,128)}, u32[]{:S(2)}) copy-start(f32[64,256]{1,0:T(8,128)} %get-tuple-element.25) | copy-start | bytes 196612
  181.5 18.8 %all-to-all-start.4 = ((f16[8,64,256]{2,1,0:T(8,128)(2,1)}), f16[8,64,256]{2,1,0:T(8,128)(2,1)S(1)}, u32[]{:S(2)}, u32[]{:S(2)}) async-start(f16[8,64,256]{2,1,0:T(8,128)(2,1)} %fusion.5), calls=%async_computation.4 | async-start | bytes 524288 | tf_op jit(solution)/shard_map/all_to_all | solution.py:271
  188.3 4.4 %collective-permute-start.14 = (f32[64,256]{1,0:T(8,128)S(1)}, f32[64,256]{1,0:T(8,128)S(1)}, u32[]{:S(2)}, u32[]{:S(2)}) collective-permute-start(f32[64,256]{1,0:T(8,128)S(1)} %copy-done.22), channel_id=1, source_target_pairs={{0,1},{65,64},{64,0},{1,65},{2,3},{67,66},{66,2},{3,67},{4,5},{69,... | collective-permute-start | bytes 196616 | tf_op jit(solution)/shard_map/ppermute | solution.py:38
  188.4 4.2 %collective-permute-start.15 = (f32[64,256]{1,0:T(8,128)S(1)}, f32[64,256]{1,0:T(8,128)S(1)}, u32[]{:S(2)}, u32[]{:S(2)}) collective-permute-start(f32[64,256]{1,0:T(8,128)S(1)} %copy-done.21), channel_id=1, source_target_pairs={{64,1},{1,64},{66,3},{3,66},{68,5},{5,68},{70,7},{7,70},{72,9},{9,... | collective-permute-start | bytes 196616 | tf_op jit(solution)/shard_map/ppermute | solution.py:39

commit v3 on v2

--- a/solution.py
+++ b/solution.py
@@ -1,3 +1,5 @@
+import functools
+
 import jax
 import jax.numpy as jnp
 from jax import lax
@@ -17,7 +19,7 @@
 PAIR_SCALE = 128.0
 PLANE_SCALE = 64.0
 WHOLE_SCALE = 32.0
-WIDE = 55 * 1024 * 1024
+WIDE = 20 * 1024 * 1024
 LIGHT = pl.CostEstimate(flops=1000, bytes_accessed=1000, transcendentals=0)
 
 
@@ -44,25 +46,25 @@
     return lax.ppermute(value, axis, [(i, (i + step) % size) for i in range(size)])
 
 
-def round_kernel(a_ref, b_ref, c_ref, d_ref, line_ref, other_ref, rows_ref, next_ref):
-    for i, ref in enumerate((a_ref, b_ref, c_ref, d_ref)):
+def round_kernel(a_ref, b_ref, c_ref, line_ref, side_ref, cross_ref, rows_ref, next_ref):
+    for i, ref in enumerate((a_ref, b_ref, c_ref)):
         rows_ref[i] = ref[...]
 
 
-def next_round(pieces, line, other):
+def next_round(pieces, line, side, cross):
     vmem = pl.BlockSpec(memory_space=pltpu.VMEM)
     anywhere = pl.BlockSpec(memory_space=pl.ANY)
     return pl.pallas_call(
         round_kernel,
-        in_specs=[vmem] * 4 + [anywhere] * 2,
+        in_specs=[vmem] * 3 + [anywhere] * 3,
         out_specs=[vmem, anywhere],
         out_shape=[
-            jax.ShapeDtypeStruct((4,) + pieces[0].shape, pieces[0].dtype),
+            jax.ShapeDtypeStruct((3,) + pieces[0].shape, pieces[0].dtype),
             jax.ShapeDtypeStruct(line.shape, line.dtype),
         ],
-        input_output_aliases={4: 1},
-        cost_estimate=LIGHT,
-    )(*pieces, line, other)
+        input_output_aliases={3: 1},
+        cost_estimate=LIGHT,
+    )(*pieces, line, side, cross)
 
 
 def gate_kernel(value_ref, after_ref, o_ref):
@@ -100,27 +102,32 @@
         put(cross_ref, side_ref)
 
 
-def weave_kernel(place_ref, own_ref, side_ref, cross_ref, o_ref):
+def weave_kernel(place_ref, own0_ref, side0_ref, cross0_ref, own_ref, side_ref, cross_ref, o_ref):
+    def put_near(low, high):
+        o_ref[0, :, :64] = low[...]
+        o_ref[0, :, 64:] = high[...]
+
     def put(low, high):
-        o_ref[:, :, :64] = low[...]
-        o_ref[:, :, 64:] = high[...]
-
+        o_ref[1:, :, :64] = low[...]
+        o_ref[1:, :, 64:] = high[...]
+
+    put_in_order(place_ref, own0_ref, side0_ref, cross0_ref, put_near)
     put_in_order(place_ref, own_ref, side_ref, cross_ref, put)
 
 
-def weave(place, own, side, cross):
+def weave(place, near, rest):
     vmem = pl.BlockSpec(memory_space=pltpu.VMEM)
     return pl.pallas_call(
         weave_kernel,
-        in_specs=[pl.BlockSpec(memory_space=pltpu.SMEM)] + [vmem] * 3,
+        in_specs=[pl.BlockSpec(memory_space=pltpu.SMEM)] + [vmem] * 6,
         out_specs=vmem,
         out_shape=jax.ShapeDtypeStruct((4, 8, 128, PART), jnp.bfloat16),
         compiler_params=pltpu.CompilerParams(vmem_limit_bytes=16 * 1024 * 1024),
         cost_estimate=LIGHT,
-    )(place, own, side, cross)
-
-
-def join_kernel(place_ref, own_ref, side_ref, cross_ref, start_ref, drift_ref, o_ref):
+    )(place, *near, *rest)
+
+
+def join_kernel(place_ref, own_ref, side_ref, cross_ref, start_ref, drift_ref, other_ref, o_ref):
     def put(low, high):
         o_ref[:64] = low[...]
         o_ref[64:] = high[...]
@@ -132,43 +139,50 @@
     vmem = pl.BlockSpec(memory_space=pltpu.VMEM)
     return pl.pallas_call(
         join_kernel,
-        in_specs=[pl.BlockSpec(memory_space=pltpu.SMEM)] + [vmem] * 3 + [pl.BlockSpec(memory_space=pl.ANY)] * 2,
+        in_specs=[pl.BlockSpec(memory_space=pltpu.SMEM)] + [vmem] * 3 + [pl.BlockSpec(memory_space=pl.ANY)] * 3,
         out_specs=vmem,
         out_shape=jax.ShapeDtypeStruct((128, PART), jnp.bfloat16),
         cost_estimate=LIGHT,
     )(place, own, side, cross, *after)
 
 
-def pre_kernel(place_ref, *refs):
-    columns, first, second, o_ref = refs[:4], refs[4:8], refs[8:12], refs[13]
-    for k, weights in enumerate((first, second)):
-        total = None
-        for column, part in zip(columns, weights):
-            term = jnp.dot(column[...], part[...].reshape(LINE, PART), preferred_element_type=jnp.float32)
-            total = term if total is None else total + term
-        o_ref[:, k * PART : (k + 1) * PART] = total
-
-
-def project(place, columns, first, second, after):
+def pre_kernel(count, place_ref, *refs):
+    columns, weights, o_ref = refs[:count], refs[count : 2 * count], refs[-1]
+    total = None if len(refs) == 2 * count + 2 else refs[2 * count][...]
+    for column, part in zip(columns, weights):
+        term = jnp.dot(column[...], part[...].reshape(LINE, PART), preferred_element_type=jnp.float32)
+        total = term if total is None else total + term
+    o_ref[...] = total
+
+
+def project(place, columns, weights, steps, begun, after):
     rows = 320
 
     def column_spec(step):
         return pl.BlockSpec((rows, LINE), lambda i, p: (i, p[0] + lax.rem(p[1] + step, 4)))
 
-    weight_specs = [pl.BlockSpec((LINE, PART), lambda i, p: (0, 0))] * 4
-    weight_specs += [pl.BlockSpec((1, 8, 128, PART), lambda i, p, s=step: (s, 0, 0, 0)) for step in range(4)]
-    return pl.pallas_call(
-        pre_kernel,
+    out = pl.BlockSpec((rows, PART), lambda i, p: (i, 0))
+    if isinstance(weights, list):
+        weight_specs = [pl.BlockSpec((LINE, PART), lambda i, p: (0, 0))] * len(steps)
+    else:
+        weight_specs = [pl.BlockSpec((1, 8, 128, PART), lambda i, p, s=step: (s, 0, 0, 0)) for step in steps]
+        weights = [weights] * len(steps)
+    more = [] if begun is None else [begun]
+    return pl.pallas_call(
+        functools.partial(pre_kernel, len(steps)),
         grid_spec=pltpu.PrefetchScalarGridSpec(
             num_scalar_prefetch=1,
             grid=(TOK // rows,),
-            in_specs=[column_spec(step) for step in range(4)] + weight_specs + [pl.BlockSpec(memory_space=pl.ANY)],
-            out_specs=pl.BlockSpec((rows, KV), lambda i, p: (i, 0)),
+            in_specs=[column_spec(step) for step in steps]
+            + weight_specs
+            + [out] * len(more)
+            + [pl.BlockSpec(memory_space=pl.ANY)],
+            out_specs=out,
         ),
-        out_shape=jax.ShapeDtypeStruct((TOK, KV), jnp.float32),
+        out_shape=jax.ShapeDtypeStruct((TOK, PART), jnp.float32),
         compiler_params=pltpu.CompilerParams(vmem_limit_bytes=WIDE),
         cost_estimate=LIGHT,
-    )(place, *[columns] * 4, *first, *[second] * 4, after)
+    )(place, *[columns] * len(steps), *weights, *more, after)
 
 
 def error_kernel(own_ref, got_ref, cot_ref, o_ref):
@@ -178,40 +192,39 @@
     o_ref[...] = (cot_ref[...].astype(jnp.float32) * slope).astype(jnp.bfloat16)
 
 
-def error_of(own, got, cotangent):
-    rows = 160
-    block = pl.BlockSpec((rows, KV), lambda i: (i, 0))
+def error_of(own, got, cotangent, part):
+    whole = pl.BlockSpec((TOK, PART), lambda i: (0, 0))
     return pl.pallas_call(
         error_kernel,
-        grid=(TOK // rows,),
-        in_specs=[block] * 3,
-        out_specs=block,
-        out_shape=jax.ShapeDtypeStruct((TOK, KV), jnp.bfloat16),
+        grid=(1,),
+        in_specs=[whole, whole, pl.BlockSpec((TOK, PART), lambda i: (0, part))],
+        out_specs=whole,
+        out_shape=jax.ShapeDtypeStruct((TOK, PART), jnp.bfloat16),
         compiler_params=pltpu.CompilerParams(vmem_limit_bytes=16 * 1024 * 1024),
         cost_estimate=LIGHT,
     )(own, got, cotangent)
 
 
-def grad_kernel(place_ref, xo_ref, xr_ref, eo_ref, er_ref, first_ref, second_ref):
+def grad_kernel(place_ref, xo_ref, xr_ref, eo0_ref, er0_ref, eo1_ref, er1_ref, first_ref, second_ref):
     dims = (((0,), (0,)), ((), ()))
-    part = lax.dot_general(xo_ref[...], eo_ref[...], dims, preferred_element_type=jnp.float32)
-    part = part + lax.dot_general(xr_ref[...], er_ref[...], dims, preferred_element_type=jnp.float32)
-    first_ref[...] = part[:, :PART]
-    second_ref[...] = part[:, PART:]
-
-
-def gradient(place, own, other, err_own, err_other):
+    own, other = xo_ref[...], xr_ref[...]
+    for eo_ref, er_ref, o_ref in ((eo0_ref, er0_ref, first_ref), (eo1_ref, er1_ref, second_ref)):
+        part = lax.dot_general(own, eo_ref[...], dims, preferred_element_type=jnp.float32)
+        o_ref[...] = part + lax.dot_general(other, er_ref[...], dims, preferred_element_type=jnp.float32)
+
+
+def gradient(place, own, other, errors):
     width = 1024
     each = LINE // width
     x_spec = pl.BlockSpec((TOK, width), lambda i, p: (0, p[0] * each + i))
-    e_spec = pl.BlockSpec((TOK, KV), lambda i, p: (0, 0))
+    e_spec = pl.BlockSpec((TOK, PART), lambda i, p: (0, 0))
     shape = jax.ShapeDtypeStruct((HALF, PART), jnp.float32)
     first, second = pl.pallas_call(
         grad_kernel,
         grid_spec=pltpu.PrefetchScalarGridSpec(
             num_scalar_prefetch=1,
             grid=(4 * each,),
-            in_specs=[x_spec, x_spec, e_spec, e_spec],
+            in_specs=[x_spec, x_spec] + [e_spec] * 4,
             out_specs=[
                 pl.BlockSpec((width, PART), lambda i, p: (i, 0)),
                 pl.BlockSpec((width, PART), lambda i, p: (lax.rem(i // each + 4 - p[1], 4) * each + lax.rem(i, each), 0)),
@@ -220,7 +233,7 @@
         out_shape=[shape, shape],
         compiler_params=pltpu.CompilerParams(vmem_limit_bytes=WIDE),
         cost_estimate=LIGHT,
-    )(place, own, other, err_own, err_other)
+    )(place, own, other, *errors)
     return first.reshape(4, 8, 128, PART), second.reshape(4, 8, 128, PART)
 
 
@@ -285,24 +298,33 @@
     side, cross = spread(cast[:, :PART])
     drift_other = swap(drift[0], "r")
     other = swap(inputs, "c")
-    block = join(place, cast[:, :PART], side, cross, start, drift_other)
+    block = join(place, cast[:, :PART], side, cross, start, drift_other, other)
+    near = start.reshape(8, 64, PART)
+    near = (near,) + spread(near)
     column = gather_plane(start)
-    rows, line = next_round(column, gather_line(block), other)
+    rest, line = next_round(column[1:], gather_line(block), near[1], near[2])
     half0 = gather_plane(line)
-    rows = rows.reshape(4, 8, 64, PART)
-    half1 = weave(place, rows, *spread(rows))
+    rest = rest.reshape(3, 8, 64, PART)
+    half1 = weave(place, near, (rest,) + spread(rest))
 
     delta = -(drift[0] + drift_other) / 2
     new_momentum = 0.9 * momentum + delta
     new_anchor = anchor - 0.7 * (delta + 0.9 * new_momentum)
 
     at = jnp.concatenate([4 * q, y])
-    pre_other = project(at, other, half0, half1, q)
-    got = swap(pre_other, "c")
-    pre = project(at, inputs, half0, half1, pre_other)
-    error = error_of(pre, got, cotangent)
-    error_other = swap(error, "c")
-    whole0, whole1 = gradient(at, inputs, other, error, error_other)
+    begun_other = project(at, other, half0[:1], (0,), None, q)
+    begun = project(at, inputs, half0[:1], (0,), None, begun_other)
+    pre1_other = project(at, other, half1, (0, 1, 2, 3), None, begun)
+    got1 = swap(pre1_other, "c")
+    pre1 = project(at, inputs, half1, (0, 1, 2, 3), None, pre1_other)
+    pre0_other = project(at, other, half0[1:], (1, 2, 3), begun_other, pre1)
+    got0 = swap(pre0_other, "c")
+    pre0 = project(at, inputs, half0[1:], (1, 2, 3), begun, pre0_other)
+    error1 = error_of(pre1, got1, cotangent, 1)
+    error0 = error_of(pre0, got0, cotangent, 0)
+    error1_other = swap(error1, "c")
+    error0_other = swap(error0, "c")
+    whole0, whole1 = gradient(at, inputs, other, (error0, error0_other, error1, error1_other))
     got0 = lax.all_to_all((whole0 * PART_SCALE).astype(jnp.float16), "y", 0, 0, tiled=True)
     low, high = whole1[:, :, :64], whole1[:, :, 64:]
     same, else_ = jnp.where(first_core, low, high), jnp.where(first_core, high, low)

time: 204 us -> 187 us (0.917)
  waiting for transfers between devices: 84.6 us -> 62.5 us
  starting transfers between devices: 49.3 us -> 57 us
  other arithmetic: 23.3 us -> 21 us
    ppermute x2 -> x3, waiting for transfers between devices: 19.2 us -> 3.68 us  [spread(): lax.ppermute(value, ('x', 'c'), SIDE)]
    ppermute x9, waiting for transfers between devices: 18.9 us -> 13.2 us  [shift(): lax.ppermute(value, axis, [(i, (i + step) % size) for i in range(size)])]
    pallas_call x1, Pallas kernels: 12.2 us -> 9.56 us  [gradient(): pl.pallas_call(grad_kernel, grid_spec=pltpu.PrefetchScalarGridSpec(num_sc...]
    ppermute x4 -> x6, starting transfers between devices: 1.35 us -> 3.46 us  [swap(): return lax.ppermute(value, axis, [(0, 1), (1, 0)])]
    ppermute x2 -> x3, starting transfers between devices: 3.29 us -> 4.49 us  [spread(): lax.ppermute(value, ('x', 'c'), SIDE)]
    pallas_call x4 -> x9, Pallas kernels: 18.5 us -> 19.4 us  [the longest x6 17 us: project(): pl.pallas_call(functools.partial(pre_kernel, len(steps)), grid_spec=pltpu...]
    unnamed x50 -> x62, local copies, waits for them, and re-layouts: 6.42 us -> 7.15 us
  transfers between devices with their start and end apart: 26 -> 30, of which waited for: 13 -> 13; matrix products, arithmetic and copies ran while one was open for 9% -> 9% of each run, Pallas kernels for 5% -> 10%
where the time goes in v3:
time: 187 us; the launch traced here: 185 us
  waiting for transfers between devices  62.5 us (33%)
  starting transfers between devices  57 us (30%)
  Pallas kernels  33.6 us (18%)
  other arithmetic  21 us (11%)
  local copies, waits for them, and re-layouts  9.54 us (5%)
  between operations  1.89 us (1%)
    all_to_all x1, waiting for transfers between devices, on_device(): lax.all_to_all((whole0 * PART_SCALE).astype(jnp.float16), 'y', 0, 0, tile...  19.7 us
    pallas_call x6, Pallas kernels, project(): pl.pallas_call(functools.partial(pre_kernel, len(steps)), grid_spec=pltpu...  17 us
    all_to_all x2, waiting for transfers between devices, scatter_line(): got = lax.all_to_all(total.astype(jnp.float16), 'z', 0, 0, tiled=True)  15.1 us
    ppermute x9, starting transfers between devices, shift(): lax.ppermute(value, axis, [(i, (i + step) % size) for i in range(size)])  14.3 us
    all_to_all x2, starting transfers between devices, scatter_line(): got = lax.all_to_all(total.astype(jnp.float16), 'z', 0, 0, tiled=True)  13.5 us
    ppermute x9, waiting for transfers between devices, shift(): lax.ppermute(value, axis, [(i, (i + step) % size) for i in range(size)])  13.2 us
    all_to_all x2, starting transfers between devices, gather_line(): lax.all_to_all(jnp.broadcast_to(block[None], (8, rows, PART)), 'z', 0, 0,...  12 us
    pallas_call x1, Pallas kernels, gradient(): pl.pallas_call(grad_kernel, grid_spec=pltpu.PrefetchScalarGridSpec(num_sc...  9.56 us
  transfers between devices with their start and end apart: 30, of which 13 were waited for; matrix products, arithmetic and copies ran while one was open for 9% of the time, Pallas kernels for 10%

profile of v3, /device:TPU:4, one launch (start us, length us, event | category | flops | bytes accessed | tf_op | source)
XLA Modules:
  0.0 185.5 jit_solution(7407507178961629296)
XLA Ops:
  0.7 0.9 bitcast_convert_fusion
  1.7 0.7 broadcast_in_dim.24
  2.4 8.5 %all-to-all-start = ((bf16[8,64,256]{2,1,0:T(8,128)(2,1)}), bf16[8,64,256]{2,1,0:T(8,128)(2,1)S(1)}, u32[]{:S(2)}, u32[]{:S(2)}) async-start(bf16[8,64,256]{2,1,0:T(8,128)(2,1)} %broadcast_in_dim.24), calls=%async_computation | async-start | bytes 524288 | tf_op jit(solution)/shard_map/all_to_all | solution.py:265
  11.4 2.1 %collective-permute-start.4 = (bf16[64,256]{1,0:T(8,128)(2,1)S(1)}, bf16[64,256]{1,0:T(8,128)(2,1)S(1)}, u32[]{:S(2)}, u32[]{:S(2)}) collective-permute-start(bf16[64,256]{1,0:T(8,128)(2,1)S(1)} %get-tuple-element.31.own_ref), channel_id=1, source_target_pairs={{1,0},{64,65},{0,64},{65,1},{3,2},{66,67},{2,66},{67,3},{5,4},{68,... | collective-permute-start | bytes 98312 | tf_op jit(solution)/shard_map/ppermute | solution.py:35
  13.5 0.7 collective-permute-start.5
  14.1 0.7 pad_add_fusion.1.place_ref
  14.8 2.1 %collective-permute-done.4.side_ref = bf16[64,256]{1,0:T(8,128)(2,1)S(1)} collective-permute-done((bf16[64,256]{1,0:T(8,128)(2,1)S(1)}, bf16[64,256]{1,0:T(8,128)(2,1)S(1)}, u32[]{:S(2)}, u32[]{:S(2)}) %collective-permute-start.4) | collective-permute-done | bytes 32800 | tf_op jit(solution)/shard_map/ppermute | solution.py:35
  16.9 1.6 collective-permute-done.6.drift_ref
  18.5 4.9 %all-to-all-done.own0_ref = bf16[8,64,256]{2,1,0:T(8,128)(2,1)S(1)} async-done(((bf16[8,64,256]{2,1,0:T(8,128)(2,1)}), bf16[8,64,256]{2,1,0:T(8,128)(2,1)S(1)}, u32[]{:S(2)}, u32[]{:S(2)}) %all-to-all-start) | async-done | bytes 262176 | tf_op jit(solution)/shard_map/all_to_all | solution.py:265
  23.4 0.7 copy-done.6
  24.1 1.5 shard_map.136
  25.6 1.7 broadcast_in_dim.25
  27.2 3.5 %all-to-all-start.1 = ((bf16[8,128,256]{2,1,0:T(8,128)(2,1)}), bf16[8,128,256]{2,1,0:T(8,128)(2,1)S(1)}, u32[]{:S(2)}, u32[]{:S(2)}) async-start(bf16[8,128,256]{2,1,0:T(8,128)(2,1)} %broadcast_in_dim.25), calls=%async_computation.1 | async-start | bytes 1048576 | tf_op jit(solution)/shard_map/all_to_all | solution.py:265
  30.7 3.1 %collective-permute-start.1 = (bf16[512,256]{1,0:T(8,128)(2,1)}, bf16[512,256]{1,0:T(8,128)(2,1)S(1)}, u32[]{:S(2)}, u32[]{:S(2)}) collective-permute-start(bf16[512,256]{1,0:T(8,128)(2,1)} %bitcast.43), channel_id=1, source_target_pairs={{0,48},{16,0},{32,16},{48,32},{1,49},{17,1},{33,17},{49,33},{2,50}... | collective-permute-start | bytes 786440 | tf_op jit(solution)/shard_map/ppermute | solution.py:46
  34.5 1.0 collective-permute-start.3
  35.4 1.2 collective-permute-start.7
  36.6 0.7 collective-permute-start.8
  37.3 8.2 %collective-permute-done.1.a_ref = bf16[512,256]{1,0:T(8,128)(2,1)S(1)} collective-permute-done((bf16[512,256]{1,0:T(8,128)(2,1)}, bf16[512,256]{1,0:T(8,128)(2,1)S(1)}, u32[]{:S(2)}, u32[]{:S(2)}) %collective-permute-start.1) | collective-permute-done | bytes 262176 | tf_op jit(solution)/shard_map/ppermute | solution.py:46
  45.5 3.6 %collective-permute-done.3.c_ref = bf16[512,256]{1,0:T(8,128)(2,1)S(1)} collective-permute-done((bf16[512,256]{1,0:T(8,128)(2,1)}, bf16[512,256]{1,0:T(8,128)(2,1)S(1)}, u32[]{:S(2)}, u32[]{:S(2)}) %collective-permute-start.3) | collective-permute-done | bytes 262176 | tf_op jit(solution)/shard_map/ppermute | solution.py:46
  49.2 0.6 copy-done.19
  50.3 2.0 %shard_map.137 = (bf16[3,512,256]{2,1,0:T(8,128)(2,1)}, bf16[1024,256]{1,0:T(8,128)(2,1)}) custom-call(bf16[512,256]{1,0:T(8,128)(2,1)} %copy-done.17, bf16[512,256]{1,0:T(8,128)(2,1)} %copy-done.18, bf16[512,256]{1,0:T(8,128)(2,1)} %copy-done.19, bf16[1024,256]{1,0:T(8,128)(2,1)} %bitcast.41, ...), custom_call_target="tpu_custom_call", output_to_operand_aliasing={{1}: (3, {})} | custom-call | flops 1000 | bytes 1000 | tf_op jit(solution)/shard_map/pallas_call | solution.py:57
  52.3 1.2 collective-permute-start.12
  53.5 0.7 collective-permute-start.13
  54.2 2.5 %collective-permute-start.10 = (bf16[1024,256]{1,0:T(8,128)(2,1)}, bf16[1024,256]{1,0:T(8,128)(2,1)S(1)}, u32[]{:S(2)}, u32[]{:S(2)}) collective-permute-start(bf16[1024,256]{1,0:T(8,128)(2,1)} %get-tuple-element.14.refs_1_), channel_id=1, source_target_pairs={{0,32},{16,48},{32,0},{48,16},{1,33},{17,49},{33,1},{49,17},{2,34}... | collective-permute-start | bytes 1572872 | tf_op jit(solution)/shard_map/ppermute | solution.py:46
  56.7 0.7 collective-permute-start.11
  57.3 2.6 %collective-permute-start.9 = (bf16[1024,256]{1,0:T(8,128)(2,1)}, bf16[1024,256]{1,0:T(8,128)(2,1)S(1)}, u32[]{:S(2)}, u32[]{:S(2)}) collective-permute-start(bf16[1024,256]{1,0:T(8,128)(2,1)} %get-tuple-element.14.refs_1_), channel_id=1, source_target_pairs={{0,48},{16,0},{32,16},{48,32},{1,49},{17,1},{33,17},{49,33},{2,50}... | collective-permute-start | bytes 1572872 | tf_op jit(solution)/shard_map/ppermute | solution.py:46
  60.0 1.0 copy-done.3
  61.0 2.4 %shard_map.138.refs_2_.refs_6_ = f32[640,256]{1,0:T(8,128)S(1)} custom-call(s32[2]{0:T(128)S(1)} %pad_add_fusion.place_ref, bf16[640,8192]{1,0:T(8,128)(2,1)} %collective-permute-done.other_ref.refs_0_.refs_1_.refs_2_.refs_3_.xr_ref, bf16[1024,256]{1,0:T(8,128)(2,1)S(1)} %copy-done.3, s32[1]{0:T(128)} %bitcast.1.refs_2_), custom_call_target="tpu_custom_call" | custom-call | flops 1000 | bytes 1000 | tf_op jit(solution)/shard_map/pallas_call | solution.py:171
  63.4 4.0 %copy-done = bf16[640,8192]{1,0:T(8,128)(2,1)S(1)} copy-done((bf16[640,8192]{1,0:T(8,128)(2,1)S(1)}, bf16[640,8192]{1,0:T(8,128)(2,1)}, u32[]{:S(2)}) %copy-start) | copy-done | bytes 10485784
  67.4 1.4 shard_map.139.refs_8_.refs_6_
  68.8 1.6 collective-permute-done.12.side_ref
  70.4 0.7 shard_map.140.refs_4_.refs_5_.refs_6_.refs_7_
  71.2 4.7 %shard_map.141.refs_8_ = f32[640,256]{1,0:T(8,128)S(1)} custom-call(s32[2]{0:T(128)S(1)} %pad_add_fusion.place_ref, bf16[640,8192]{1,0:T(8,128)(2,1)} %collective-permute-done.other_ref.refs_0_.refs_1_.refs_2_.refs_3_.xr_ref, bf16[640,8192]{1,0:T(8,128)(2,1)} %collective-permute-done.other_ref.refs_0_.refs_1_.refs_2_.refs_3_.xr_ref, ...), custom_call_target="tpu_custom_call" | custom-call | flops 1000 | bytes 1000 | tf_op jit(solution)/shard_map/pallas_call | solution.py:171
  75.9 2.0 %collective-permute-start.16 = (f32[640,256]{1,0:T(8,128)S(1)}, f32[640,256]{1,0:T(8,128)S(1)}, u32[]{:S(2)}, u32[]{:S(2)}) collective-permute-start(f32[640,256]{1,0:T(8,128)S(1)} %shard_map.141.refs_8_), channel_id=1, source_target_pairs={{0,1},{1,0},{2,3},{3,2},{4,5},{5,4},{6,7},{7,6},{8,9},{9,8},{10,11... | collective-permute-start | bytes 1966088 | tf_op jit(solution)/shard_map/ppermute | solution.py:27
  77.9 2.8 %shard_map.142.refs_7_.own_ref = f32[640,256]{1,0:T(8,128)S(1)} custom-call(s32[2]{0:T(128)S(1)} %pad_add_fusion.place_ref, bf16[640,8192]{1,0:T(8,128)(2,1)S(1)} %bitcast.38, bf16[640,8192]{1,0:T(8,128)(2,1)S(1)} %bitcast.38, bf16[640,8192]{1,0:T(8,128)(2,1)S(1)} %bitcast.38, bf16[640,8192]{1,0:T(8,128)(2,1)S(1)} %bitcast.38, ...), custom_call_target="tpu_custom_call" | custom-call | flops 1000 | bytes 1000 | tf_op jit(solution)/shard_map/pallas_call | solution.py:171
  80.6 1.4 collective-permute-done.11.refs_5_
  82.0 3.5 %shard_map.143.refs_7_ = f32[640,256]{1,0:T(8,128)S(1)} custom-call(s32[2]{0:T(128)S(1)} %pad_add_fusion.place_ref, bf16[640,8192]{1,0:T(8,128)(2,1)} %collective-permute-done.other_ref.refs_0_.refs_1_.refs_2_.refs_3_.xr_ref, bf16[640,8192]{1,0:T(8,128)(2,1)} %collective-permute-done.other_ref.refs_0_.refs_1_.refs_2_.refs_3_.xr_ref, ...), custom_call_target="tpu_custom_call" | custom-call | flops 1000 | bytes 1000 | tf_op jit(solution)/shard_map/pallas_call | solution.py:171
  85.7 2.3 %shard_map.144.own_ref = f32[640,256]{1,0:T(8,128)S(1)} custom-call(s32[2]{0:T(128)S(1)} %pad_add_fusion.place_ref, bf16[640,8192]{1,0:T(8,128)(2,1)S(1)} %bitcast.38, bf16[640,8192]{1,0:T(8,128)(2,1)S(1)} %bitcast.38, bf16[640,8192]{1,0:T(8,128)(2,1)S(1)} %bitcast.38, bf16[1024,256]{1,0:T(8,128)(2,1)S(1)} %collective-permute-done.9.refs_3_, ...), custom_call_target="tpu_custom_call" | custom-call | flops 1000 | bytes 1000 | tf_op jit(solution)/shard_map/pallas_call | solution.py:171
  89.2 0.8 collective-permute-done.17.er1_ref
  90.0 0.7 collective-permute-done.15.er0_ref
  90.7 9.6 %shard_map.147 = (f32[4096,256]{1,0:T(8,128)S(1)}, f32[4096,256]{1,0:T(8,128)S(1)}) custom-call(s32[2]{0:T(128)S(1)} %pad_add_fusion.place_ref, bf16[640,8192]{1,0:T(8,128)(2,1)S(1)} %bitcast.38, bf16[640,8192]{1,0:T(8,128)(2,1)} %collective-permute-done.other_ref.refs_0_.refs_1_.refs_2_.refs_3_.xr_ref, bf16[640,256]{1,0:T(8,128)(2,1)S(1)} %shard_map.145.eo0_ref, ...), custom_call_target="tpu_custom_call" | custom-call | flops 1000 | bytes 1000 | tf_op jit(solution)/shard_map/pallas_call | solution.py:222
  100.3 2.4 %multiply_convert_fusion = f16[4096,256]{1,0:T(8,128)(2,1)} fusion(f32[4096,256]{1,0:T(8,128)S(1)} %get-tuple-element.16), kind=kLoop, calls=%fused_computation.1 | loop fusion | flops 2097152 | bytes 6291456 | tf_op jit(solution)/shard_map/convert_element_type | solution.py:328
  102.9 3.6 %all-to-all-start.2 = ((f16[4,8,128,256]{3,2,1,0:T(8,128)(2,1)}), f16[4,8,128,256]{3,2,1,0:T(8,128)(2,1)S(1)}, u32[]{:S(2)}, u32[]{:S(2)}) async-start(f16[4,8,128,256]{3,2,1,0:T(8,128)(2,1)} %bitcast.10), calls=%async_computation.2 | async-start | bytes 4194304 | tf_op jit(solution)/shard_map/all_to_all | solution.py:328
  106.5 4.3 %multiply_convert_fusion.2 = (f16[4,8,64,256]{3,2,1,0:T(8,128)(2,1)}, f16[4,8,64,256]{3,2,1,0:T(8,128)(2,1)}) fusion(f32[4,8,128,256]{3,2,1,0:T(8,128)} %bitcast.39, pred[]{:T(512)} %bitcast.3, pred[]{:T(512)} %bitcast.2), kind=kLoop, calls=%fused_computation.4 | loop fusion | flops 3670016 | bytes 6291458 | tf_op jit(solution)/shard_map/convert_element_type | solution.py:332
  110.8 1.7 collective-permute-start.20
  112.5 1.3 collective-permute-start.21
  113.7 19.7 %all-to-all-done.2 = f16[4,8,128,256]{3,2,1,0:T(8,128)(2,1)S(1)} async-done(((f16[4,8,128,256]{3,2,1,0:T(8,128)(2,1)}), f16[4,8,128,256]{3,2,1,0:T(8,128)(2,1)S(1)}, u32[]{:S(2)}, u32[]{:S(2)}) %all-to-all-start.2) | async-done | bytes 2097184 | tf_op jit(solution)/shard_map/all_to_all | solution.py:328
  133.8 0.9 multiply_convert_fusion.3
  134.8 6.8 %all-to-all-start.3 = ((f16[8,128,256]{2,1,0:T(8,128)(2,1)}), f16[8,128,256]{2,1,0:T(8,128)(2,1)S(1)}, u32[]{:S(2)}, u32[]{:S(2)}) async-start(f16[8,128,256]{2,1,0:T(8,128)(2,1)} %multiply_convert_fusion.3), calls=%async_computation.3 | async-start | bytes 1048576 | tf_op jit(solution)/shard_map/all_to_all | solution.py:284
  142.9 3.5 %multiply_add_fusion = f32[4,8,64,256]{3,2,1,0:T(8,128)S(1)} fusion(f16[4,8,64,256]{3,2,1,0:T(8,128)(2,1)} %collective-permute-done.21, f16[4,8,64,256]{3,2,1,0:T(8,128)(2,1)} %collective-permute-done.20, pred[]{:T(512)} %bitcast.2, f32[4,8,128,256]{3,2,1,0:T(8,128)} %bitcast.40, pred[]{:T(512)} %bitcast.3), kind=kLoop, calls=%fused_computation.2 | loop fusion | flops 3670016 | bytes 8388610 | tf_op jit(solution)/shard_map/add | solution.py:334
  146.6 0.6 collective-permute-start.22
  147.3 1.5 collective-permute-start.23
  148.7 1.8 collective-permute-start.24
  150.5 8.0 %all-to-all-done.3 = f16[8,128,256]{2,1,0:T(8,128)(2,1)S(1)} async-done(((f16[8,128,256]{2,1,0:T(8,128)(2,1)}), f16[8,128,256]{2,1,0:T(8,128)(2,1)S(1)}, u32[]{:S(2)}, u32[]{:S(2)}) %all-to-all-start.3) | async-done | bytes 524320 | tf_op jit(solution)/shard_map/all_to_all | solution.py:284
  158.6 0.7 broadcast_multiply_fusion.after_ref
  159.8 1.5 broadcast_select_fusion
  161.4 2.7 %fusion.5 = f16[8,64,256]{2,1,0:T(8,128)(2,1)} fusion(f32[4,8,64,256]{3,2,1,0:T(8,128)S(1)} %multiply_add_fusion, f16[8,64,256]{2,1,0:T(8,128)(2,1)} %collective-permute-done.24, f16[8,64,256]{2,1,0:T(8,128)(2,1)} %collective-permute-done.23, f16[8,64,256]{2,1,0:T(8,128)(2,1)} %collective-permute-done.22, f32[]{:T(128)} %bitcast.16), kind=kLoop, calls=%fused_computation.18 | loop fusion | flops 1179648 | bytes 1572868 | tf_op jit(solution)/shard_map/convert_element_type | solution.py:284
  164.1 6.7 %all-to-all-start.4 = ((f16[8,64,256]{2,1,0:T(8,128)(2,1)}), f16[8,64,256]{2,1,0:T(8,128)(2,1)S(1)}, u32[]{:S(2)}, u32[]{:S(2)}) async-start(f16[8,64,256]{2,1,0:T(8,128)(2,1)} %fusion.5), calls=%async_computation.4 | async-start | bytes 524288 | tf_op jit(solution)/shard_map/all_to_all | solution.py:284
  170.9 0.7 collective-permute-start.19
  171.6 0.7 multiply_subtract_fusion
  172.4 2.8 %collective-permute-done.18 = f32[64,256]{1,0:T(8,128)S(1)} collective-permute-done((f32[64,256]{1,0:T(8,128)S(1)}, f32[64,256]{1,0:T(8,128)S(1)}, u32[]{:S(2)}, u32[]{:S(2)}) %collective-permute-start.18) | collective-permute-done | bytes 65568 | tf_op jit(solution)/shard_map/ppermute | solution.py:40
  175.2 0.6 select_add_fusion.g0_ref
  175.8 7.1 %all-to-all-done.4 = f16[8,64,256]{2,1,0:T(8,128)(2,1)S(1)} async-done(((f16[8,64,256]{2,1,0:T(8,128)(2,1)}), f16[8,64,256]{2,1,0:T(8,128)(2,1)S(1)}, u32[]{:S(2)}, u32[]{:S(2)}) %all-to-all-start.4) | async-done | bytes 262176 | tf_op jit(solution)/shard_map/all_to_all | solution.py:284
  183.5 1.9 %shard_map.149 = (f32[64,512]{1,0:T(8,128)}, f32[64,512]{1,0:T(8,128)}, f32[64,512]{1,0:T(8,128)}, f32[64,512]{1,0:T(8,128)}) custom-call(f32[2]{0:T(128)} %pad_maximum_fusion.s_ref, f32[64,256]{1,0:T(8,128)} %select_add_fusion.g0_ref, f32[64,256]{1,0:T(8,128)} %broadcast_multiply_fusion.1.g1_ref, f32[64,512]{1,0:T(8,128)} %bitcast.49, f32[64,512]{1,0:T(8,128)} %bitcast.50, ...), custom_call_target="tpu_custom_call" | custom-call | tf_op jit(solution)/shard_map/pallas_call | solution.py:255
  (94 shorter events, 6.1 us)
Async XLA Ops:
  0.6 22.8 %collective-permute-start = (bf16[640,8192]{1,0:T(8,128)(2,1)}, bf16[640,8192]{1,0:T(8,128)(2,1)}, u32[]{:S(2)}, u32[]{:S(2)}) collective-permute-start(bf16[640,8192]{1,0:T(8,128)(2,1)} %xo_ref.1), channel_id=1, source_target_pairs={{0,1},{1,0},{2,3},{3,2},{4,5},{5,4},{6,7},{7,6},{8,9},{9,8},{10,11... | collective-permute-start | bytes 31457288 | tf_op jit(solution)/shard_map/ppermute | solution.py:27
  1.7 21.7 %copy-start.20 = (bf16[64,256]{1,0:T(8,128)(2,1)}, bf16[64,256]{1,0:T(8,128)(2,1)S(1)}, u32[]{:S(2)}) copy-start(bf16[64,256]{1,0:T(8,128)(2,1)S(1)} %get-tuple-element.31.own_ref) | copy-start | bytes 98308
  2.4 21.0 %all-to-all-start = ((bf16[8,64,256]{2,1,0:T(8,128)(2,1)}), bf16[8,64,256]{2,1,0:T(8,128)(2,1)S(1)}, u32[]{:S(2)}, u32[]{:S(2)}) async-start(bf16[8,64,256]{2,1,0:T(8,128)(2,1)} %broadcast_in_dim.24), calls=%async_computation | async-start | bytes 524288 | tf_op jit(solution)/shard_map/all_to_all | solution.py:265
  10.9 7.6 %collective-permute-start.6 = (f32[64,512]{1,0:T(8,128)}, f32[64,512]{1,0:T(8,128)S(1)}, u32[]{:S(2)}, u32[]{:S(2)}) collective-permute-start(f32[64,512]{1,0:T(8,128)} %bitcast.52), channel_id=1, source_target_pairs={{0,128},{128,0},{1,129},{129,1},{2,130},{130,2},{3,131},{131,3},{4... | collective-permute-start | bytes 393224 | tf_op jit(solution)/shard_map/ppermute | solution.py:27
  11.4 5.5 %collective-permute-start.4 = (bf16[64,256]{1,0:T(8,128)(2,1)S(1)}, bf16[64,256]{1,0:T(8,128)(2,1)S(1)}, u32[]{:S(2)}, u32[]{:S(2)}) collective-permute-start(bf16[64,256]{1,0:T(8,128)(2,1)S(1)} %get-tuple-element.31.own_ref), channel_id=1, source_target_pairs={{1,0},{64,65},{0,64},{65,1},{3,2},{66,67},{2,66},{67,3},{5,4},{68,... | collective-permute-start | bytes 98312 | tf_op jit(solution)/shard_map/ppermute | solution.py:35
  13.5 3.5 %collective-permute-start.5 = (bf16[64,256]{1,0:T(8,128)(2,1)S(1)}, bf16[64,256]{1,0:T(8,128)(2,1)S(1)}, u32[]{:S(2)}, u32[]{:S(2)}) collective-permute-start(bf16[64,256]{1,0:T(8,128)(2,1)S(1)} %get-tuple-element.31.own_ref), channel_id=1, source_target_pairs={{1,64},{64,1},{3,66},{66,3},{5,68},{68,5},{7,70},{70,7},{9,72},{72... | collective-permute-start | bytes 98312 | tf_op jit(solution)/shard_map/ppermute | solution.py:35
  16.9 6.5 %copy-start.26 = (bf16[64,256]{1,0:T(8,128)(2,1)}, bf16[64,256]{1,0:T(8,128)(2,1)S(1)}, u32[]{:S(2)}) copy-start(bf16[64,256]{1,0:T(8,128)(2,1)S(1)} %collective-permute-done.4.side_ref) | copy-start | bytes 98308
  16.9 6.5 %copy-start.27 = (bf16[64,256]{1,0:T(8,128)(2,1)}, bf16[64,256]{1,0:T(8,128)(2,1)S(1)}, u32[]{:S(2)}) copy-start(bf16[64,256]{1,0:T(8,128)(2,1)S(1)} %collective-permute-done.5.cross_ref) | copy-start | bytes 98308
  18.5 4.9 %copy-start.15 = (f32[64,512]{1,0:T(8,128)}, f32[64,512]{1,0:T(8,128)S(1)}, u32[]{:S(2)}) copy-start(f32[64,512]{1,0:T(8,128)S(1)} %collective-permute-done.6.drift_ref) | copy-start | bytes 393220
  23.4 0.7 copy-start.6
  27.2 21.9 %all-to-all-start.1 = ((bf16[8,128,256]{2,1,0:T(8,128)(2,1)}), bf16[8,128,256]{2,1,0:T(8,128)(2,1)S(1)}, u32[]{:S(2)}, u32[]{:S(2)}) async-start(bf16[8,128,256]{2,1,0:T(8,128)(2,1)} %broadcast_in_dim.25), calls=%async_computation.1 | async-start | bytes 1048576 | tf_op jit(solution)/shard_map/all_to_all | solution.py:265
  30.7 14.8 %collective-permute-start.1 = (bf16[512,256]{1,0:T(8,128)(2,1)}, bf16[512,256]{1,0:T(8,128)(2,1)S(1)}, u32[]{:S(2)}, u32[]{:S(2)}) collective-permute-start(bf16[512,256]{1,0:T(8,128)(2,1)} %bitcast.43), channel_id=1, source_target_pairs={{0,48},{16,0},{32,16},{48,32},{1,49},{17,1},{33,17},{49,33},{2,50}... | collective-permute-start | bytes 786440 | tf_op jit(solution)/shard_map/ppermute | solution.py:46
  33.8 11.7 %collective-permute-start.2 = (bf16[512,256]{1,0:T(8,128)(2,1)}, bf16[512,256]{1,0:T(8,128)(2,1)S(1)}, u32[]{:S(2)}, u32[]{:S(2)}) collective-permute-start(bf16[512,256]{1,0:T(8,128)(2,1)} %bitcast.44), channel_id=1, source_target_pairs={{0,32},{16,48},{32,0},{48,16},{1,33},{17,49},{33,1},{49,17},{2,34}... | collective-permute-start | bytes 786440 | tf_op jit(solution)/shard_map/ppermute | solution.py:46
  34.5 14.7 %collective-permute-start.3 = (bf16[512,256]{1,0:T(8,128)(2,1)}, bf16[512,256]{1,0:T(8,128)(2,1)S(1)}, u32[]{:S(2)}, u32[]{:S(2)}) collective-permute-start(bf16[512,256]{1,0:T(8,128)(2,1)} %bitcast.45), channel_id=1, source_target_pairs={{0,16},{16,32},{32,48},{48,0},{1,17},{17,33},{33,49},{49,1},{2,18}... | collective-permute-start | bytes 786440 | tf_op jit(solution)/shard_map/ppermute | solution.py:46
  35.4 13.7 %collective-permute-start.7 = (bf16[8,64,256]{2,1,0:T(8,128)(2,1)}, bf16[8,64,256]{2,1,0:T(8,128)(2,1)S(1)}, u32[]{:S(2)}, u32[]{:S(2)}) collective-permute-start(bf16[8,64,256]{2,1,0:T(8,128)(2,1)} %copy-done.6), channel_id=1, source_target_pairs={{1,0},{64,65},{0,64},{65,1},{3,2},{66,67},{2,66},{67,3},{5,4},{68,... | collective-permute-start | bytes 786440 | tf_op jit(solution)/shard_map/ppermute | solution.py:35
  36.6 12.5 %collective-permute-start.8 = (bf16[8,64,256]{2,1,0:T(8,128)(2,1)}, bf16[8,64,256]{2,1,0:T(8,128)(2,1)S(1)}, u32[]{:S(2)}, u32[]{:S(2)}) collective-permute-start(bf16[8,64,256]{2,1,0:T(8,128)(2,1)} %copy-done.6), channel_id=1, source_target_pairs={{1,64},{64,1},{3,66},{66,3},{5,68},{68,5},{7,70},{70,7},{9,72},{72... | collective-permute-start | bytes 786440 | tf_op jit(solution)/shard_map/ppermute | solution.py:35
  45.5 3.6 %copy-start.17 = (bf16[512,256]{1,0:T(8,128)(2,1)}, bf16[512,256]{1,0:T(8,128)(2,1)S(1)}, u32[]{:S(2)}) copy-start(bf16[512,256]{1,0:T(8,128)(2,1)S(1)} %collective-permute-done.1.a_ref) | copy-start | bytes 786436
  45.5 3.7 %copy-start.18 = (bf16[512,256]{1,0:T(8,128)(2,1)}, bf16[512,256]{1,0:T(8,128)(2,1)S(1)}, u32[]{:S(2)}) copy-start(bf16[512,256]{1,0:T(8,128)(2,1)S(1)} %collective-permute-done.2.b_ref) | copy-start | bytes 786436
  49.1 0.7 copy-start.19
  49.1 0.8 copy-start.8
  49.2 0.9 copy-start.10
  49.2 1.1 copy-start.2
  52.3 18.1 %collective-permute-start.12 = (bf16[3,8,64,256]{3,2,1,0:T(8,128)(2,1)}, bf16[3,8,64,256]{3,2,1,0:T(8,128)(2,1)S(1)}, u32[]{:S(2)}, u32[]{:S(2)}) collective-permute-start(bf16[3,8,64,256]{3,2,1,0:T(8,128)(2,1)} %bitcast.46), channel_id=1, source_target_pairs={{1,0},{64,65},{0,64},{65,1},{3,2},{66,67},{2,66},{67,3},{5,4},{68,... | collective-permute-start | bytes 2359304 | tf_op jit(solution)/shard_map/ppermute | solution.py:35
  53.5 16.9 %collective-permute-start.13 = (bf16[3,8,64,256]{3,2,1,0:T(8,128)(2,1)}, bf16[3,8,64,256]{3,2,1,0:T(8,128)(2,1)S(1)}, u32[]{:S(2)}, u32[]{:S(2)}) collective-permute-start(bf16[3,8,64,256]{3,2,1,0:T(8,128)(2,1)} %bitcast.47), channel_id=1, source_target_pairs={{1,64},{64,1},{3,66},{66,3},{5,68},{68,5},{7,70},{70,7},{9,72},{72... | collective-permute-start | bytes 2359304 | tf_op jit(solution)/shard_map/ppermute | solution.py:35
  54.2 26.4 %collective-permute-start.10 = (bf16[1024,256]{1,0:T(8,128)(2,1)}, bf16[1024,256]{1,0:T(8,128)(2,1)S(1)}, u32[]{:S(2)}, u32[]{:S(2)}) collective-permute-start(bf16[1024,256]{1,0:T(8,128)(2,1)} %get-tuple-element.14.refs_1_), channel_id=1, source_target_pairs={{0,32},{16,48},{32,0},{48,16},{1,33},{17,49},{33,1},{49,17},{2,34}... | collective-permute-start | bytes 1572872 | tf_op jit(solution)/shard_map/ppermute | solution.py:46
  56.7 25.4 %collective-permute-start.11 = (bf16[1024,256]{1,0:T(8,128)(2,1)}, bf16[1024,256]{1,0:T(8,128)(2,1)S(1)}, u32[]{:S(2)}, u32[]{:S(2)}) collective-permute-start(bf16[1024,256]{1,0:T(8,128)(2,1)} %get-tuple-element.14.refs_1_), channel_id=1, source_target_pairs={{0,16},{16,32},{32,48},{48,0},{1,17},{17,33},{33,49},{49,1},{2,18}... | collective-permute-start | bytes 1572872 | tf_op jit(solution)/shard_map/ppermute | solution.py:46
  57.3 24.7 %collective-permute-start.9 = (bf16[1024,256]{1,0:T(8,128)(2,1)}, bf16[1024,256]{1,0:T(8,128)(2,1)S(1)}, u32[]{:S(2)}, u32[]{:S(2)}) collective-permute-start(bf16[1024,256]{1,0:T(8,128)(2,1)} %get-tuple-element.14.refs_1_), channel_id=1, source_target_pairs={{0,48},{16,0},{32,16},{48,32},{1,49},{17,1},{33,17},{49,33},{2,50}... | collective-permute-start | bytes 1572872 | tf_op jit(solution)/shard_map/ppermute | solution.py:46
  60.0 1.0 copy-start.3
  61.0 2.4 %copy-start.4 = (bf16[1024,256]{1,0:T(8,128)(2,1)S(1)}, bf16[1024,256]{1,0:T(8,128)(2,1)}, u32[]{:S(2)}) copy-start(bf16[1024,256]{1,0:T(8,128)(2,1)} %get-tuple-element.14.refs_1_) | copy-start | bytes 1572868
  63.4 4.0 %copy-start = (bf16[640,8192]{1,0:T(8,128)(2,1)S(1)}, bf16[640,8192]{1,0:T(8,128)(2,1)}, u32[]{:S(2)}) copy-start(bf16[640,8192]{1,0:T(8,128)(2,1)} %xo_ref.1) | copy-start | bytes 31457284
  67.4 3.0 %copy-start.7 = (bf16[8,64,256]{2,1,0:T(8,128)(2,1)S(1)}, bf16[8,64,256]{2,1,0:T(8,128)(2,1)}, u32[]{:S(2)}) copy-start(bf16[8,64,256]{2,1,0:T(8,128)(2,1)} %copy-done.6) | copy-start | bytes 786436
  67.4 3.0 %copy-start.9 = (bf16[8,64,256]{2,1,0:T(8,128)(2,1)S(1)}, bf16[8,64,256]{2,1,0:T(8,128)(2,1)}, u32[]{:S(2)}) copy-start(bf16[8,64,256]{2,1,0:T(8,128)(2,1)} %copy-done.8) | copy-start | bytes 786436
  67.4 3.0 %copy-start.11 = (bf16[8,64,256]{2,1,0:T(8,128)(2,1)S(1)}, bf16[8,64,256]{2,1,0:T(8,128)(2,1)}, u32[]{:S(2)}) copy-start(bf16[8,64,256]{2,1,0:T(8,128)(2,1)} %copy-done.10) | copy-start | bytes 786436
  67.4 3.0 %copy-start.12 = (bf16[3,512,256]{2,1,0:T(8,128)(2,1)S(1)}, bf16[3,512,256]{2,1,0:T(8,128)(2,1)}, u32[]{:S(2)}) copy-start(bf16[3,512,256]{2,1,0:T(8,128)(2,1)} %get-tuple-element.15) | copy-start | bytes 2359300
  67.4 3.0 %copy-start.13 = (s32[2]{0:T(128)S(1)}, s32[2]{0:T(128)}, u32[]{:S(2)}) copy-start(s32[2]{0:T(128)} %pad_add_fusion.1.place_ref) | copy-start | bytes 28
  70.4 7.4 %slice-start = ((s8[10485760]{0:T(1024)(128)(4,1)}), s8[4194304]{0:T(1024)(128)(4,1)S(1)}, s32[]{:S(2)}) async-start(s8[10485760]{0:T(1024)(128)(4,1)} %bitcast.37), calls=%async_computation.5 | async-start | bytes 8388608
  71.1 6.7 %slice-start.1 = ((s8[10485760]{0:T(1024)(128)(4,1)}), s8[4194304]{0:T(1024)(128)(4,1)S(1)}, s32[]{:S(2)}) async-start(s8[10485760]{0:T(1024)(128)(4,1)} %bitcast.37), calls=%async_computation.6 | async-start | bytes 8388608
  71.2 6.7 %slice-start.2 = ((s8[10485760]{0:T(1024)(128)(4,1)}), s8[2097152]{0:T(1024)(128)(4,1)S(1)}, s32[]{:S(2)}) async-start(s8[10485760]{0:T(1024)(128)(4,1)} %bitcast.37), calls=%async_computation.7 | async-start | bytes 4194304
  75.9 12.2 %collective-permute-start.16 = (f32[640,256]{1,0:T(8,128)S(1)}, f32[640,256]{1,0:T(8,128)S(1)}, u32[]{:S(2)}, u32[]{:S(2)}) collective-permute-start(f32[640,256]{1,0:T(8,128)S(1)} %shard_map.141.refs_8_), channel_id=1, source_target_pairs={{0,1},{1,0},{2,3},{3,2},{4,5},{5,4},{6,7},{7,6},{8,9},{9,8},{10,11... | collective-permute-start | bytes 1966088 | tf_op jit(solution)/shard_map/ppermute | solution.py:27
  85.5 2.5 %copy-start.5 = (bf16[640,512]{1,0:T(8,128)(2,1)S(1)}, bf16[640,512]{1,0:T(8,128)(2,1)}, u32[]{:S(2)}) copy-start(bf16[640,512]{1,0:T(8,128)(2,1)} %cot_ref.3) | copy-start | bytes 1966084
  85.5 3.2 %collective-permute-start.14 = (f32[640,256]{1,0:T(8,128)S(1)}, f32[640,256]{1,0:T(8,128)S(1)}, u32[]{:S(2)}, u32[]{:S(2)}) collective-permute-start(f32[640,256]{1,0:T(8,128)S(1)} %shard_map.143.refs_7_), channel_id=1, source_target_pairs={{0,1},{1,0},{2,3},{3,2},{4,5},{5,4},{6,7},{7,6},{8,9},{9,8},{10,11... | collective-permute-start | bytes 1966088 | tf_op jit(solution)/shard_map/ppermute | solution.py:27
  88.3 1.7 collective-permute-start.17
  89.0 1.7 collective-permute-start.15
  100.2 2.6 %copy-start.1 = (f32[4096,256]{1,0:T(8,128)}, f32[4096,256]{1,0:T(8,128)S(1)}, u32[]{:S(2)}) copy-start(f32[4096,256]{1,0:T(8,128)S(1)} %get-tuple-element.17) | copy-start | bytes 12582916
  102.9 30.5 %all-to-all-start.2 = ((f16[4,8,128,256]{3,2,1,0:T(8,128)(2,1)}), f16[4,8,128,256]{3,2,1,0:T(8,128)(2,1)S(1)}, u32[]{:S(2)}, u32[]{:S(2)}) async-start(f16[4,8,128,256]{3,2,1,0:T(8,128)(2,1)} %bitcast.10), calls=%async_computation.2 | async-start | bytes 4194304 | tf_op jit(solution)/shard_map/all_to_all | solution.py:328
  110.8 32.1 %collective-permute-start.20 = (f16[4,8,64,256]{3,2,1,0:T(8,128)(2,1)}, f16[4,8,64,256]{3,2,1,0:T(8,128)(2,1)}, u32[]{:S(2)}, u32[]{:S(2)}) collective-permute-start(f16[4,8,64,256]{3,2,1,0:T(8,128)(2,1)} %get-tuple-element.26), channel_id=1, source_target_pairs={{64,1},{1,64},{66,3},{3,66},{68,5},{5,68},{70,7},{7,70},{72,9},{9,... | collective-permute-start | bytes 3145736 | tf_op jit(solution)/shard_map/ppermute | solution.py:41
  112.5 30.4 %collective-permute-start.21 = (f16[4,8,64,256]{3,2,1,0:T(8,128)(2,1)}, f16[4,8,64,256]{3,2,1,0:T(8,128)(2,1)}, u32[]{:S(2)}, u32[]{:S(2)}) collective-permute-start(f16[4,8,64,256]{3,2,1,0:T(8,128)(2,1)} %get-tuple-element.27), channel_id=1, source_target_pairs={{0,1},{65,64},{64,0},{1,65},{2,3},{67,66},{66,2},{3,67},{4,5},{69,... | collective-permute-start | bytes 3145736 | tf_op jit(solution)/shard_map/ppermute | solution.py:40
  134.8 23.8 %all-to-all-start.3 = ((f16[8,128,256]{2,1,0:T(8,128)(2,1)}), f16[8,128,256]{2,1,0:T(8,128)(2,1)S(1)}, u32[]{:S(2)}, u32[]{:S(2)}) async-start(f16[8,128,256]{2,1,0:T(8,128)(2,1)} %multiply_convert_fusion.3), calls=%async_computation.3 | async-start | bytes 1048576 | tf_op jit(solution)/shard_map/all_to_all | solution.py:284
  146.6 25.0 %copy-start.16 = (f32[64,512]{1,0:T(8,128)S(1)}, f32[64,512]{1,0:T(8,128)}, u32[]{:S(2)}) copy-start(f32[64,512]{1,0:T(8,128)} %copy-done.15) | copy-start | bytes 393220
  146.6 14.7 %collective-permute-start.22 = (f16[8,64,256]{2,1,0:T(8,128)(2,1)S(1)}, f16[8,64,256]{2,1,0:T(8,128)(2,1)}, u32[]{:S(2)}, u32[]{:S(2)}) collective-permute-start(f16[8,64,256]{2,1,0:T(8,128)(2,1)S(1)} %get-tuple-element.28), channel_id=1, source_target_pairs={{0,32},{16,48},{32,0},{48,16},{1,33},{17,49},{33,1},{49,17},{2,34}... | collective-permute-start | bytes 786440 | tf_op jit(solution)/shard_map/ppermute | solution.py:46
  147.3 14.1 %collective-permute-start.23 = (f16[8,64,256]{2,1,0:T(8,128)(2,1)S(1)}, f16[8,64,256]{2,1,0:T(8,128)(2,1)}, u32[]{:S(2)}, u32[]{:S(2)}) collective-permute-start(f16[8,64,256]{2,1,0:T(8,128)(2,1)S(1)} %get-tuple-element.30), channel_id=1, source_target_pairs={{0,16},{16,32},{32,48},{48,0},{1,17},{17,33},{33,49},{49,1},{2,18}... | collective-permute-start | bytes 786440 | tf_op jit(solution)/shard_map/ppermute | solution.py:46
  148.7 12.7 %collective-permute-start.24 = (f16[8,64,256]{2,1,0:T(8,128)(2,1)S(1)}, f16[8,64,256]{2,1,0:T(8,128)(2,1)}, u32[]{:S(2)}, u32[]{:S(2)}) collective-permute-start(f16[8,64,256]{2,1,0:T(8,128)(2,1)S(1)} %get-tuple-element.29), channel_id=1, source_target_pairs={{0,48},{16,0},{32,16},{48,32},{1,49},{17,1},{33,17},{49,33},{2,50}... | collective-permute-start | bytes 786440 | tf_op jit(solution)/shard_map/ppermute | solution.py:46
  158.6 13.0 %copy-start.21 = (f32[1,64,512]{2,1,0:T(8,128)S(1)}, f32[1,64,512]{2,1,0:T(8,128)}, u32[]{:S(2)}) copy-start(f32[1,64,512]{2,1,0:T(8,128)} %param.16) | copy-start | bytes 393220
  159.3 15.9 %copy-start.14 = (f32[128,256]{1,0:T(8,128)S(1)}, f32[128,256]{1,0:T(8,128)}, u32[]{:S(2)}) copy-start(f32[128,256]{1,0:T(8,128)} %broadcast_multiply_fusion.after_ref) | copy-start | bytes 393220
  161.3 10.2 %copy-start.22 = (f32[64,512]{1,0:T(8,128)S(1)}, f32[64,512]{1,0:T(8,128)}, u32[]{:S(2)}) copy-start(f32[64,512]{1,0:T(8,128)} %param.15) | copy-start | bytes 393220
  161.4 10.3 %copy-start.23 = (f32[64,512]{1,0:T(8,128)S(1)}, f32[64,512]{1,0:T(8,128)}, u32[]{:S(2)}) copy-start(f32[64,512]{1,0:T(8,128)} %param.17) | copy-start | bytes 393220
  161.4 9.4 %copy-start.25 = (f32[64,256]{1,0:T(8,128)S(1)}, f32[64,256]{1,0:T(8,128)}, u32[]{:S(2)}) copy-start(f32[64,256]{1,0:T(8,128)} %get-tuple-element.24) | copy-start | bytes 196612
  161.4 9.5 %copy-start.24 = (f32[64,256]{1,0:T(8,128)S(1)}, f32[64,256]{1,0:T(8,128)}, u32[]{:S(2)}) copy-start(f32[64,256]{1,0:T(8,128)} %get-tuple-element.25) | copy-start | bytes 196612
  164.1 18.8 %all-to-all-start.4 = ((f16[8,64,256]{2,1,0:T(8,128)(2,1)}), f16[8,64,256]{2,1,0:T(8,128)(2,1)S(1)}, u32[]{:S(2)}, u32[]{:S(2)}) async-start(f16[8,64,256]{2,1,0:T(8,128)(2,1)} %fusion.5), calls=%async_computation.4 | async-start | bytes 524288 | tf_op jit(solution)/shard_map/all_to_all | solution.py:284
  170.8 4.4 %collective-permute-start.18 = (f32[64,256]{1,0:T(8,128)S(1)}, f32[64,256]{1,0:T(8,128)S(1)}, u32[]{:S(2)}, u32[]{:S(2)}) collective-permute-start(f32[64,256]{1,0:T(8,128)S(1)} %copy-done.25), channel_id=1, source_target_pairs={{0,1},{65,64},{64,0},{1,65},{2,3},{67,66},{66,2},{3,67},{4,5},{69,... | collective-permute-start | bytes 196616 | tf_op jit(solution)/shard_map/ppermute | solution.py:40
  170.9 4.2 %collective-permute-start.19 = (f32[64,256]{1,0:T(8,128)S(1)}, f32[64,256]{1,0:T(8,128)S(1)}, u32[]{:S(2)}, u32[]{:S(2)}) collective-permute-start(f32[64,256]{1,0:T(8,128)S(1)} %copy-done.24), channel_id=1, source_target_pairs={{64,1},{1,64},{66,3},{3,66},{68,5},{5,68},{70,7},{7,70},{72,9},{9,... | collective-permute-start | bytes 196616 | tf_op jit(solution)/shard_map/ppermute | solution.py:41

commit v4 on v3

--- a/solution.py
+++ b/solution.py
@@ -67,21 +67,6 @@
     )(*pieces, line, side, cross)
 
 
-def gate_kernel(value_ref, after_ref, o_ref):
-    o_ref[0] = value_ref[0]
-
-
-def gate(value, after):
-    smem = pl.BlockSpec(memory_space=pltpu.SMEM)
-    return pl.pallas_call(
-        gate_kernel,
-        in_specs=[smem, pl.BlockSpec(memory_space=pl.ANY)],
-        out_specs=smem,
-        out_shape=jax.ShapeDtypeStruct((1,), jnp.float32),
-        cost_estimate=LIGHT,
-    )(jnp.full((1,), value, jnp.float32), after)[0]
-
-
 def put_in_order(place_ref, own_ref, side_ref, cross_ref, put):
     x, q = place_ref[0], place_ref[1]
 
@@ -205,36 +190,28 @@
     )(own, got, cotangent)
 
 
-def grad_kernel(place_ref, xo_ref, xr_ref, eo0_ref, er0_ref, eo1_ref, er1_ref, first_ref, second_ref):
+def grad_kernel(place_ref, xo_ref, xr_ref, eo_ref, er_ref, after_ref, o_ref):
     dims = (((0,), (0,)), ((), ()))
-    own, other = xo_ref[...], xr_ref[...]
-    for eo_ref, er_ref, o_ref in ((eo0_ref, er0_ref, first_ref), (eo1_ref, er1_ref, second_ref)):
-        part = lax.dot_general(own, eo_ref[...], dims, preferred_element_type=jnp.float32)
-        o_ref[...] = part + lax.dot_general(other, er_ref[...], dims, preferred_element_type=jnp.float32)
-
-
-def gradient(place, own, other, errors):
-    width = 1024
-    each = LINE // width
-    x_spec = pl.BlockSpec((TOK, width), lambda i, p: (0, p[0] * each + i))
+    part = lax.dot_general(xo_ref[...], eo_ref[...], dims, preferred_element_type=jnp.float32)
+    o_ref[...] = part + lax.dot_general(xr_ref[...], er_ref[...], dims, preferred_element_type=jnp.float32)
+
+
+def gradient(place, own, other, err_own, err_other, after):
+    x_spec = pl.BlockSpec((TOK, LINE), lambda i, p: (0, p[0] + lax.rem(p[1] + i, 4)))
     e_spec = pl.BlockSpec((TOK, PART), lambda i, p: (0, 0))
-    shape = jax.ShapeDtypeStruct((HALF, PART), jnp.float32)
-    first, second = pl.pallas_call(
+    out = pl.pallas_call(
         grad_kernel,
         grid_spec=pltpu.PrefetchScalarGridSpec(
             num_scalar_prefetch=1,
-            grid=(4 * each,),
-            in_specs=[x_spec, x_spec] + [e_spec] * 4,
-            out_specs=[
-                pl.BlockSpec((width, PART), lambda i, p: (i, 0)),
-                pl.BlockSpec((width, PART), lambda i, p: (lax.rem(i // each + 4 - p[1], 4) * each + lax.rem(i, each), 0)),
-            ],
+            grid=(4,),
+            in_specs=[x_spec, x_spec, e_spec, e_spec, pl.BlockSpec(memory_space=pl.ANY)],
+            out_specs=pl.BlockSpec((LINE, PART), lambda i, p: (i, 0)),
         ),
-        out_shape=[shape, shape],
+        out_shape=jax.ShapeDtypeStruct((HALF, PART), jnp.float32),
         compiler_params=pltpu.CompilerParams(vmem_limit_bytes=WIDE),
         cost_estimate=LIGHT,
-    )(place, own, other, *errors)
-    return first.reshape(4, 8, 128, PART), second.reshape(4, 8, 128, PART)
+    )(place, own, other, err_own, err_other, after)
+    return out.reshape(4, 8, 128, PART)
 
 
 def adam_kernel(s_ref, g0_ref, g1_ref, w_ref, m_ref, v_ref, nw_ref, nm_ref, nv_ref, st_ref):
@@ -279,10 +256,17 @@
     return own + sum(g.astype(jnp.float32) for g in got) * (1.0 / scale)
 
 
-def scatter_line(total, scale, applied=None):
-    total = total * (scale if applied is None else applied)
-    got = lax.all_to_all(total.astype(jnp.float16), "z", 0, 0, tiled=True)
+def scatter_line(total, scale):
+    got = lax.all_to_all((total * scale).astype(jnp.float16), "z", 0, 0, tiled=True)
     return jnp.sum(got.astype(jnp.float32), axis=0) * (1.0 / scale)
+
+
+def scatter_by_steps(total, scale):
+    z = lax.axis_index("z")
+    turned = lax.dynamic_slice_in_dim(jnp.concatenate([total, total], axis=0), z, 8, 0)
+    sent = (turned * scale).astype(jnp.float16)
+    got = [shift(sent[step], "z", 8, step) for step in (4, 3, 5, 2, 6, 1, 7)]
+    return turned[0] + sum(g.astype(jnp.float32) for g in got) * (1.0 / scale)
 
 
 def on_device(inputs, cotangent, weight, first, second, roster_step, anchor, drift, momentum):
@@ -324,7 +308,9 @@
     error0 = error_of(pre0, got0, cotangent, 0)
     error1_other = swap(error1, "c")
     error0_other = swap(error0, "c")
-    whole0, whole1 = gradient(at, inputs, other, (error0, error0_other, error1, error1_other))
+    at_first = jnp.concatenate([4 * q, 0 * y])
+    whole1 = gradient(at, inputs, other, error1, error1_other, pre0)
+    whole0 = gradient(at_first, inputs, other, error0, error0_other, whole1)
     got0 = lax.all_to_all((whole0 * PART_SCALE).astype(jnp.float16), "y", 0, 0, tiled=True)
     low, high = whole1[:, :, :64], whole1[:, :, 64:]
     same, else_ = jnp.where(first_core, low, high), jnp.where(first_core, high, low)
@@ -342,7 +328,7 @@
     same, else_ = jnp.where(first_core, low, high), jnp.where(first_core, high, low)
     side, cross = collect(jnp.where(level, else_, same), else_)
     first0 = side + jnp.where(level, same, cross)
-    total1 = scatter_line(total_of(met1[0], sent1, PAIR_SCALE), WHOLE_SCALE, gate(WHOLE_SCALE, total0))
+    total1 = scatter_by_steps(total_of(met1[0], sent1, PAIR_SCALE), WHOLE_SCALE)
 
     step_f = roster_step[0].astype(jnp.float32)
     corr = jnp.stack([1.0 - jnp.power(jnp.float32(0.9), step_f), 1.0 - jnp.power(jnp.float32(0.95), step_f)])

time: 187 us -> 183 us (0.979); the launches traced: 185 us -> 179 us
  waiting for transfers between devices: 62.5 us -> 54.4 us
  other arithmetic: 21 us -> 16.7 us
  starting transfers between devices: 57 us -> 60.4 us
  Pallas kernels: 33.6 us -> 36.7 us
    ppermute x9 -> x16, starting transfers between devices: 14.3 us -> 24.5 us  [shift(): lax.ppermute(value, axis, [(i, (i + step) % size) for i in range(size)])]
    all_to_all x2 -> x1, waiting for transfers between devices: 15.1 us -> 5.15 us  [scatter_line(): lax.all_to_all((total * scale).astype(jnp.float16), 'z', 0, 0, tiled=True)]
    all_to_all x2 -> x1, starting transfers between devices: 13.5 us -> 5.11 us  [scatter_line(): lax.all_to_all((total * scale).astype(jnp.float16), 'z', 0, 0, tiled=True)]
    ppermute x9 -> x16, waiting for transfers between devices: 13.2 us -> 20.9 us  [shift(): lax.ppermute(value, axis, [(i, (i + step) % size) for i in range(size)])]
    pallas_call x1 -> x2, Pallas kernels: 9.56 us -> 13.3 us  [gradient(): pl.pallas_call(grad_kernel, grid_spec=pltpu.PrefetchScalarGridSpec(num_sc...]
    convert_element_type x1, other arithmetic: 4.25 us -> 0.73 us  [on_device(): cross_out = (else_ * PART_SCALE).astype(jnp.float16)]
    all_to_all x1, waiting for transfers between devices: 19.7 us -> 16.4 us  [on_device(): lax.all_to_all((whole0 * PART_SCALE).astype(jnp.float16), 'y', 0, 0, tile...]
    ppermute x2, waiting for transfers between devices: 2.79 us -> 0.01 us  [collect(): lax.ppermute(side, ('x', 'c'), [(d, s) for s, d in SIDE])]
  transfers between devices with their start and end apart: 30 -> 36, of which waited for: 13 -> 12; matrix products, arithmetic and copies ran while one was open for 9% -> 9% of each run, Pallas kernels for 10% -> 17%
where the time goes in v4:
time: 183 us; the launch traced here: 179 us
  starting transfers between devices  60.4 us (33%)
  waiting for transfers between devices  54.4 us (30%)
  Pallas kernels  36.7 us (20%)
  other arithmetic  16.7 us (9%)
  local copies, waits for them, and re-layouts  9.28 us (5%)
  between operations  1.86 us (1%)
    ppermute x16, starting transfers between devices, shift(): lax.ppermute(value, axis, [(i, (i + step) % size) for i in range(size)])  24.5 us
    ppermute x16, waiting for transfers between devices, shift(): lax.ppermute(value, axis, [(i, (i + step) % size) for i in range(size)])  20.9 us
    pallas_call x6, Pallas kernels, project(): pl.pallas_call(functools.partial(pre_kernel, len(steps)), grid_spec=pltpu...  16.9 us
    all_to_all x1, waiting for transfers between devices, on_device(): lax.all_to_all((whole0 * PART_SCALE).astype(jnp.float16), 'y', 0, 0, tile...  16.4 us
    pallas_call x2, Pallas kernels, gradient(): pl.pallas_call(grad_kernel, grid_spec=pltpu.PrefetchScalarGridSpec(num_sc...  13.3 us
    all_to_all x2, starting transfers between devices, gather_line(): lax.all_to_all(jnp.broadcast_to(block[None], (8, rows, PART)), 'z', 0, 0,...  12 us
    unnamed x50, local copies, waits for them, and re-layouts  6.85 us
    ppermute x3, waiting for transfers between devices, spread(): lax.ppermute(value, ('x', 'c'), SIDE)  5.5 us
  transfers between devices with their start and end apart: 36, of which 12 were waited for; matrix products, arithmetic and copies ran while one was open for 9% of the time, Pallas kernels for 17%

profile of v4, /device:TPU:4, one launch (start us, length us, event | category | flops | bytes accessed | tf_op | source)
XLA Modules:
  0.0 179.4 jit_solution(5349917341970198125)
XLA Ops:
  0.7 0.9 bitcast_convert_fusion
  1.7 0.7 broadcast_in_dim.24
  2.4 8.5 %all-to-all-start = ((bf16[8,64,256]{2,1,0:T(8,128)(2,1)}), bf16[8,64,256]{2,1,0:T(8,128)(2,1)S(1)}, u32[]{:S(2)}, u32[]{:S(2)}) async-start(bf16[8,64,256]{2,1,0:T(8,128)(2,1)} %broadcast_in_dim.24), calls=%async_computation | async-start | bytes 524288 | tf_op jit(solution)/shard_map/all_to_all | solution.py:242
  11.4 2.1 %collective-permute-start.4 = (bf16[64,256]{1,0:T(8,128)(2,1)S(1)}, bf16[64,256]{1,0:T(8,128)(2,1)S(1)}, u32[]{:S(2)}, u32[]{:S(2)}) collective-permute-start(bf16[64,256]{1,0:T(8,128)(2,1)S(1)} %get-tuple-element.36.own_ref), channel_id=1, source_target_pairs={{1,0},{64,65},{0,64},{65,1},{3,2},{66,67},{2,66},{67,3},{5,4},{68,... | collective-permute-start | bytes 98312 | tf_op jit(solution)/shard_map/ppermute | solution.py:35
  13.5 0.7 collective-permute-start.5
  14.1 0.7 pad_add_fusion.2.place_ref
  14.8 2.1 %collective-permute-done.4.side_ref = bf16[64,256]{1,0:T(8,128)(2,1)S(1)} collective-permute-done((bf16[64,256]{1,0:T(8,128)(2,1)S(1)}, bf16[64,256]{1,0:T(8,128)(2,1)S(1)}, u32[]{:S(2)}, u32[]{:S(2)}) %collective-permute-start.4) | collective-permute-done | bytes 32800 | tf_op jit(solution)/shard_map/ppermute | solution.py:35
  16.9 1.6 collective-permute-done.6.drift_ref
  18.5 4.9 %all-to-all-done.own0_ref = bf16[8,64,256]{2,1,0:T(8,128)(2,1)S(1)} async-done(((bf16[8,64,256]{2,1,0:T(8,128)(2,1)}), bf16[8,64,256]{2,1,0:T(8,128)(2,1)S(1)}, u32[]{:S(2)}, u32[]{:S(2)}) %all-to-all-start) | async-done | bytes 262176 | tf_op jit(solution)/shard_map/all_to_all | solution.py:242
  23.4 0.7 copy-done.6
  24.1 1.5 shard_map.136
  25.6 1.7 broadcast_in_dim.25
  27.2 3.5 %all-to-all-start.1 = ((bf16[8,128,256]{2,1,0:T(8,128)(2,1)}), bf16[8,128,256]{2,1,0:T(8,128)(2,1)S(1)}, u32[]{:S(2)}, u32[]{:S(2)}) async-start(bf16[8,128,256]{2,1,0:T(8,128)(2,1)} %broadcast_in_dim.25), calls=%async_computation.1 | async-start | bytes 1048576 | tf_op jit(solution)/shard_map/all_to_all | solution.py:242
  30.7 3.1 %collective-permute-start.1 = (bf16[512,256]{1,0:T(8,128)(2,1)}, bf16[512,256]{1,0:T(8,128)(2,1)S(1)}, u32[]{:S(2)}, u32[]{:S(2)}) collective-permute-start(bf16[512,256]{1,0:T(8,128)(2,1)} %bitcast.57), channel_id=1, source_target_pairs={{0,48},{16,0},{32,16},{48,32},{1,49},{17,1},{33,17},{49,33},{2,50}... | collective-permute-start | bytes 786440 | tf_op jit(solution)/shard_map/ppermute | solution.py:46
  34.5 1.0 collective-permute-start.3
  35.4 1.2 collective-permute-start.7
  36.6 0.7 collective-permute-start.8
  37.3 8.2 %collective-permute-done.1.a_ref = bf16[512,256]{1,0:T(8,128)(2,1)S(1)} collective-permute-done((bf16[512,256]{1,0:T(8,128)(2,1)}, bf16[512,256]{1,0:T(8,128)(2,1)S(1)}, u32[]{:S(2)}, u32[]{:S(2)}) %collective-permute-start.1) | collective-permute-done | bytes 262176 | tf_op jit(solution)/shard_map/ppermute | solution.py:46
  45.5 3.6 %collective-permute-done.3.c_ref = bf16[512,256]{1,0:T(8,128)(2,1)S(1)} collective-permute-done((bf16[512,256]{1,0:T(8,128)(2,1)}, bf16[512,256]{1,0:T(8,128)(2,1)S(1)}, u32[]{:S(2)}, u32[]{:S(2)}) %collective-permute-start.3) | collective-permute-done | bytes 262176 | tf_op jit(solution)/shard_map/ppermute | solution.py:46
  50.2 2.0 %shard_map.137 = (bf16[3,512,256]{2,1,0:T(8,128)(2,1)}, bf16[1024,256]{1,0:T(8,128)(2,1)}) custom-call(bf16[512,256]{1,0:T(8,128)(2,1)} %copy-done.16, bf16[512,256]{1,0:T(8,128)(2,1)} %copy-done.17, bf16[512,256]{1,0:T(8,128)(2,1)} %copy-done.18, bf16[1024,256]{1,0:T(8,128)(2,1)} %bitcast.55, ...), custom_call_target="tpu_custom_call", output_to_operand_aliasing={{1}: (3, {})} | custom-call | flops 1000 | bytes 1000 | tf_op jit(solution)/shard_map/pallas_call | solution.py:57
  52.3 1.2 collective-permute-start.12
  53.5 0.7 collective-permute-start.13
  54.2 2.3 %collective-permute-start.9 = (bf16[1024,256]{1,0:T(8,128)(2,1)}, bf16[1024,256]{1,0:T(8,128)(2,1)S(1)}, u32[]{:S(2)}, u32[]{:S(2)}) collective-permute-start(bf16[1024,256]{1,0:T(8,128)(2,1)} %get-tuple-element.12.refs_1_), channel_id=1, source_target_pairs={{0,48},{16,0},{32,16},{48,32},{1,49},{17,1},{33,17},{49,33},{2,50}... | collective-permute-start | bytes 1572872 | tf_op jit(solution)/shard_map/ppermute | solution.py:46
  57.1 1.0 collective-permute-start.11
  58.2 1.0 copy-done.3
  59.2 2.4 %shard_map.138.refs_2_.refs_6_ = f32[640,256]{1,0:T(8,128)S(1)} custom-call(s32[2]{0:T(128)S(1)} %pad_add_fusion.1.place_ref, bf16[640,8192]{1,0:T(8,128)(2,1)} %collective-permute-done.other_ref.refs_0_.refs_1_.refs_2_.refs_3_.xr_ref, bf16[1024,256]{1,0:T(8,128)(2,1)S(1)} %copy-done.3, s32[1]{0:T(128)} %bitcast.1.refs_2_), custom_call_target="tpu_custom_call" | custom-call | flops 1000 | bytes 1000 | tf_op jit(solution)/shard_map/pallas_call | solution.py:156
  61.6 4.0 %copy-done = bf16[640,8192]{1,0:T(8,128)(2,1)S(1)} copy-done((bf16[640,8192]{1,0:T(8,128)(2,1)S(1)}, bf16[640,8192]{1,0:T(8,128)(2,1)}, u32[]{:S(2)}) %copy-start) | copy-done | bytes 10485784
  65.6 1.4 shard_map.139.refs_8_.refs_6_
  67.0 3.4 %collective-permute-done.12.side_ref = bf16[3,8,64,256]{3,2,1,0:T(8,128)(2,1)S(1)} collective-permute-done((bf16[3,8,64,256]{3,2,1,0:T(8,128)(2,1)}, bf16[3,8,64,256]{3,2,1,0:T(8,128)(2,1)S(1)}, u32[]{:S(2)}, u32[]{:S(2)}) %collective-permute-start.12) | collective-permute-done | bytes 786464 | tf_op jit(solution)/shard_map/ppermute | solution.py:35
  70.4 0.7 shard_map.140.refs_4_.refs_5_.refs_6_.refs_7_
  71.2 4.7 %shard_map.141.refs_8_ = f32[640,256]{1,0:T(8,128)S(1)} custom-call(s32[2]{0:T(128)S(1)} %pad_add_fusion.1.place_ref, bf16[640,8192]{1,0:T(8,128)(2,1)} %collective-permute-done.other_ref.refs_0_.refs_1_.refs_2_.refs_3_.xr_ref, bf16[640,8192]{1,0:T(8,128)(2,1)} %collective-permute-done.other_ref.refs_0_.refs_1_.refs_2_.refs_3_.xr_ref, ...), custom_call_target="tpu_custom_call" | custom-call | flops 1000 | bytes 1000 | tf_op jit(solution)/shard_map/pallas_call | solution.py:156
  75.8 2.0 %collective-permute-start.16 = (f32[640,256]{1,0:T(8,128)S(1)}, f32[640,256]{1,0:T(8,128)S(1)}, u32[]{:S(2)}, u32[]{:S(2)}) collective-permute-start(f32[640,256]{1,0:T(8,128)S(1)} %shard_map.141.refs_8_), channel_id=1, source_target_pairs={{0,1},{1,0},{2,3},{3,2},{4,5},{5,4},{6,7},{7,6},{8,9},{9,8},{10,11... | collective-permute-start | bytes 1966088 | tf_op jit(solution)/shard_map/ppermute | solution.py:27
  77.8 2.7 %shard_map.142.refs_7_.own_ref = f32[640,256]{1,0:T(8,128)S(1)} custom-call(s32[2]{0:T(128)S(1)} %pad_add_fusion.1.place_ref, bf16[640,8192]{1,0:T(8,128)(2,1)S(1)} %bitcast.51, bf16[640,8192]{1,0:T(8,128)(2,1)S(1)} %bitcast.51, bf16[640,8192]{1,0:T(8,128)(2,1)S(1)} %bitcast.51, bf16[640,8192]{1,0:T(8,128)(2,1)S(1)} %bitcast.51, ...), custom_call_target="tpu_custom_call" | custom-call | flops 1000 | bytes 1000 | tf_op jit(solution)/shard_map/pallas_call | solution.py:156
  80.6 3.6 %collective-permute-done.11.refs_5_ = bf16[1024,256]{1,0:T(8,128)(2,1)S(1)} collective-permute-done((bf16[1024,256]{1,0:T(8,128)(2,1)}, bf16[1024,256]{1,0:T(8,128)(2,1)S(1)}, u32[]{:S(2)}, u32[]{:S(2)}) %collective-permute-start.11) | collective-permute-done | bytes 524320 | tf_op jit(solution)/shard_map/ppermute | solution.py:46
  84.2 3.5 %shard_map.143.refs_7_ = f32[640,256]{1,0:T(8,128)S(1)} custom-call(s32[2]{0:T(128)S(1)} %pad_add_fusion.1.place_ref, bf16[640,8192]{1,0:T(8,128)(2,1)} %collective-permute-done.other_ref.refs_0_.refs_1_.refs_2_.refs_3_.xr_ref, bf16[640,8192]{1,0:T(8,128)(2,1)} %collective-permute-done.other_ref.refs_0_.refs_1_.refs_2_.refs_3_.xr_ref, ...), custom_call_target="tpu_custom_call" | custom-call | flops 1000 | bytes 1000 | tf_op jit(solution)/shard_map/pallas_call | solution.py:156
  88.7 2.3 %shard_map.144.own_ref.after_ref = f32[640,256]{1,0:T(8,128)S(1)} custom-call(s32[2]{0:T(128)S(1)} %pad_add_fusion.1.place_ref, bf16[640,8192]{1,0:T(8,128)(2,1)S(1)} %bitcast.51, bf16[640,8192]{1,0:T(8,128)(2,1)S(1)} %bitcast.51, bf16[640,8192]{1,0:T(8,128)(2,1)S(1)} %bitcast.51, bf16[1024,256]{1,0:T(8,128)(2,1)S(1)} %collective-permute-done.9.refs_3_, ...), custom_call_target="tpu_custom_call" | custom-call | flops 1000 | bytes 1000 | tf_op jit(solution)/shard_map/pallas_call | solution.py:156
  91.4 6.6 %shard_map.147 = f32[4096,256]{1,0:T(8,128)S(1)} custom-call(s32[2]{0:T(128)S(1)} %pad_add_fusion.1.place_ref, bf16[640,8192]{1,0:T(8,128)(2,1)S(1)} %bitcast.51, bf16[640,8192]{1,0:T(8,128)(2,1)} %collective-permute-done.other_ref.refs_0_.refs_1_.refs_2_.refs_3_.xr_ref, bf16[640,256]{1,0:T(8,128)(2,1)S(1)} %shard_map.146.eo_ref, ...), custom_call_target="tpu_custom_call" | custom-call | flops 1000 | bytes 1000 | tf_op jit(solution)/shard_map/pallas_call | solution.py:202
  98.1 0.7 multiply_convert_fusion.2
  99.3 1.6 collective-permute-start.20
  100.9 6.7 %shard_map.148 = f32[4096,256]{1,0:T(8,128)S(1)} custom-call(s32[2]{0:T(128)S(1)} %pad_add_fusion.place_ref, bf16[640,8192]{1,0:T(8,128)(2,1)S(1)} %bitcast.51, bf16[640,8192]{1,0:T(8,128)(2,1)} %collective-permute-done.other_ref.refs_0_.refs_1_.refs_2_.refs_3_.xr_ref, bf16[640,256]{1,0:T(8,128)(2,1)S(1)} %shard_map.145.eo_ref, ...), custom_call_target="tpu_custom_call" | custom-call | flops 1000 | bytes 1000 | tf_op jit(solution)/shard_map/pallas_call | solution.py:202
  107.6 2.0 %multiply_convert_fusion = f16[4096,256]{1,0:T(8,128)(2,1)} fusion(f32[4096,256]{1,0:T(8,128)S(1)} %shard_map.148), kind=kLoop, calls=%fused_computation.1 | loop fusion | flops 2097152 | bytes 6291456 | tf_op jit(solution)/shard_map/convert_element_type | solution.py:314
  109.6 4.5 %all-to-all-start.2 = ((f16[4,8,128,256]{3,2,1,0:T(8,128)(2,1)}), f16[4,8,128,256]{3,2,1,0:T(8,128)(2,1)}, u32[]{:S(2)}, u32[]{:S(2)}) async-start(f16[4,8,128,256]{3,2,1,0:T(8,128)(2,1)} %bitcast.11), calls=%async_computation.2 | async-start | bytes 4194304 | tf_op jit(solution)/shard_map/all_to_all | solution.py:314
  114.8 3.2 %multiply_add_fusion = f32[4,8,64,256]{3,2,1,0:T(8,128)S(1)} fusion(f16[4,8,64,256]{3,2,1,0:T(8,128)(2,1)S(1)} %collective-permute-done.21, f16[4,8,64,256]{3,2,1,0:T(8,128)(2,1)} %collective-permute-done.20, pred[]{:T(512)} %bitcast.2, f32[4,8,128,256]{3,2,1,0:T(8,128)} %bitcast.54, pred[]{:T(512)} %bitcast.3), kind=kLoop, calls=%fused_computation.2 | loop fusion | flops 3670016 | bytes 8388610 | tf_op jit(solution)/shard_map/add | solution.py:320
  118.0 1.0 fusion.5
  119.0 3.2 %collective-permute-start.24 = (f16[8,64,256]{2,1,0:T(8,128)(2,1)}, f16[8,64,256]{2,1,0:T(8,128)(2,1)S(1)}, u32[]{:S(2)}, u32[]{:S(2)}) collective-permute-start(f16[8,64,256]{2,1,0:T(8,128)(2,1)} %get-tuple-element.27), channel_id=1, source_target_pairs={{0,48},{16,0},{32,16},{48,32},{1,49},{17,1},{33,17},{49,33},{2,50}... | collective-permute-start | bytes 786440 | tf_op jit(solution)/shard_map/ppermute | solution.py:46
  122.2 2.3 %collective-permute-start.22 = (f16[8,64,256]{2,1,0:T(8,128)(2,1)S(1)}, f16[8,64,256]{2,1,0:T(8,128)(2,1)}, u32[]{:S(2)}, u32[]{:S(2)}) collective-permute-start(f16[8,64,256]{2,1,0:T(8,128)(2,1)S(1)} %get-tuple-element.26), channel_id=1, source_target_pairs={{0,32},{16,48},{32,0},{48,16},{1,33},{17,49},{33,1},{49,17},{2,34}... | collective-permute-start | bytes 786440 | tf_op jit(solution)/shard_map/ppermute | solution.py:46
  124.5 16.4 %all-to-all-done.2 = f16[4,8,128,256]{3,2,1,0:T(8,128)(2,1)} async-done(((f16[4,8,128,256]{3,2,1,0:T(8,128)(2,1)}), f16[4,8,128,256]{3,2,1,0:T(8,128)(2,1)}, u32[]{:S(2)}, u32[]{:S(2)}) %all-to-all-start.2) | async-done | bytes 2097184 | tf_op jit(solution)/shard_map/all_to_all | solution.py:314
  140.9 2.2 %convert_reduce_fusion = f32[8,128,256]{2,1,0:T(8,128)S(1)} fusion(f16[4,8,128,256]{3,2,1,0:T(8,128)(2,1)} %all-to-all-done.2), kind=kLoop, calls=%fused_computation | loop fusion | flops 1835008 | bytes 3145728 | tf_op jit(solution)/shard_map/reduce_sum | solution.py:325
  143.1 0.9 multiply_convert_fusion.3
  144.0 5.1 %all-to-all-start.3 = ((f16[8,128,256]{2,1,0:T(8,128)(2,1)}), f16[8,128,256]{2,1,0:T(8,128)(2,1)S(1)}, u32[]{:S(2)}, u32[]{:S(2)}) async-start(f16[8,128,256]{2,1,0:T(8,128)(2,1)} %multiply_convert_fusion.3), calls=%async_computation.3 | async-start | bytes 1048576 | tf_op jit(solution)/shard_map/all_to_all | solution.py:260
  149.7 1.8 multiply_subtract_fusion
  152.1 1.1 fusion.4
  153.3 2.8 %collective-permute-start.31 = (f16[64,256]{1,0:T(8,128)(2,1)S(1)}, f16[64,256]{1,0:T(8,128)(2,1)S(1)}, u32[]{:S(2)}, u32[]{:S(2)}) collective-permute-start(f16[64,256]{1,0:T(8,128)(2,1)S(1)} %get-tuple-element.30), channel_id=1, source_target_pairs={{0,14},{2,0},{4,2},{6,4},{8,6},{10,8},{12,10},{14,12},{1,15},{3,1}... | collective-permute-start | bytes 98312 | tf_op jit(solution)/shard_map/ppermute | solution.py:46
  156.1 2.9 %collective-permute-start.29 = (f16[64,256]{1,0:T(8,128)(2,1)S(1)}, f16[64,256]{1,0:T(8,128)(2,1)S(1)}, u32[]{:S(2)}, u32[]{:S(2)}) collective-permute-start(f16[64,256]{1,0:T(8,128)(2,1)S(1)} %get-tuple-element.32), channel_id=1, source_target_pairs={{0,12},{2,14},{4,0},{6,2},{8,4},{10,6},{12,8},{14,10},{1,13},{3,15... | collective-permute-start | bytes 98312 | tf_op jit(solution)/shard_map/ppermute | solution.py:46
  159.0 3.8 %collective-permute-start.27 = (f16[64,256]{1,0:T(8,128)(2,1)S(1)}, f16[64,256]{1,0:T(8,128)(2,1)S(1)}, u32[]{:S(2)}, u32[]{:S(2)}) collective-permute-start(f16[64,256]{1,0:T(8,128)(2,1)S(1)} %get-tuple-element.34), channel_id=1, source_target_pairs={{0,10},{2,12},{4,14},{6,0},{8,2},{10,4},{12,6},{14,8},{1,11},{3,13... | collective-permute-start | bytes 98312 | tf_op jit(solution)/shard_map/ppermute | solution.py:46
  162.8 5.2 %all-to-all-done.3 = f16[8,128,256]{2,1,0:T(8,128)(2,1)S(1)} async-done(((f16[8,128,256]{2,1,0:T(8,128)(2,1)}), f16[8,128,256]{2,1,0:T(8,128)(2,1)S(1)}, u32[]{:S(2)}, u32[]{:S(2)}) %all-to-all-start.3) | async-done | bytes 524320 | tf_op jit(solution)/shard_map/all_to_all | solution.py:260
  168.2 0.9 collective-permute-start.25
  169.1 1.6 collective-permute-start.18
  170.7 0.7 collective-permute-start.19
  171.3 3.8 %collective-permute-done.26 = f16[64,256]{1,0:T(8,128)(2,1)S(1)} collective-permute-done((f16[64,256]{1,0:T(8,128)(2,1)S(1)}, f16[64,256]{1,0:T(8,128)(2,1)S(1)}, u32[]{:S(2)}, u32[]{:S(2)}) %collective-permute-start.26) | collective-permute-done | bytes 32800 | tf_op jit(solution)/shard_map/ppermute | solution.py:46
  175.1 1.0 collective-permute-done.25
  176.2 0.7 fusion.8.g1_ref
  176.8 0.6 select_add_fusion.g0_ref
  177.5 1.9 %shard_map.149 = (f32[64,512]{1,0:T(8,128)}, f32[64,512]{1,0:T(8,128)}, f32[64,512]{1,0:T(8,128)}, f32[64,512]{1,0:T(8,128)}) custom-call(f32[2]{0:T(128)} %pad_maximum_fusion.s_ref, f32[64,256]{1,0:T(8,128)} %select_add_fusion.g0_ref, f32[64,256]{1,0:T(8,128)} %fusion.8.g1_ref, f32[64,512]{1,0:T(8,128)} %bitcast.63, f32[64,512]{1,0:T(8,128)} %bitcast.64, ...), custom_call_target="tpu_custom_call" | custom-call | tf_op jit(solution)/shard_map/pallas_call | solution.py:232
  (96 shorter events, 6.6 us)
Async XLA Ops:
  0.6 22.8 %collective-permute-start = (bf16[640,8192]{1,0:T(8,128)(2,1)}, bf16[640,8192]{1,0:T(8,128)(2,1)}, u32[]{:S(2)}, u32[]{:S(2)}) collective-permute-start(bf16[640,8192]{1,0:T(8,128)(2,1)} %xo_ref.3), channel_id=1, source_target_pairs={{0,1},{1,0},{2,3},{3,2},{4,5},{5,4},{6,7},{7,6},{8,9},{9,8},{10,11... | collective-permute-start | bytes 31457288 | tf_op jit(solution)/shard_map/ppermute | solution.py:27
  1.7 21.7 %copy-start.19 = (bf16[64,256]{1,0:T(8,128)(2,1)}, bf16[64,256]{1,0:T(8,128)(2,1)S(1)}, u32[]{:S(2)}) copy-start(bf16[64,256]{1,0:T(8,128)(2,1)S(1)} %get-tuple-element.36.own_ref) | copy-start | bytes 98308
  2.4 21.0 %all-to-all-start = ((bf16[8,64,256]{2,1,0:T(8,128)(2,1)}), bf16[8,64,256]{2,1,0:T(8,128)(2,1)S(1)}, u32[]{:S(2)}, u32[]{:S(2)}) async-start(bf16[8,64,256]{2,1,0:T(8,128)(2,1)} %broadcast_in_dim.24), calls=%async_computation | async-start | bytes 524288 | tf_op jit(solution)/shard_map/all_to_all | solution.py:242
  10.9 7.6 %collective-permute-start.6 = (f32[64,512]{1,0:T(8,128)}, f32[64,512]{1,0:T(8,128)S(1)}, u32[]{:S(2)}, u32[]{:S(2)}) collective-permute-start(f32[64,512]{1,0:T(8,128)} %bitcast.66), channel_id=1, source_target_pairs={{0,128},{128,0},{1,129},{129,1},{2,130},{130,2},{3,131},{131,3},{4... | collective-permute-start | bytes 393224 | tf_op jit(solution)/shard_map/ppermute | solution.py:27
  11.4 5.5 %collective-permute-start.4 = (bf16[64,256]{1,0:T(8,128)(2,1)S(1)}, bf16[64,256]{1,0:T(8,128)(2,1)S(1)}, u32[]{:S(2)}, u32[]{:S(2)}) collective-permute-start(bf16[64,256]{1,0:T(8,128)(2,1)S(1)} %get-tuple-element.36.own_ref), channel_id=1, source_target_pairs={{1,0},{64,65},{0,64},{65,1},{3,2},{66,67},{2,66},{67,3},{5,4},{68,... | collective-permute-start | bytes 98312 | tf_op jit(solution)/shard_map/ppermute | solution.py:35
  13.5 3.5 %collective-permute-start.5 = (bf16[64,256]{1,0:T(8,128)(2,1)S(1)}, bf16[64,256]{1,0:T(8,128)(2,1)S(1)}, u32[]{:S(2)}, u32[]{:S(2)}) collective-permute-start(bf16[64,256]{1,0:T(8,128)(2,1)S(1)} %get-tuple-element.36.own_ref), channel_id=1, source_target_pairs={{1,64},{64,1},{3,66},{66,3},{5,68},{68,5},{7,70},{70,7},{9,72},{72... | collective-permute-start | bytes 98312 | tf_op jit(solution)/shard_map/ppermute | solution.py:35
  16.9 6.5 %copy-start.20 = (bf16[64,256]{1,0:T(8,128)(2,1)}, bf16[64,256]{1,0:T(8,128)(2,1)S(1)}, u32[]{:S(2)}) copy-start(bf16[64,256]{1,0:T(8,128)(2,1)S(1)} %collective-permute-done.4.side_ref) | copy-start | bytes 98308
  16.9 6.5 %copy-start.21 = (bf16[64,256]{1,0:T(8,128)(2,1)}, bf16[64,256]{1,0:T(8,128)(2,1)S(1)}, u32[]{:S(2)}) copy-start(bf16[64,256]{1,0:T(8,128)(2,1)S(1)} %collective-permute-done.5.cross_ref) | copy-start | bytes 98308
  18.5 4.9 %copy-start.14 = (f32[64,512]{1,0:T(8,128)}, f32[64,512]{1,0:T(8,128)S(1)}, u32[]{:S(2)}) copy-start(f32[64,512]{1,0:T(8,128)S(1)} %collective-permute-done.6.drift_ref) | copy-start | bytes 393220
  23.4 0.7 copy-start.6
  27.2 21.9 %all-to-all-start.1 = ((bf16[8,128,256]{2,1,0:T(8,128)(2,1)}), bf16[8,128,256]{2,1,0:T(8,128)(2,1)S(1)}, u32[]{:S(2)}, u32[]{:S(2)}) async-start(bf16[8,128,256]{2,1,0:T(8,128)(2,1)} %broadcast_in_dim.25), calls=%async_computation.1 | async-start | bytes 1048576 | tf_op jit(solution)/shard_map/all_to_all | solution.py:242
  30.7 14.8 %collective-permute-start.1 = (bf16[512,256]{1,0:T(8,128)(2,1)}, bf16[512,256]{1,0:T(8,128)(2,1)S(1)}, u32[]{:S(2)}, u32[]{:S(2)}) collective-permute-start(bf16[512,256]{1,0:T(8,128)(2,1)} %bitcast.57), channel_id=1, source_target_pairs={{0,48},{16,0},{32,16},{48,32},{1,49},{17,1},{33,17},{49,33},{2,50}... | collective-permute-start | bytes 786440 | tf_op jit(solution)/shard_map/ppermute | solution.py:46
  33.8 11.7 %collective-permute-start.2 = (bf16[512,256]{1,0:T(8,128)(2,1)}, bf16[512,256]{1,0:T(8,128)(2,1)S(1)}, u32[]{:S(2)}, u32[]{:S(2)}) collective-permute-start(bf16[512,256]{1,0:T(8,128)(2,1)} %bitcast.58), channel_id=1, source_target_pairs={{0,32},{16,48},{32,0},{48,16},{1,33},{17,49},{33,1},{49,17},{2,34}... | collective-permute-start | bytes 786440 | tf_op jit(solution)/shard_map/ppermute | solution.py:46
  34.5 14.7 %collective-permute-start.3 = (bf16[512,256]{1,0:T(8,128)(2,1)}, bf16[512,256]{1,0:T(8,128)(2,1)S(1)}, u32[]{:S(2)}, u32[]{:S(2)}) collective-permute-start(bf16[512,256]{1,0:T(8,128)(2,1)} %bitcast.59), channel_id=1, source_target_pairs={{0,16},{16,32},{32,48},{48,0},{1,17},{17,33},{33,49},{49,1},{2,18}... | collective-permute-start | bytes 786440 | tf_op jit(solution)/shard_map/ppermute | solution.py:46
  35.4 13.7 %collective-permute-start.7 = (bf16[8,64,256]{2,1,0:T(8,128)(2,1)}, bf16[8,64,256]{2,1,0:T(8,128)(2,1)S(1)}, u32[]{:S(2)}, u32[]{:S(2)}) collective-permute-start(bf16[8,64,256]{2,1,0:T(8,128)(2,1)} %copy-done.6), channel_id=1, source_target_pairs={{1,0},{64,65},{0,64},{65,1},{3,2},{66,67},{2,66},{67,3},{5,4},{68,... | collective-permute-start | bytes 786440 | tf_op jit(solution)/shard_map/ppermute | solution.py:35
  36.6 12.5 %collective-permute-start.8 = (bf16[8,64,256]{2,1,0:T(8,128)(2,1)}, bf16[8,64,256]{2,1,0:T(8,128)(2,1)S(1)}, u32[]{:S(2)}, u32[]{:S(2)}) collective-permute-start(bf16[8,64,256]{2,1,0:T(8,128)(2,1)} %copy-done.6), channel_id=1, source_target_pairs={{1,64},{64,1},{3,66},{66,3},{5,68},{68,5},{7,70},{70,7},{9,72},{72... | collective-permute-start | bytes 786440 | tf_op jit(solution)/shard_map/ppermute | solution.py:35
  45.5 3.6 %copy-start.16 = (bf16[512,256]{1,0:T(8,128)(2,1)}, bf16[512,256]{1,0:T(8,128)(2,1)S(1)}, u32[]{:S(2)}) copy-start(bf16[512,256]{1,0:T(8,128)(2,1)S(1)} %collective-permute-done.1.a_ref) | copy-start | bytes 786436
  45.5 3.7 %copy-start.17 = (bf16[512,256]{1,0:T(8,128)(2,1)}, bf16[512,256]{1,0:T(8,128)(2,1)S(1)}, u32[]{:S(2)}) copy-start(bf16[512,256]{1,0:T(8,128)(2,1)S(1)} %collective-permute-done.2.b_ref) | copy-start | bytes 786436
  49.1 0.7 copy-start.18
  49.1 0.8 copy-start.8
  49.2 0.9 copy-start.10
  49.2 1.1 copy-start.2
  52.3 18.1 %collective-permute-start.12 = (bf16[3,8,64,256]{3,2,1,0:T(8,128)(2,1)}, bf16[3,8,64,256]{3,2,1,0:T(8,128)(2,1)S(1)}, u32[]{:S(2)}, u32[]{:S(2)}) collective-permute-start(bf16[3,8,64,256]{3,2,1,0:T(8,128)(2,1)} %bitcast.60), channel_id=1, source_target_pairs={{1,0},{64,65},{0,64},{65,1},{3,2},{66,67},{2,66},{67,3},{5,4},{68,... | collective-permute-start | bytes 2359304 | tf_op jit(solution)/shard_map/ppermute | solution.py:35
  53.5 16.9 %collective-permute-start.13 = (bf16[3,8,64,256]{3,2,1,0:T(8,128)(2,1)}, bf16[3,8,64,256]{3,2,1,0:T(8,128)(2,1)S(1)}, u32[]{:S(2)}, u32[]{:S(2)}) collective-permute-start(bf16[3,8,64,256]{3,2,1,0:T(8,128)(2,1)} %bitcast.61), channel_id=1, source_target_pairs={{1,64},{64,1},{3,66},{66,3},{5,68},{68,5},{7,70},{70,7},{9,72},{72... | collective-permute-start | bytes 2359304 | tf_op jit(solution)/shard_map/ppermute | solution.py:35
  54.2 26.4 %collective-permute-start.9 = (bf16[1024,256]{1,0:T(8,128)(2,1)}, bf16[1024,256]{1,0:T(8,128)(2,1)S(1)}, u32[]{:S(2)}, u32[]{:S(2)}) collective-permute-start(bf16[1024,256]{1,0:T(8,128)(2,1)} %get-tuple-element.12.refs_1_), channel_id=1, source_target_pairs={{0,48},{16,0},{32,16},{48,32},{1,49},{17,1},{33,17},{49,33},{2,50}... | collective-permute-start | bytes 1572872 | tf_op jit(solution)/shard_map/ppermute | solution.py:46
  56.5 24.1 %collective-permute-start.10 = (bf16[1024,256]{1,0:T(8,128)(2,1)}, bf16[1024,256]{1,0:T(8,128)(2,1)S(1)}, u32[]{:S(2)}, u32[]{:S(2)}) collective-permute-start(bf16[1024,256]{1,0:T(8,128)(2,1)} %get-tuple-element.12.refs_1_), channel_id=1, source_target_pairs={{0,32},{16,48},{32,0},{48,16},{1,33},{17,49},{33,1},{49,17},{2,34}... | collective-permute-start | bytes 1572872 | tf_op jit(solution)/shard_map/ppermute | solution.py:46
  57.1 27.1 %collective-permute-start.11 = (bf16[1024,256]{1,0:T(8,128)(2,1)}, bf16[1024,256]{1,0:T(8,128)(2,1)S(1)}, u32[]{:S(2)}, u32[]{:S(2)}) collective-permute-start(bf16[1024,256]{1,0:T(8,128)(2,1)} %get-tuple-element.12.refs_1_), channel_id=1, source_target_pairs={{0,16},{16,32},{32,48},{48,0},{1,17},{17,33},{33,49},{49,1},{2,18}... | collective-permute-start | bytes 1572872 | tf_op jit(solution)/shard_map/ppermute | solution.py:46
  58.2 1.0 copy-start.3
  59.2 2.4 %copy-start.4 = (bf16[1024,256]{1,0:T(8,128)(2,1)S(1)}, bf16[1024,256]{1,0:T(8,128)(2,1)}, u32[]{:S(2)}) copy-start(bf16[1024,256]{1,0:T(8,128)(2,1)} %get-tuple-element.12.refs_1_) | copy-start | bytes 1572868
  61.6 4.0 %copy-start = (bf16[640,8192]{1,0:T(8,128)(2,1)S(1)}, bf16[640,8192]{1,0:T(8,128)(2,1)}, u32[]{:S(2)}) copy-start(bf16[640,8192]{1,0:T(8,128)(2,1)} %xo_ref.3) | copy-start | bytes 31457284
  65.6 4.8 %copy-start.7 = (bf16[8,64,256]{2,1,0:T(8,128)(2,1)S(1)}, bf16[8,64,256]{2,1,0:T(8,128)(2,1)}, u32[]{:S(2)}) copy-start(bf16[8,64,256]{2,1,0:T(8,128)(2,1)} %copy-done.6) | copy-start | bytes 786436
  65.6 4.8 %copy-start.9 = (bf16[8,64,256]{2,1,0:T(8,128)(2,1)S(1)}, bf16[8,64,256]{2,1,0:T(8,128)(2,1)}, u32[]{:S(2)}) copy-start(bf16[8,64,256]{2,1,0:T(8,128)(2,1)} %copy-done.8) | copy-start | bytes 786436
  65.6 4.8 %copy-start.11 = (bf16[8,64,256]{2,1,0:T(8,128)(2,1)S(1)}, bf16[8,64,256]{2,1,0:T(8,128)(2,1)}, u32[]{:S(2)}) copy-start(bf16[8,64,256]{2,1,0:T(8,128)(2,1)} %copy-done.10) | copy-start | bytes 786436
  65.6 4.8 %copy-start.12 = (bf16[3,512,256]{2,1,0:T(8,128)(2,1)S(1)}, bf16[3,512,256]{2,1,0:T(8,128)(2,1)}, u32[]{:S(2)}) copy-start(bf16[3,512,256]{2,1,0:T(8,128)(2,1)} %get-tuple-element.13) | copy-start | bytes 2359300
  65.6 4.8 %copy-start.13 = (s32[2]{0:T(128)S(1)}, s32[2]{0:T(128)}, u32[]{:S(2)}) copy-start(s32[2]{0:T(128)} %pad_add_fusion.2.place_ref) | copy-start | bytes 28
  70.4 7.4 %slice-start = ((s8[10485760]{0:T(1024)(128)(4,1)}), s8[4194304]{0:T(1024)(128)(4,1)S(1)}, s32[]{:S(2)}) async-start(s8[10485760]{0:T(1024)(128)(4,1)} %bitcast.50), calls=%async_computation.4 | async-start | bytes 8388608
  71.1 6.7 %slice-start.1 = ((s8[10485760]{0:T(1024)(128)(4,1)}), s8[4194304]{0:T(1024)(128)(4,1)S(1)}, s32[]{:S(2)}) async-start(s8[10485760]{0:T(1024)(128)(4,1)} %bitcast.50), calls=%async_computation.5 | async-start | bytes 8388608
  71.1 6.7 %slice-start.2 = ((s8[10485760]{0:T(1024)(128)(4,1)}), s8[2097152]{0:T(1024)(128)(4,1)S(1)}, s32[]{:S(2)}) async-start(s8[10485760]{0:T(1024)(128)(4,1)} %bitcast.50), calls=%async_computation.6 | async-start | bytes 4194304
  75.8 12.1 %collective-permute-start.16 = (f32[640,256]{1,0:T(8,128)S(1)}, f32[640,256]{1,0:T(8,128)S(1)}, u32[]{:S(2)}, u32[]{:S(2)}) collective-permute-start(f32[640,256]{1,0:T(8,128)S(1)} %shard_map.141.refs_8_), channel_id=1, source_target_pairs={{0,1},{1,0},{2,3},{3,2},{4,5},{5,4},{6,7},{7,6},{8,9},{9,8},{10,11... | collective-permute-start | bytes 1966088 | tf_op jit(solution)/shard_map/ppermute | solution.py:27
  80.5 7.4 %copy-start.5 = (bf16[640,512]{1,0:T(8,128)(2,1)S(1)}, bf16[640,512]{1,0:T(8,128)(2,1)}, u32[]{:S(2)}) copy-start(bf16[640,512]{1,0:T(8,128)(2,1)} %cot_ref.3) | copy-start | bytes 1966084
  87.7 3.3 %collective-permute-start.14 = (f32[640,256]{1,0:T(8,128)S(1)}, f32[640,256]{1,0:T(8,128)S(1)}, u32[]{:S(2)}, u32[]{:S(2)}) collective-permute-start(f32[640,256]{1,0:T(8,128)S(1)} %shard_map.143.refs_7_), channel_id=1, source_target_pairs={{0,1},{1,0},{2,3},{3,2},{4,5},{5,4},{6,7},{7,6},{8,9},{9,8},{10,11... | collective-permute-start | bytes 1966088 | tf_op jit(solution)/shard_map/ppermute | solution.py:27
  88.1 3.3 %collective-permute-start.17 = (bf16[640,256]{1,0:T(8,128)(2,1)S(1)}, bf16[640,256]{1,0:T(8,128)(2,1)S(1)}, u32[]{:S(2)}, u32[]{:S(2)}) collective-permute-start(bf16[640,256]{1,0:T(8,128)(2,1)S(1)} %shard_map.146.eo_ref), channel_id=1, source_target_pairs={{0,1},{1,0},{2,3},{3,2},{4,5},{5,4},{6,7},{7,6},{8,9},{9,8},{10,11... | collective-permute-start | bytes 983048 | tf_op jit(solution)/shard_map/ppermute | solution.py:27
  91.2 9.7 %collective-permute-start.15 = (bf16[640,256]{1,0:T(8,128)(2,1)S(1)}, bf16[640,256]{1,0:T(8,128)(2,1)S(1)}, u32[]{:S(2)}, u32[]{:S(2)}) collective-permute-start(bf16[640,256]{1,0:T(8,128)(2,1)S(1)} %shard_map.145.eo_ref), channel_id=1, source_target_pairs={{0,1},{1,0},{2,3},{3,2},{4,5},{5,4},{6,7},{7,6},{8,9},{9,8},{10,11... | collective-permute-start | bytes 983048 | tf_op jit(solution)/shard_map/ppermute | solution.py:27
  98.0 2.9 %copy-start.1 = (f32[4096,256]{1,0:T(8,128)}, f32[4096,256]{1,0:T(8,128)S(1)}, u32[]{:S(2)}) copy-start(f32[4096,256]{1,0:T(8,128)S(1)} %shard_map.147) | copy-start | bytes 12582916
  98.8 16.0 %collective-permute-start.21 = (f16[4,8,64,256]{3,2,1,0:T(8,128)(2,1)S(1)}, f16[4,8,64,256]{3,2,1,0:T(8,128)(2,1)S(1)}, u32[]{:S(2)}, u32[]{:S(2)}) collective-permute-start(f16[4,8,64,256]{3,2,1,0:T(8,128)(2,1)S(1)} %get-tuple-element.25), channel_id=1, source_target_pairs={{0,1},{65,64},{64,0},{1,65},{2,3},{67,66},{66,2},{3,67},{4,5},{69,... | collective-permute-start | bytes 3145736 | tf_op jit(solution)/shard_map/ppermute | solution.py:40
  99.3 15.5 %collective-permute-start.20 = (f16[4,8,64,256]{3,2,1,0:T(8,128)(2,1)S(1)}, f16[4,8,64,256]{3,2,1,0:T(8,128)(2,1)}, u32[]{:S(2)}, u32[]{:S(2)}) collective-permute-start(f16[4,8,64,256]{3,2,1,0:T(8,128)(2,1)S(1)} %get-tuple-element.24), channel_id=1, source_target_pairs={{64,1},{1,64},{66,3},{3,66},{68,5},{5,68},{70,7},{7,70},{72,9},{9,... | collective-permute-start | bytes 3145736 | tf_op jit(solution)/shard_map/ppermute | solution.py:41
  109.6 31.3 %all-to-all-start.2 = ((f16[4,8,128,256]{3,2,1,0:T(8,128)(2,1)}), f16[4,8,128,256]{3,2,1,0:T(8,128)(2,1)}, u32[]{:S(2)}, u32[]{:S(2)}) async-start(f16[4,8,128,256]{3,2,1,0:T(8,128)(2,1)} %bitcast.11), calls=%async_computation.2 | async-start | bytes 4194304 | tf_op jit(solution)/shard_map/all_to_all | solution.py:314
  119.0 32.5 %collective-permute-start.24 = (f16[8,64,256]{2,1,0:T(8,128)(2,1)}, f16[8,64,256]{2,1,0:T(8,128)(2,1)S(1)}, u32[]{:S(2)}, u32[]{:S(2)}) collective-permute-start(f16[8,64,256]{2,1,0:T(8,128)(2,1)} %get-tuple-element.27), channel_id=1, source_target_pairs={{0,48},{16,0},{32,16},{48,32},{1,49},{17,1},{33,17},{49,33},{2,50}... | collective-permute-start | bytes 786440 | tf_op jit(solution)/shard_map/ppermute | solution.py:46
  122.2 29.3 %collective-permute-start.23 = (f16[8,64,256]{2,1,0:T(8,128)(2,1)}, f16[8,64,256]{2,1,0:T(8,128)(2,1)S(1)}, u32[]{:S(2)}, u32[]{:S(2)}) collective-permute-start(f16[8,64,256]{2,1,0:T(8,128)(2,1)} %get-tuple-element.28), channel_id=1, source_target_pairs={{0,16},{16,32},{32,48},{48,0},{1,17},{17,33},{33,49},{49,1},{2,18}... | collective-permute-start | bytes 786440 | tf_op jit(solution)/shard_map/ppermute | solution.py:46
  122.2 29.9 %collective-permute-start.22 = (f16[8,64,256]{2,1,0:T(8,128)(2,1)S(1)}, f16[8,64,256]{2,1,0:T(8,128)(2,1)}, u32[]{:S(2)}, u32[]{:S(2)}) collective-permute-start(f16[8,64,256]{2,1,0:T(8,128)(2,1)S(1)} %get-tuple-element.26), channel_id=1, source_target_pairs={{0,32},{16,48},{32,0},{48,16},{1,33},{17,49},{33,1},{49,17},{2,34}... | collective-permute-start | bytes 786440 | tf_op jit(solution)/shard_map/ppermute | solution.py:46
  143.0 6.7 %copy-start.15 = (f32[64,512]{1,0:T(8,128)S(1)}, f32[64,512]{1,0:T(8,128)}, u32[]{:S(2)}) copy-start(f32[64,512]{1,0:T(8,128)} %copy-done.14) | copy-start | bytes 393220
  144.0 24.0 %all-to-all-start.3 = ((f16[8,128,256]{2,1,0:T(8,128)(2,1)}), f16[8,128,256]{2,1,0:T(8,128)(2,1)S(1)}, u32[]{:S(2)}, u32[]{:S(2)}) async-start(f16[8,128,256]{2,1,0:T(8,128)(2,1)} %multiply_convert_fusion.3), calls=%async_computation.3 | async-start | bytes 1048576 | tf_op jit(solution)/shard_map/all_to_all | solution.py:260
  153.3 14.7 %collective-permute-start.31 = (f16[64,256]{1,0:T(8,128)(2,1)S(1)}, f16[64,256]{1,0:T(8,128)(2,1)S(1)}, u32[]{:S(2)}, u32[]{:S(2)}) collective-permute-start(f16[64,256]{1,0:T(8,128)(2,1)S(1)} %get-tuple-element.30), channel_id=1, source_target_pairs={{0,14},{2,0},{4,2},{6,4},{8,6},{10,8},{12,10},{14,12},{1,15},{3,1}... | collective-permute-start | bytes 98312 | tf_op jit(solution)/shard_map/ppermute | solution.py:46
  156.1 12.1 %collective-permute-start.30 = (f16[64,256]{1,0:T(8,128)(2,1)S(1)}, f16[64,256]{1,0:T(8,128)(2,1)S(1)}, u32[]{:S(2)}, u32[]{:S(2)}) collective-permute-start(f16[64,256]{1,0:T(8,128)(2,1)S(1)} %get-tuple-element.31), channel_id=1, source_target_pairs={{0,2},{2,4},{4,6},{6,8},{8,10},{10,12},{12,14},{14,0},{1,3},{3,5},... | collective-permute-start | bytes 98312 | tf_op jit(solution)/shard_map/ppermute | solution.py:46
  156.1 13.0 %collective-permute-start.29 = (f16[64,256]{1,0:T(8,128)(2,1)S(1)}, f16[64,256]{1,0:T(8,128)(2,1)S(1)}, u32[]{:S(2)}, u32[]{:S(2)}) collective-permute-start(f16[64,256]{1,0:T(8,128)(2,1)S(1)} %get-tuple-element.32), channel_id=1, source_target_pairs={{0,12},{2,14},{4,0},{6,2},{8,4},{10,6},{12,8},{14,10},{1,13},{3,15... | collective-permute-start | bytes 98312 | tf_op jit(solution)/shard_map/ppermute | solution.py:46
  159.0 11.6 %collective-permute-start.28 = (f16[64,256]{1,0:T(8,128)(2,1)S(1)}, f16[64,256]{1,0:T(8,128)(2,1)S(1)}, u32[]{:S(2)}, u32[]{:S(2)}) collective-permute-start(f16[64,256]{1,0:T(8,128)(2,1)S(1)} %get-tuple-element.33), channel_id=1, source_target_pairs={{0,4},{2,6},{4,8},{6,10},{8,12},{10,14},{12,0},{14,2},{1,5},{3,7},... | collective-permute-start | bytes 98312 | tf_op jit(solution)/shard_map/ppermute | solution.py:46
  159.0 12.3 %collective-permute-start.27 = (f16[64,256]{1,0:T(8,128)(2,1)S(1)}, f16[64,256]{1,0:T(8,128)(2,1)S(1)}, u32[]{:S(2)}, u32[]{:S(2)}) collective-permute-start(f16[64,256]{1,0:T(8,128)(2,1)S(1)} %get-tuple-element.34), channel_id=1, source_target_pairs={{0,10},{2,12},{4,14},{6,0},{8,2},{10,4},{12,6},{14,8},{1,11},{3,13... | collective-permute-start | bytes 98312 | tf_op jit(solution)/shard_map/ppermute | solution.py:46
  168.1 7.0 %collective-permute-start.26 = (f16[64,256]{1,0:T(8,128)(2,1)S(1)}, f16[64,256]{1,0:T(8,128)(2,1)S(1)}, u32[]{:S(2)}, u32[]{:S(2)}) collective-permute-start(f16[64,256]{1,0:T(8,128)(2,1)S(1)} %get-tuple-element.35), channel_id=1, source_target_pairs={{0,6},{2,8},{4,10},{6,12},{8,14},{10,0},{12,2},{14,4},{1,7},{3,9},... | collective-permute-start | bytes 98312 | tf_op jit(solution)/shard_map/ppermute | solution.py:46
  168.2 8.0 %collective-permute-start.25 = (f16[64,256]{1,0:T(8,128)(2,1)S(1)}, f16[64,256]{1,0:T(8,128)(2,1)S(1)}, u32[]{:S(2)}, u32[]{:S(2)}) collective-permute-start(f16[64,256]{1,0:T(8,128)(2,1)S(1)} %get-tuple-element.29), channel_id=1, source_target_pairs={{0,8},{2,10},{4,12},{6,14},{8,0},{10,2},{12,4},{14,6},{1,9},{3,11}... | collective-permute-start | bytes 98312 | tf_op jit(solution)/shard_map/ppermute | solution.py:46
  169.1 7.7 %collective-permute-start.18 = (f32[64,256]{1,0:T(8,128)S(1)}, f32[64,256]{1,0:T(8,128)S(1)}, u32[]{:S(2)}, u32[]{:S(2)}) collective-permute-start(f32[64,256]{1,0:T(8,128)S(1)} %get-tuple-element.22), channel_id=1, source_target_pairs={{0,1},{65,64},{64,0},{1,65},{2,3},{67,66},{66,2},{3,67},{4,5},{69,... | collective-permute-start | bytes 196616 | tf_op jit(solution)/shard_map/ppermute | solution.py:40
  170.7 6.2 %collective-permute-start.19 = (f32[64,256]{1,0:T(8,128)S(1)}, f32[64,256]{1,0:T(8,128)S(1)}, u32[]{:S(2)}, u32[]{:S(2)}) collective-permute-start(f32[64,256]{1,0:T(8,128)S(1)} %get-tuple-element.23), channel_id=1, source_target_pairs={{64,1},{1,64},{66,3},{3,66},{68,5},{5,68},{70,7},{7,70},{72,9},{9,... | collective-permute-start | bytes 196616 | tf_op jit(solution)/shard_map/ppermute | solution.py:41

commit v5 on v4

--- a/solution.py
+++ b/solution.py
@@ -46,25 +46,20 @@
     return lax.ppermute(value, axis, [(i, (i + step) % size) for i in range(size)])
 
 
-def round_kernel(a_ref, b_ref, c_ref, line_ref, side_ref, cross_ref, rows_ref, next_ref):
+def stack_kernel(a_ref, b_ref, c_ref, line_ref, side_ref, cross_ref, rows_ref):
     for i, ref in enumerate((a_ref, b_ref, c_ref)):
         rows_ref[i] = ref[...]
 
 
-def next_round(pieces, line, side, cross):
+def stack_after(pieces, *after):
     vmem = pl.BlockSpec(memory_space=pltpu.VMEM)
-    anywhere = pl.BlockSpec(memory_space=pl.ANY)
-    return pl.pallas_call(
-        round_kernel,
-        in_specs=[vmem] * 3 + [anywhere] * 3,
-        out_specs=[vmem, anywhere],
-        out_shape=[
-            jax.ShapeDtypeStruct((3,) + pieces[0].shape, pieces[0].dtype),
-            jax.ShapeDtypeStruct(line.shape, line.dtype),
-        ],
-        input_output_aliases={3: 1},
-        cost_estimate=LIGHT,
-    )(*pieces, line, side, cross)
+    return pl.pallas_call(
+        stack_kernel,
+        in_specs=[vmem] * 3 + [pl.BlockSpec(memory_space=pl.ANY)] * 3,
+        out_specs=vmem,
+        out_shape=jax.ShapeDtypeStruct((3,) + pieces[0].shape, pieces[0].dtype),
+        cost_estimate=LIGHT,
+    )(*pieces, *after)
 
 
 def put_in_order(place_ref, own_ref, side_ref, cross_ref, put):
@@ -286,9 +281,9 @@
     near = start.reshape(8, 64, PART)
     near = (near,) + spread(near)
     column = gather_plane(start)
-    rest, line = next_round(column[1:], gather_line(block), near[1], near[2])
+    line = gather_line(block)
     half0 = gather_plane(line)
-    rest = rest.reshape(3, 8, 64, PART)
+    rest = stack_after(column[1:], line, near[1], near[2]).reshape(3, 8, 64, PART)
     half1 = weave(place, near, (rest,) + spread(rest))
 
     delta = -(drift[0] + drift_other) / 2

time: 183 us -> 185 us (1.011)
    all_to_all x1, starting transfers between devices: 5.11 us -> 7.08 us  [scatter_line(): lax.all_to_all((total * scale).astype(jnp.float16), 'z', 0, 0, tiled=True)]
where the time goes in v5:
time: 185 us; the launch traced here: 181 us
  starting transfers between devices  61.7 us (33%)
  waiting for transfers between devices  55.3 us (30%)
  Pallas kernels  36.7 us (20%)
  other arithmetic  16.7 us (9%)
  local copies, waits for them, and re-layouts  9.12 us (5%)
  between operations  1.85 us (1%)
    ppermute x16, starting transfers between devices, shift(): lax.ppermute(value, axis, [(i, (i + step) % size) for i in range(size)])  23.4 us
    ppermute x16, waiting for transfers between devices, shift(): lax.ppermute(value, axis, [(i, (i + step) % size) for i in range(size)])  20.1 us
    pallas_call x6, Pallas kernels, project(): pl.pallas_call(functools.partial(pre_kernel, len(steps)), grid_spec=pltpu...  16.9 us
    all_to_all x1, waiting for transfers between devices, on_device(): lax.all_to_all((whole0 * PART_SCALE).astype(jnp.float16), 'y', 0, 0, tile...  16.4 us
    pallas_call x2, Pallas kernels, gradient(): pl.pallas_call(grad_kernel, grid_spec=pltpu.PrefetchScalarGridSpec(num_sc...  13.3 us
    all_to_all x2, starting transfers between devices, gather_line(): lax.all_to_all(jnp.broadcast_to(block[None], (8, rows, PART)), 'z', 0, 0,...  12 us
    ppermute x3, waiting for transfers between devices, spread(): lax.ppermute(value, ('x', 'c'), SIDE)  7.14 us
    all_to_all x1, starting transfers between devices, scatter_line(): lax.all_to_all((total * scale).astype(jnp.float16), 'z', 0, 0, tiled=True)  7.08 us
  transfers between devices with their start and end apart: 36, of which 12 were waited for; matrix products, arithmetic and copies ran while one was open for 9% of the time, Pallas kernels for 17%

profile of v5, /device:TPU:4, one launch (start us, length us, event | category | flops | bytes accessed | tf_op | source)
XLA Modules:
  0.0 181.3 jit_solution(16660916163383935698)
XLA Ops:
  0.7 0.9 bitcast_convert_fusion
  1.7 0.7 broadcast_in_dim.24
  2.4 8.5 %all-to-all-start = ((bf16[8,64,256]{2,1,0:T(8,128)(2,1)}), bf16[8,64,256]{2,1,0:T(8,128)(2,1)S(1)}, u32[]{:S(2)}, u32[]{:S(2)}) async-start(bf16[8,64,256]{2,1,0:T(8,128)(2,1)} %broadcast_in_dim.24), calls=%async_computation | async-start | bytes 524288 | tf_op jit(solution)/shard_map/all_to_all | solution.py:237
  11.4 2.1 %collective-permute-start.1 = (bf16[64,256]{1,0:T(8,128)(2,1)S(1)}, bf16[64,256]{1,0:T(8,128)(2,1)S(1)}, u32[]{:S(2)}, u32[]{:S(2)}) collective-permute-start(bf16[64,256]{1,0:T(8,128)(2,1)S(1)} %get-tuple-element.33.own_ref), channel_id=1, source_target_pairs={{1,0},{64,65},{0,64},{65,1},{3,2},{66,67},{2,66},{67,3},{5,4},{68,... | collective-permute-start | bytes 98312 | tf_op jit(solution)/shard_map/ppermute | solution.py:35
  13.5 0.7 collective-permute-start.2
  14.8 2.2 %collective-permute-done.1.side_ref = bf16[64,256]{1,0:T(8,128)(2,1)S(1)} collective-permute-done((bf16[64,256]{1,0:T(8,128)(2,1)S(1)}, bf16[64,256]{1,0:T(8,128)(2,1)S(1)}, u32[]{:S(2)}, u32[]{:S(2)}) %collective-permute-start.1) | collective-permute-done | bytes 32800 | tf_op jit(solution)/shard_map/ppermute | solution.py:35
  16.9 1.6 collective-permute-done.3.drift_ref
  18.5 4.9 %all-to-all-done.own0_ref = bf16[8,64,256]{2,1,0:T(8,128)(2,1)S(1)} async-done(((bf16[8,64,256]{2,1,0:T(8,128)(2,1)}), bf16[8,64,256]{2,1,0:T(8,128)(2,1)S(1)}, u32[]{:S(2)}, u32[]{:S(2)}) %all-to-all-start) | async-done | bytes 262176 | tf_op jit(solution)/shard_map/all_to_all | solution.py:237
  23.5 0.7 copy-done.7
  24.1 1.5 shard_map.136
  25.6 1.6 broadcast_in_dim.25
  27.2 3.5 %all-to-all-start.1 = ((bf16[8,128,256]{2,1,0:T(8,128)(2,1)}), bf16[8,128,256]{2,1,0:T(8,128)(2,1)S(1)}, u32[]{:S(2)}, u32[]{:S(2)}) async-start(bf16[8,128,256]{2,1,0:T(8,128)(2,1)} %broadcast_in_dim.25), calls=%async_computation.1 | async-start | bytes 1048576 | tf_op jit(solution)/shard_map/all_to_all | solution.py:237
  30.7 1.3 collective-permute-start.7
  32.0 0.7 collective-permute-start.8
  32.7 3.1 %collective-permute-start.9 = (bf16[512,256]{1,0:T(8,128)(2,1)}, bf16[512,256]{1,0:T(8,128)(2,1)S(1)}, u32[]{:S(2)}, u32[]{:S(2)}) collective-permute-start(bf16[512,256]{1,0:T(8,128)(2,1)} %bitcast.65), channel_id=1, source_target_pairs={{0,48},{16,0},{32,16},{48,32},{1,49},{17,1},{33,17},{49,33},{2,50}... | collective-permute-start | bytes 786440 | tf_op jit(solution)/shard_map/ppermute | solution.py:46
  35.8 0.6 collective-permute-start.10
  36.4 1.0 collective-permute-start.11
  37.6 10.3 %collective-permute-done.9.a_ref = bf16[512,256]{1,0:T(8,128)(2,1)S(1)} collective-permute-done((bf16[512,256]{1,0:T(8,128)(2,1)}, bf16[512,256]{1,0:T(8,128)(2,1)S(1)}, u32[]{:S(2)}, u32[]{:S(2)}) %collective-permute-start.9) | collective-permute-done | bytes 262176 | tf_op jit(solution)/shard_map/ppermute | solution.py:46
  48.0 4.4 %collective-permute-done.11.c_ref = bf16[512,256]{1,0:T(8,128)(2,1)S(1)} collective-permute-done((bf16[512,256]{1,0:T(8,128)(2,1)}, bf16[512,256]{1,0:T(8,128)(2,1)S(1)}, u32[]{:S(2)}, u32[]{:S(2)}) %collective-permute-start.11) | collective-permute-done | bytes 262176 | tf_op jit(solution)/shard_map/ppermute | solution.py:46
  52.4 0.6 copy-done.18
  53.2 2.0 %shard_map.139 = bf16[3,512,256]{2,1,0:T(8,128)(2,1)} custom-call(bf16[512,256]{1,0:T(8,128)(2,1)} %copy-done.16, bf16[512,256]{1,0:T(8,128)(2,1)} %copy-done.17, bf16[512,256]{1,0:T(8,128)(2,1)} %copy-done.18, bf16[1024,256]{1,0:T(8,128)(2,1)} %bitcast.55, bf16[8,64,256]{2,1,0:T(8,128)(2,1)} %copy-done.9, bf16[8,64,256]{2,1,0:T(8,128)(2,1)} %copy-done.11), custom_call_target="tpu_custom_call" | custom-call | flops 1000 | bytes 1000 | tf_op jit(solution)/shard_map/pallas_call | solution.py:56
  55.3 0.7 collective-permute-start.13
  56.5 0.6 collective-permute-start.5
  57.1 1.0 collective-permute-start.6
  58.2 1.0 copy-done.3
  59.2 2.4 %shard_map.137.refs_2_.refs_6_ = f32[640,256]{1,0:T(8,128)S(1)} custom-call(s32[2]{0:T(128)S(1)} %pad_add_fusion.1.place_ref, bf16[640,8192]{1,0:T(8,128)(2,1)} %collective-permute-done.other_ref.refs_0_.refs_1_.refs_2_.refs_3_.xr_ref, bf16[1024,256]{1,0:T(8,128)(2,1)S(1)} %bitcast.59, s32[1]{0:T(128)} %bitcast.1.refs_2_), custom_call_target="tpu_custom_call" | custom-call | flops 1000 | bytes 1000 | tf_op jit(solution)/shard_map/pallas_call | solution.py:151
  61.6 4.0 %copy-done = bf16[640,8192]{1,0:T(8,128)(2,1)S(1)} copy-done((bf16[640,8192]{1,0:T(8,128)(2,1)S(1)}, bf16[640,8192]{1,0:T(8,128)(2,1)}, u32[]{:S(2)}) %copy-start) | copy-done | bytes 10485784
  65.6 1.4 shard_map.138.refs_8_.refs_6_
  67.0 4.7 %collective-permute-done.12.side_ref = bf16[3,8,64,256]{3,2,1,0:T(8,128)(2,1)S(1)} collective-permute-done((bf16[3,8,64,256]{3,2,1,0:T(8,128)(2,1)}, bf16[3,8,64,256]{3,2,1,0:T(8,128)(2,1)S(1)}, u32[]{:S(2)}, u32[]{:S(2)}) %collective-permute-start.12) | collective-permute-done | bytes 786464 | tf_op jit(solution)/shard_map/ppermute | solution.py:35
  71.8 0.7 shard_map.140.refs_4_.refs_5_.refs_6_.refs_7_
  72.5 4.7 %shard_map.141.refs_8_ = f32[640,256]{1,0:T(8,128)S(1)} custom-call(s32[2]{0:T(128)S(1)} %pad_add_fusion.1.place_ref, bf16[640,8192]{1,0:T(8,128)(2,1)} %collective-permute-done.other_ref.refs_0_.refs_1_.refs_2_.refs_3_.xr_ref, bf16[640,8192]{1,0:T(8,128)(2,1)} %collective-permute-done.other_ref.refs_0_.refs_1_.refs_2_.refs_3_.xr_ref, ...), custom_call_target="tpu_custom_call" | custom-call | flops 1000 | bytes 1000 | tf_op jit(solution)/shard_map/pallas_call | solution.py:151
  77.2 3.7 %collective-permute-start.16 = (f32[640,256]{1,0:T(8,128)S(1)}, f32[640,256]{1,0:T(8,128)S(1)}, u32[]{:S(2)}, u32[]{:S(2)}) collective-permute-start(f32[640,256]{1,0:T(8,128)S(1)} %shard_map.141.refs_8_), channel_id=1, source_target_pairs={{0,1},{1,0},{2,3},{3,2},{4,5},{5,4},{6,7},{7,6},{8,9},{9,8},{10,11... | collective-permute-start | bytes 1966088 | tf_op jit(solution)/shard_map/ppermute | solution.py:27
  80.9 2.7 %shard_map.142.refs_7_.own_ref = f32[640,256]{1,0:T(8,128)S(1)} custom-call(s32[2]{0:T(128)S(1)} %pad_add_fusion.1.place_ref, bf16[640,8192]{1,0:T(8,128)(2,1)S(1)} %bitcast.51, bf16[640,8192]{1,0:T(8,128)(2,1)S(1)} %bitcast.51, bf16[640,8192]{1,0:T(8,128)(2,1)S(1)} %bitcast.51, bf16[640,8192]{1,0:T(8,128)(2,1)S(1)} %bitcast.51, ...), custom_call_target="tpu_custom_call" | custom-call | flops 1000 | bytes 1000 | tf_op jit(solution)/shard_map/pallas_call | solution.py:151
  84.2 3.5 %shard_map.143.refs_7_ = f32[640,256]{1,0:T(8,128)S(1)} custom-call(s32[2]{0:T(128)S(1)} %pad_add_fusion.1.place_ref, bf16[640,8192]{1,0:T(8,128)(2,1)} %collective-permute-done.other_ref.refs_0_.refs_1_.refs_2_.refs_3_.xr_ref, bf16[640,8192]{1,0:T(8,128)(2,1)} %collective-permute-done.other_ref.refs_0_.refs_1_.refs_2_.refs_3_.xr_ref, ...), custom_call_target="tpu_custom_call" | custom-call | flops 1000 | bytes 1000 | tf_op jit(solution)/shard_map/pallas_call | solution.py:151
  88.7 2.3 %shard_map.144.own_ref.after_ref = f32[640,256]{1,0:T(8,128)S(1)} custom-call(s32[2]{0:T(128)S(1)} %pad_add_fusion.1.place_ref, bf16[640,8192]{1,0:T(8,128)(2,1)S(1)} %bitcast.51, bf16[640,8192]{1,0:T(8,128)(2,1)S(1)} %bitcast.51, bf16[640,8192]{1,0:T(8,128)(2,1)S(1)} %bitcast.51, bf16[1024,256]{1,0:T(8,128)(2,1)S(1)} %collective-permute-done.4.refs_3_, ...), custom_call_target="tpu_custom_call" | custom-call | flops 1000 | bytes 1000 | tf_op jit(solution)/shard_map/pallas_call | solution.py:151
  91.4 6.6 %shard_map.147 = f32[4096,256]{1,0:T(8,128)S(1)} custom-call(s32[2]{0:T(128)S(1)} %pad_add_fusion.1.place_ref, bf16[640,8192]{1,0:T(8,128)(2,1)S(1)} %bitcast.51, bf16[640,8192]{1,0:T(8,128)(2,1)} %collective-permute-done.other_ref.refs_0_.refs_1_.refs_2_.refs_3_.xr_ref, bf16[640,256]{1,0:T(8,128)(2,1)S(1)} %shard_map.146.eo_ref, ...), custom_call_target="tpu_custom_call" | custom-call | flops 1000 | bytes 1000 | tf_op jit(solution)/shard_map/pallas_call | solution.py:197
  98.1 0.7 multiply_convert_fusion.2
  99.3 1.6 collective-permute-start.20
  100.9 6.7 %shard_map.148 = f32[4096,256]{1,0:T(8,128)S(1)} custom-call(s32[2]{0:T(128)S(1)} %pad_add_fusion.place_ref, bf16[640,8192]{1,0:T(8,128)(2,1)S(1)} %bitcast.51, bf16[640,8192]{1,0:T(8,128)(2,1)} %collective-permute-done.other_ref.refs_0_.refs_1_.refs_2_.refs_3_.xr_ref, bf16[640,256]{1,0:T(8,128)(2,1)S(1)} %shard_map.145.eo_ref, ...), custom_call_target="tpu_custom_call" | custom-call | flops 1000 | bytes 1000 | tf_op jit(solution)/shard_map/pallas_call | solution.py:197
  107.6 2.0 %multiply_convert_fusion = f16[4096,256]{1,0:T(8,128)(2,1)} fusion(f32[4096,256]{1,0:T(8,128)S(1)} %shard_map.148), kind=kLoop, calls=%fused_computation.1 | loop fusion | flops 2097152 | bytes 6291456 | tf_op jit(solution)/shard_map/convert_element_type | solution.py:309
  109.6 4.5 %all-to-all-start.2 = ((f16[4,8,128,256]{3,2,1,0:T(8,128)(2,1)}), f16[4,8,128,256]{3,2,1,0:T(8,128)(2,1)}, u32[]{:S(2)}, u32[]{:S(2)}) async-start(f16[4,8,128,256]{3,2,1,0:T(8,128)(2,1)} %bitcast.11), calls=%async_computation.2 | async-start | bytes 4194304 | tf_op jit(solution)/shard_map/all_to_all | solution.py:309
  114.8 3.2 %multiply_add_fusion = f32[4,8,64,256]{3,2,1,0:T(8,128)S(1)} fusion(f16[4,8,64,256]{3,2,1,0:T(8,128)(2,1)S(1)} %collective-permute-done.21, f16[4,8,64,256]{3,2,1,0:T(8,128)(2,1)} %collective-permute-done.20, pred[]{:T(512)} %bitcast.2, f32[4,8,128,256]{3,2,1,0:T(8,128)} %bitcast.54, pred[]{:T(512)} %bitcast.3), kind=kLoop, calls=%fused_computation.2 | loop fusion | flops 3670016 | bytes 8388610 | tf_op jit(solution)/shard_map/add | solution.py:315
  118.0 1.0 fusion.5
  119.0 3.2 %collective-permute-start.24 = (f16[8,64,256]{2,1,0:T(8,128)(2,1)}, f16[8,64,256]{2,1,0:T(8,128)(2,1)S(1)}, u32[]{:S(2)}, u32[]{:S(2)}) collective-permute-start(f16[8,64,256]{2,1,0:T(8,128)(2,1)} %get-tuple-element.23), channel_id=1, source_target_pairs={{0,48},{16,0},{32,16},{48,32},{1,49},{17,1},{33,17},{49,33},{2,50}... | collective-permute-start | bytes 786440 | tf_op jit(solution)/shard_map/ppermute | solution.py:46
  122.2 2.3 %collective-permute-start.22 = (f16[8,64,256]{2,1,0:T(8,128)(2,1)S(1)}, f16[8,64,256]{2,1,0:T(8,128)(2,1)}, u32[]{:S(2)}, u32[]{:S(2)}) collective-permute-start(f16[8,64,256]{2,1,0:T(8,128)(2,1)S(1)} %get-tuple-element.22), channel_id=1, source_target_pairs={{0,32},{16,48},{32,0},{48,16},{1,33},{17,49},{33,1},{49,17},{2,34}... | collective-permute-start | bytes 786440 | tf_op jit(solution)/shard_map/ppermute | solution.py:46
  124.5 16.4 %all-to-all-done.2 = f16[4,8,128,256]{3,2,1,0:T(8,128)(2,1)} async-done(((f16[4,8,128,256]{3,2,1,0:T(8,128)(2,1)}), f16[4,8,128,256]{3,2,1,0:T(8,128)(2,1)}, u32[]{:S(2)}, u32[]{:S(2)}) %all-to-all-start.2) | async-done | bytes 2097184 | tf_op jit(solution)/shard_map/all_to_all | solution.py:309
  140.9 2.2 %convert_reduce_fusion = f32[8,128,256]{2,1,0:T(8,128)S(1)} fusion(f16[4,8,128,256]{3,2,1,0:T(8,128)(2,1)} %all-to-all-done.2), kind=kLoop, calls=%fused_computation | loop fusion | flops 1835008 | bytes 3145728 | tf_op jit(solution)/shard_map/reduce_sum | solution.py:320
  143.0 0.9 multiply_convert_fusion.3
  143.9 7.1 %all-to-all-start.3 = ((f16[8,128,256]{2,1,0:T(8,128)(2,1)}), f16[8,128,256]{2,1,0:T(8,128)(2,1)S(1)}, u32[]{:S(2)}, u32[]{:S(2)}) async-start(f16[8,128,256]{2,1,0:T(8,128)(2,1)} %multiply_convert_fusion.3), calls=%async_computation.3 | async-start | bytes 1048576 | tf_op jit(solution)/shard_map/all_to_all | solution.py:255
  151.0 0.6 pad_maximum_fusion.s_ref
  151.7 1.8 multiply_subtract_fusion
  153.5 1.1 fusion.4
  154.7 3.3 %collective-permute-start.31 = (f16[64,256]{1,0:T(8,128)(2,1)S(1)}, f16[64,256]{1,0:T(8,128)(2,1)S(1)}, u32[]{:S(2)}, u32[]{:S(2)}) collective-permute-start(f16[64,256]{1,0:T(8,128)(2,1)S(1)} %get-tuple-element.26), channel_id=1, source_target_pairs={{0,14},{2,0},{4,2},{6,4},{8,6},{10,8},{12,10},{14,12},{1,15},{3,1}... | collective-permute-start | bytes 98312 | tf_op jit(solution)/shard_map/ppermute | solution.py:46
  158.1 2.9 %collective-permute-start.29 = (f16[64,256]{1,0:T(8,128)(2,1)S(1)}, f16[64,256]{1,0:T(8,128)(2,1)S(1)}, u32[]{:S(2)}, u32[]{:S(2)}) collective-permute-start(f16[64,256]{1,0:T(8,128)(2,1)S(1)} %get-tuple-element.28), channel_id=1, source_target_pairs={{0,12},{2,14},{4,0},{6,2},{8,4},{10,6},{12,8},{14,10},{1,13},{3,15... | collective-permute-start | bytes 98312 | tf_op jit(solution)/shard_map/ppermute | solution.py:46
  161.0 3.8 %collective-permute-start.27 = (f16[64,256]{1,0:T(8,128)(2,1)S(1)}, f16[64,256]{1,0:T(8,128)(2,1)S(1)}, u32[]{:S(2)}, u32[]{:S(2)}) collective-permute-start(f16[64,256]{1,0:T(8,128)(2,1)S(1)} %get-tuple-element.30), channel_id=1, source_target_pairs={{0,10},{2,12},{4,14},{6,0},{8,2},{10,4},{12,6},{14,8},{1,11},{3,13... | collective-permute-start | bytes 98312 | tf_op jit(solution)/shard_map/ppermute | solution.py:46
  164.8 5.1 %all-to-all-done.3 = f16[8,128,256]{2,1,0:T(8,128)(2,1)S(1)} async-done(((f16[8,128,256]{2,1,0:T(8,128)(2,1)}), f16[8,128,256]{2,1,0:T(8,128)(2,1)S(1)}, u32[]{:S(2)}, u32[]{:S(2)}) %all-to-all-start.3) | async-done | bytes 524320 | tf_op jit(solution)/shard_map/all_to_all | solution.py:255
  170.1 0.9 collective-permute-start.25
  171.0 1.5 collective-permute-start.18
  172.5 0.7 collective-permute-start.19
  173.2 3.8 %collective-permute-done.26 = f16[64,256]{1,0:T(8,128)(2,1)S(1)} collective-permute-done((f16[64,256]{1,0:T(8,128)(2,1)S(1)}, f16[64,256]{1,0:T(8,128)(2,1)S(1)}, u32[]{:S(2)}, u32[]{:S(2)}) %collective-permute-start.26) | collective-permute-done | bytes 32800 | tf_op jit(solution)/shard_map/ppermute | solution.py:46
  177.0 1.1 collective-permute-done.25
  178.1 0.7 fusion.8.g1_ref
  178.7 0.6 select_add_fusion.g0_ref
  179.4 1.9 %shard_map.149 = (f32[64,512]{1,0:T(8,128)}, f32[64,512]{1,0:T(8,128)}, f32[64,512]{1,0:T(8,128)}, f32[64,512]{1,0:T(8,128)}) custom-call(f32[2]{0:T(128)} %pad_maximum_fusion.s_ref, f32[64,256]{1,0:T(8,128)} %select_add_fusion.g0_ref, f32[64,256]{1,0:T(8,128)} %fusion.8.g1_ref, f32[64,512]{1,0:T(8,128)} %bitcast.68, f32[64,512]{1,0:T(8,128)} %bitcast.69, ...), custom_call_target="tpu_custom_call" | custom-call | tf_op jit(solution)/shard_map/pallas_call | solution.py:227
  (96 shorter events, 5.3 us)
Async XLA Ops:
  0.6 22.8 %collective-permute-start = (bf16[640,8192]{1,0:T(8,128)(2,1)}, bf16[640,8192]{1,0:T(8,128)(2,1)}, u32[]{:S(2)}, u32[]{:S(2)}) collective-permute-start(bf16[640,8192]{1,0:T(8,128)(2,1)} %xo_ref.3), channel_id=1, source_target_pairs={{0,1},{1,0},{2,3},{3,2},{4,5},{5,4},{6,7},{7,6},{8,9},{9,8},{10,11... | collective-permute-start | bytes 31457288 | tf_op jit(solution)/shard_map/ppermute | solution.py:27
  1.7 21.7 %copy-start.19 = (bf16[64,256]{1,0:T(8,128)(2,1)}, bf16[64,256]{1,0:T(8,128)(2,1)S(1)}, u32[]{:S(2)}) copy-start(bf16[64,256]{1,0:T(8,128)(2,1)S(1)} %get-tuple-element.33.own_ref) | copy-start | bytes 98308
  2.4 21.0 %all-to-all-start = ((bf16[8,64,256]{2,1,0:T(8,128)(2,1)}), bf16[8,64,256]{2,1,0:T(8,128)(2,1)S(1)}, u32[]{:S(2)}, u32[]{:S(2)}) async-start(bf16[8,64,256]{2,1,0:T(8,128)(2,1)} %broadcast_in_dim.24), calls=%async_computation | async-start | bytes 524288 | tf_op jit(solution)/shard_map/all_to_all | solution.py:237
  10.9 7.6 %collective-permute-start.3 = (f32[64,512]{1,0:T(8,128)}, f32[64,512]{1,0:T(8,128)S(1)}, u32[]{:S(2)}, u32[]{:S(2)}) collective-permute-start(f32[64,512]{1,0:T(8,128)} %bitcast.71), channel_id=1, source_target_pairs={{0,128},{128,0},{1,129},{129,1},{2,130},{130,2},{3,131},{131,3},{4... | collective-permute-start | bytes 393224 | tf_op jit(solution)/shard_map/ppermute | solution.py:27
  11.4 5.5 %collective-permute-start.1 = (bf16[64,256]{1,0:T(8,128)(2,1)S(1)}, bf16[64,256]{1,0:T(8,128)(2,1)S(1)}, u32[]{:S(2)}, u32[]{:S(2)}) collective-permute-start(bf16[64,256]{1,0:T(8,128)(2,1)S(1)} %get-tuple-element.33.own_ref), channel_id=1, source_target_pairs={{1,0},{64,65},{0,64},{65,1},{3,2},{66,67},{2,66},{67,3},{5,4},{68,... | collective-permute-start | bytes 98312 | tf_op jit(solution)/shard_map/ppermute | solution.py:35
  13.5 3.4 %collective-permute-start.2 = (bf16[64,256]{1,0:T(8,128)(2,1)S(1)}, bf16[64,256]{1,0:T(8,128)(2,1)S(1)}, u32[]{:S(2)}, u32[]{:S(2)}) collective-permute-start(bf16[64,256]{1,0:T(8,128)(2,1)S(1)} %get-tuple-element.33.own_ref), channel_id=1, source_target_pairs={{1,64},{64,1},{3,66},{66,3},{5,68},{68,5},{7,70},{70,7},{9,72},{72... | collective-permute-start | bytes 98312 | tf_op jit(solution)/shard_map/ppermute | solution.py:35
  16.9 6.5 %copy-start.20 = (bf16[64,256]{1,0:T(8,128)(2,1)}, bf16[64,256]{1,0:T(8,128)(2,1)S(1)}, u32[]{:S(2)}) copy-start(bf16[64,256]{1,0:T(8,128)(2,1)S(1)} %collective-permute-done.1.side_ref) | copy-start | bytes 98308
  16.9 6.5 %copy-start.21 = (bf16[64,256]{1,0:T(8,128)(2,1)}, bf16[64,256]{1,0:T(8,128)(2,1)S(1)}, u32[]{:S(2)}) copy-start(bf16[64,256]{1,0:T(8,128)(2,1)S(1)} %collective-permute-done.2.cross_ref) | copy-start | bytes 98308
  18.5 4.9 %copy-start.14 = (f32[64,512]{1,0:T(8,128)}, f32[64,512]{1,0:T(8,128)S(1)}, u32[]{:S(2)}) copy-start(f32[64,512]{1,0:T(8,128)S(1)} %collective-permute-done.3.drift_ref) | copy-start | bytes 393220
  23.4 0.7 copy-start.7
  27.2 25.1 %all-to-all-start.1 = ((bf16[8,128,256]{2,1,0:T(8,128)(2,1)}), bf16[8,128,256]{2,1,0:T(8,128)(2,1)S(1)}, u32[]{:S(2)}, u32[]{:S(2)}) async-start(bf16[8,128,256]{2,1,0:T(8,128)(2,1)} %broadcast_in_dim.25), calls=%async_computation.1 | async-start | bytes 1048576 | tf_op jit(solution)/shard_map/all_to_all | solution.py:237
  30.7 6.9 %collective-permute-start.7 = (bf16[8,64,256]{2,1,0:T(8,128)(2,1)}, bf16[8,64,256]{2,1,0:T(8,128)(2,1)S(1)}, u32[]{:S(2)}, u32[]{:S(2)}) collective-permute-start(bf16[8,64,256]{2,1,0:T(8,128)(2,1)} %copy-done.7), channel_id=1, source_target_pairs={{1,0},{64,65},{0,64},{65,1},{3,2},{66,67},{2,66},{67,3},{5,4},{68,... | collective-permute-start | bytes 786440 | tf_op jit(solution)/shard_map/ppermute | solution.py:35
  32.0 5.6 %collective-permute-start.8 = (bf16[8,64,256]{2,1,0:T(8,128)(2,1)}, bf16[8,64,256]{2,1,0:T(8,128)(2,1)S(1)}, u32[]{:S(2)}, u32[]{:S(2)}) collective-permute-start(bf16[8,64,256]{2,1,0:T(8,128)(2,1)} %copy-done.7), channel_id=1, source_target_pairs={{1,64},{64,1},{3,66},{66,3},{5,68},{68,5},{7,70},{70,7},{9,72},{72... | collective-permute-start | bytes 786440 | tf_op jit(solution)/shard_map/ppermute | solution.py:35
  32.7 15.2 %collective-permute-start.9 = (bf16[512,256]{1,0:T(8,128)(2,1)}, bf16[512,256]{1,0:T(8,128)(2,1)S(1)}, u32[]{:S(2)}, u32[]{:S(2)}) collective-permute-start(bf16[512,256]{1,0:T(8,128)(2,1)} %bitcast.65), channel_id=1, source_target_pairs={{0,48},{16,0},{32,16},{48,32},{1,49},{17,1},{33,17},{49,33},{2,50}... | collective-permute-start | bytes 786440 | tf_op jit(solution)/shard_map/ppermute | solution.py:46
  35.8 12.2 %collective-permute-start.10 = (bf16[512,256]{1,0:T(8,128)(2,1)}, bf16[512,256]{1,0:T(8,128)(2,1)S(1)}, u32[]{:S(2)}, u32[]{:S(2)}) collective-permute-start(bf16[512,256]{1,0:T(8,128)(2,1)} %bitcast.66), channel_id=1, source_target_pairs={{0,32},{16,48},{32,0},{48,16},{1,33},{17,49},{33,1},{49,17},{2,34}... | collective-permute-start | bytes 786440 | tf_op jit(solution)/shard_map/ppermute | solution.py:46
  36.4 15.9 %collective-permute-start.11 = (bf16[512,256]{1,0:T(8,128)(2,1)}, bf16[512,256]{1,0:T(8,128)(2,1)S(1)}, u32[]{:S(2)}, u32[]{:S(2)}) collective-permute-start(bf16[512,256]{1,0:T(8,128)(2,1)} %bitcast.67), channel_id=1, source_target_pairs={{0,16},{16,32},{32,48},{48,0},{1,17},{17,33},{33,49},{49,1},{2,18}... | collective-permute-start | bytes 786440 | tf_op jit(solution)/shard_map/ppermute | solution.py:46
  37.6 14.7 %copy-start.9 = (bf16[8,64,256]{2,1,0:T(8,128)(2,1)}, bf16[8,64,256]{2,1,0:T(8,128)(2,1)S(1)}, u32[]{:S(2)}) copy-start(bf16[8,64,256]{2,1,0:T(8,128)(2,1)S(1)} %collective-permute-done.7.side_ref.side0_ref) | copy-start | bytes 786436
  37.6 14.7 %copy-start.11 = (bf16[8,64,256]{2,1,0:T(8,128)(2,1)}, bf16[8,64,256]{2,1,0:T(8,128)(2,1)S(1)}, u32[]{:S(2)}) copy-start(bf16[8,64,256]{2,1,0:T(8,128)(2,1)S(1)} %collective-permute-done.8.cross_ref.cross0_ref) | copy-start | bytes 786436
  47.9 4.4 %copy-start.16 = (bf16[512,256]{1,0:T(8,128)(2,1)}, bf16[512,256]{1,0:T(8,128)(2,1)S(1)}, u32[]{:S(2)}) copy-start(bf16[512,256]{1,0:T(8,128)(2,1)S(1)} %collective-permute-done.9.a_ref) | copy-start | bytes 786436
  48.0 4.4 %copy-start.17 = (bf16[512,256]{1,0:T(8,128)(2,1)}, bf16[512,256]{1,0:T(8,128)(2,1)S(1)}, u32[]{:S(2)}) copy-start(bf16[512,256]{1,0:T(8,128)(2,1)S(1)} %collective-permute-done.10.b_ref) | copy-start | bytes 786436
  52.3 0.7 copy-start.18
  52.3 0.9 copy-start.2
  55.3 16.5 %collective-permute-start.12 = (bf16[3,8,64,256]{3,2,1,0:T(8,128)(2,1)}, bf16[3,8,64,256]{3,2,1,0:T(8,128)(2,1)S(1)}, u32[]{:S(2)}, u32[]{:S(2)}) collective-permute-start(bf16[3,8,64,256]{3,2,1,0:T(8,128)(2,1)} %bitcast.61), channel_id=1, source_target_pairs={{1,0},{64,65},{0,64},{65,1},{3,2},{66,67},{2,66},{67,3},{5,4},{68,... | collective-permute-start | bytes 2359304 | tf_op jit(solution)/shard_map/ppermute | solution.py:35
  55.3 16.5 %collective-permute-start.13 = (bf16[3,8,64,256]{3,2,1,0:T(8,128)(2,1)}, bf16[3,8,64,256]{3,2,1,0:T(8,128)(2,1)S(1)}, u32[]{:S(2)}, u32[]{:S(2)}) collective-permute-start(bf16[3,8,64,256]{3,2,1,0:T(8,128)(2,1)} %bitcast.62), channel_id=1, source_target_pairs={{1,64},{64,1},{3,66},{66,3},{5,68},{68,5},{7,70},{70,7},{9,72},{72... | collective-permute-start | bytes 2359304 | tf_op jit(solution)/shard_map/ppermute | solution.py:35
  56.0 27.7 %collective-permute-start.4 = (bf16[1024,256]{1,0:T(8,128)(2,1)}, bf16[1024,256]{1,0:T(8,128)(2,1)S(1)}, u32[]{:S(2)}, u32[]{:S(2)}) collective-permute-start(bf16[1024,256]{1,0:T(8,128)(2,1)} %bitcast.56), channel_id=1, source_target_pairs={{0,48},{16,0},{32,16},{48,32},{1,49},{17,1},{33,17},{49,33},{2,50}... | collective-permute-start | bytes 1572872 | tf_op jit(solution)/shard_map/ppermute | solution.py:46
  56.5 27.1 %collective-permute-start.5 = (bf16[1024,256]{1,0:T(8,128)(2,1)}, bf16[1024,256]{1,0:T(8,128)(2,1)S(1)}, u32[]{:S(2)}, u32[]{:S(2)}) collective-permute-start(bf16[1024,256]{1,0:T(8,128)(2,1)} %bitcast.57), channel_id=1, source_target_pairs={{0,32},{16,48},{32,0},{48,16},{1,33},{17,49},{33,1},{49,17},{2,34}... | collective-permute-start | bytes 1572872 | tf_op jit(solution)/shard_map/ppermute | solution.py:46
  57.1 27.1 %collective-permute-start.6 = (bf16[1024,256]{1,0:T(8,128)(2,1)}, bf16[1024,256]{1,0:T(8,128)(2,1)S(1)}, u32[]{:S(2)}, u32[]{:S(2)}) collective-permute-start(bf16[1024,256]{1,0:T(8,128)(2,1)} %bitcast.58), channel_id=1, source_target_pairs={{0,16},{16,32},{32,48},{48,0},{1,17},{17,33},{33,49},{49,1},{2,18}... | collective-permute-start | bytes 1572872 | tf_op jit(solution)/shard_map/ppermute | solution.py:46
  58.2 1.0 copy-start.3
  59.2 2.4 %copy-start.4 = (bf16[8,128,256]{2,1,0:T(8,128)(2,1)S(1)}, bf16[8,128,256]{2,1,0:T(8,128)(2,1)}, u32[]{:S(2)}) copy-start(bf16[8,128,256]{2,1,0:T(8,128)(2,1)} %copy-done.2) | copy-start | bytes 1572868
  61.6 4.0 %copy-start = (bf16[640,8192]{1,0:T(8,128)(2,1)S(1)}, bf16[640,8192]{1,0:T(8,128)(2,1)}, u32[]{:S(2)}) copy-start(bf16[640,8192]{1,0:T(8,128)(2,1)} %xo_ref.3) | copy-start | bytes 31457284
  65.6 6.1 %copy-start.5 = (bf16[3,512,256]{2,1,0:T(8,128)(2,1)S(1)}, bf16[3,512,256]{2,1,0:T(8,128)(2,1)}, u32[]{:S(2)}) copy-start(bf16[3,512,256]{2,1,0:T(8,128)(2,1)} %shard_map.139) | copy-start | bytes 2359300
  65.6 6.1 %copy-start.8 = (bf16[8,64,256]{2,1,0:T(8,128)(2,1)S(1)}, bf16[8,64,256]{2,1,0:T(8,128)(2,1)}, u32[]{:S(2)}) copy-start(bf16[8,64,256]{2,1,0:T(8,128)(2,1)} %copy-done.7) | copy-start | bytes 786436
  65.6 6.1 %copy-start.10 = (bf16[8,64,256]{2,1,0:T(8,128)(2,1)S(1)}, bf16[8,64,256]{2,1,0:T(8,128)(2,1)}, u32[]{:S(2)}) copy-start(bf16[8,64,256]{2,1,0:T(8,128)(2,1)} %copy-done.9) | copy-start | bytes 786436
  65.6 6.1 %copy-start.12 = (bf16[8,64,256]{2,1,0:T(8,128)(2,1)S(1)}, bf16[8,64,256]{2,1,0:T(8,128)(2,1)}, u32[]{:S(2)}) copy-start(bf16[8,64,256]{2,1,0:T(8,128)(2,1)} %copy-done.11) | copy-start | bytes 786436
  65.6 6.2 %copy-start.13 = (s32[2]{0:T(128)S(1)}, s32[2]{0:T(128)}, u32[]{:S(2)}) copy-start(s32[2]{0:T(128)} %pad_add_fusion.2.place_ref) | copy-start | bytes 28
  71.8 9.1 %slice-start = ((s8[10485760]{0:T(1024)(128)(4,1)}), s8[4194304]{0:T(1024)(128)(4,1)S(1)}, s32[]{:S(2)}) async-start(s8[10485760]{0:T(1024)(128)(4,1)} %bitcast.50), calls=%async_computation.4 | async-start | bytes 8388608
  72.5 8.4 %slice-start.1 = ((s8[10485760]{0:T(1024)(128)(4,1)}), s8[4194304]{0:T(1024)(128)(4,1)S(1)}, s32[]{:S(2)}) async-start(s8[10485760]{0:T(1024)(128)(4,1)} %bitcast.50), calls=%async_computation.5 | async-start | bytes 8388608
  72.5 8.4 %slice-start.2 = ((s8[10485760]{0:T(1024)(128)(4,1)}), s8[2097152]{0:T(1024)(128)(4,1)S(1)}, s32[]{:S(2)}) async-start(s8[10485760]{0:T(1024)(128)(4,1)} %bitcast.50), calls=%async_computation.6 | async-start | bytes 4194304
  77.2 10.7 %collective-permute-start.16 = (f32[640,256]{1,0:T(8,128)S(1)}, f32[640,256]{1,0:T(8,128)S(1)}, u32[]{:S(2)}, u32[]{:S(2)}) collective-permute-start(f32[640,256]{1,0:T(8,128)S(1)} %shard_map.141.refs_8_), channel_id=1, source_target_pairs={{0,1},{1,0},{2,3},{3,2},{4,5},{5,4},{6,7},{7,6},{8,9},{9,8},{10,11... | collective-permute-start | bytes 1966088 | tf_op jit(solution)/shard_map/ppermute | solution.py:27
  83.6 4.3 %copy-start.6 = (bf16[640,512]{1,0:T(8,128)(2,1)S(1)}, bf16[640,512]{1,0:T(8,128)(2,1)}, u32[]{:S(2)}) copy-start(bf16[640,512]{1,0:T(8,128)(2,1)} %cot_ref.3) | copy-start | bytes 1966084
  87.7 3.3 %collective-permute-start.14 = (f32[640,256]{1,0:T(8,128)S(1)}, f32[640,256]{1,0:T(8,128)S(1)}, u32[]{:S(2)}, u32[]{:S(2)}) collective-permute-start(f32[640,256]{1,0:T(8,128)S(1)} %shard_map.143.refs_7_), channel_id=1, source_target_pairs={{0,1},{1,0},{2,3},{3,2},{4,5},{5,4},{6,7},{7,6},{8,9},{9,8},{10,11... | collective-permute-start | bytes 1966088 | tf_op jit(solution)/shard_map/ppermute | solution.py:27
  88.2 3.3 %collective-permute-start.17 = (bf16[640,256]{1,0:T(8,128)(2,1)S(1)}, bf16[640,256]{1,0:T(8,128)(2,1)S(1)}, u32[]{:S(2)}, u32[]{:S(2)}) collective-permute-start(bf16[640,256]{1,0:T(8,128)(2,1)S(1)} %shard_map.146.eo_ref), channel_id=1, source_target_pairs={{0,1},{1,0},{2,3},{3,2},{4,5},{5,4},{6,7},{7,6},{8,9},{9,8},{10,11... | collective-permute-start | bytes 983048 | tf_op jit(solution)/shard_map/ppermute | solution.py:27
  91.2 9.7 %collective-permute-start.15 = (bf16[640,256]{1,0:T(8,128)(2,1)S(1)}, bf16[640,256]{1,0:T(8,128)(2,1)S(1)}, u32[]{:S(2)}, u32[]{:S(2)}) collective-permute-start(bf16[640,256]{1,0:T(8,128)(2,1)S(1)} %shard_map.145.eo_ref), channel_id=1, source_target_pairs={{0,1},{1,0},{2,3},{3,2},{4,5},{5,4},{6,7},{7,6},{8,9},{9,8},{10,11... | collective-permute-start | bytes 983048 | tf_op jit(solution)/shard_map/ppermute | solution.py:27
  98.1 2.9 %copy-start.1 = (f32[4096,256]{1,0:T(8,128)}, f32[4096,256]{1,0:T(8,128)S(1)}, u32[]{:S(2)}) copy-start(f32[4096,256]{1,0:T(8,128)S(1)} %shard_map.147) | copy-start | bytes 12582916
  98.8 15.9 %collective-permute-start.21 = (f16[4,8,64,256]{3,2,1,0:T(8,128)(2,1)S(1)}, f16[4,8,64,256]{3,2,1,0:T(8,128)(2,1)S(1)}, u32[]{:S(2)}, u32[]{:S(2)}) collective-permute-start(f16[4,8,64,256]{3,2,1,0:T(8,128)(2,1)S(1)} %get-tuple-element.21), channel_id=1, source_target_pairs={{0,1},{65,64},{64,0},{1,65},{2,3},{67,66},{66,2},{3,67},{4,5},{69,... | collective-permute-start | bytes 3145736 | tf_op jit(solution)/shard_map/ppermute | solution.py:40
  99.3 15.5 %collective-permute-start.20 = (f16[4,8,64,256]{3,2,1,0:T(8,128)(2,1)S(1)}, f16[4,8,64,256]{3,2,1,0:T(8,128)(2,1)}, u32[]{:S(2)}, u32[]{:S(2)}) collective-permute-start(f16[4,8,64,256]{3,2,1,0:T(8,128)(2,1)S(1)} %get-tuple-element.20), channel_id=1, source_target_pairs={{64,1},{1,64},{66,3},{3,66},{68,5},{5,68},{70,7},{7,70},{72,9},{9,... | collective-permute-start | bytes 3145736 | tf_op jit(solution)/shard_map/ppermute | solution.py:41
  109.6 31.3 %all-to-all-start.2 = ((f16[4,8,128,256]{3,2,1,0:T(8,128)(2,1)}), f16[4,8,128,256]{3,2,1,0:T(8,128)(2,1)}, u32[]{:S(2)}, u32[]{:S(2)}) async-start(f16[4,8,128,256]{3,2,1,0:T(8,128)(2,1)} %bitcast.11), calls=%async_computation.2 | async-start | bytes 4194304 | tf_op jit(solution)/shard_map/all_to_all | solution.py:309
  119.0 34.5 %collective-permute-start.24 = (f16[8,64,256]{2,1,0:T(8,128)(2,1)}, f16[8,64,256]{2,1,0:T(8,128)(2,1)S(1)}, u32[]{:S(2)}, u32[]{:S(2)}) collective-permute-start(f16[8,64,256]{2,1,0:T(8,128)(2,1)} %get-tuple-element.23), channel_id=1, source_target_pairs={{0,48},{16,0},{32,16},{48,32},{1,49},{17,1},{33,17},{49,33},{2,50}... | collective-permute-start | bytes 786440 | tf_op jit(solution)/shard_map/ppermute | solution.py:46
  122.2 31.3 %collective-permute-start.23 = (f16[8,64,256]{2,1,0:T(8,128)(2,1)}, f16[8,64,256]{2,1,0:T(8,128)(2,1)S(1)}, u32[]{:S(2)}, u32[]{:S(2)}) collective-permute-start(f16[8,64,256]{2,1,0:T(8,128)(2,1)} %get-tuple-element.24), channel_id=1, source_target_pairs={{0,16},{16,32},{32,48},{48,0},{1,17},{17,33},{33,49},{49,1},{2,18}... | collective-permute-start | bytes 786440 | tf_op jit(solution)/shard_map/ppermute | solution.py:46
  122.2 31.3 %collective-permute-start.22 = (f16[8,64,256]{2,1,0:T(8,128)(2,1)S(1)}, f16[8,64,256]{2,1,0:T(8,128)(2,1)}, u32[]{:S(2)}, u32[]{:S(2)}) collective-permute-start(f16[8,64,256]{2,1,0:T(8,128)(2,1)S(1)} %get-tuple-element.22), channel_id=1, source_target_pairs={{0,32},{16,48},{32,0},{48,16},{1,33},{17,49},{33,1},{49,17},{2,34}... | collective-permute-start | bytes 786440 | tf_op jit(solution)/shard_map/ppermute | solution.py:46
  143.0 8.7 %copy-start.15 = (f32[64,512]{1,0:T(8,128)S(1)}, f32[64,512]{1,0:T(8,128)}, u32[]{:S(2)}) copy-start(f32[64,512]{1,0:T(8,128)} %copy-done.14) | copy-start | bytes 393220
  143.9 25.9 %all-to-all-start.3 = ((f16[8,128,256]{2,1,0:T(8,128)(2,1)}), f16[8,128,256]{2,1,0:T(8,128)(2,1)S(1)}, u32[]{:S(2)}, u32[]{:S(2)}) async-start(f16[8,128,256]{2,1,0:T(8,128)(2,1)} %multiply_convert_fusion.3), calls=%async_computation.3 | async-start | bytes 1048576 | tf_op jit(solution)/shard_map/all_to_all | solution.py:255
  154.7 15.3 %collective-permute-start.31 = (f16[64,256]{1,0:T(8,128)(2,1)S(1)}, f16[64,256]{1,0:T(8,128)(2,1)S(1)}, u32[]{:S(2)}, u32[]{:S(2)}) collective-permute-start(f16[64,256]{1,0:T(8,128)(2,1)S(1)} %get-tuple-element.26), channel_id=1, source_target_pairs={{0,14},{2,0},{4,2},{6,4},{8,6},{10,8},{12,10},{14,12},{1,15},{3,1}... | collective-permute-start | bytes 98312 | tf_op jit(solution)/shard_map/ppermute | solution.py:46
  158.0 12.0 %collective-permute-start.30 = (f16[64,256]{1,0:T(8,128)(2,1)S(1)}, f16[64,256]{1,0:T(8,128)(2,1)S(1)}, u32[]{:S(2)}, u32[]{:S(2)}) collective-permute-start(f16[64,256]{1,0:T(8,128)(2,1)S(1)} %get-tuple-element.27), channel_id=1, source_target_pairs={{0,2},{2,4},{4,6},{6,8},{8,10},{10,12},{12,14},{14,0},{1,3},{3,5},... | collective-permute-start | bytes 98312 | tf_op jit(solution)/shard_map/ppermute | solution.py:46
  158.1 12.9 %collective-permute-start.29 = (f16[64,256]{1,0:T(8,128)(2,1)S(1)}, f16[64,256]{1,0:T(8,128)(2,1)S(1)}, u32[]{:S(2)}, u32[]{:S(2)}) collective-permute-start(f16[64,256]{1,0:T(8,128)(2,1)S(1)} %get-tuple-element.28), channel_id=1, source_target_pairs={{0,12},{2,14},{4,0},{6,2},{8,4},{10,6},{12,8},{14,10},{1,13},{3,15... | collective-permute-start | bytes 98312 | tf_op jit(solution)/shard_map/ppermute | solution.py:46
  161.0 11.5 %collective-permute-start.28 = (f16[64,256]{1,0:T(8,128)(2,1)S(1)}, f16[64,256]{1,0:T(8,128)(2,1)S(1)}, u32[]{:S(2)}, u32[]{:S(2)}) collective-permute-start(f16[64,256]{1,0:T(8,128)(2,1)S(1)} %get-tuple-element.29), channel_id=1, source_target_pairs={{0,4},{2,6},{4,8},{6,10},{8,12},{10,14},{12,0},{14,2},{1,5},{3,7},... | collective-permute-start | bytes 98312 | tf_op jit(solution)/shard_map/ppermute | solution.py:46
  161.0 12.2 %collective-permute-start.27 = (f16[64,256]{1,0:T(8,128)(2,1)S(1)}, f16[64,256]{1,0:T(8,128)(2,1)S(1)}, u32[]{:S(2)}, u32[]{:S(2)}) collective-permute-start(f16[64,256]{1,0:T(8,128)(2,1)S(1)} %get-tuple-element.30), channel_id=1, source_target_pairs={{0,10},{2,12},{4,14},{6,0},{8,2},{10,4},{12,6},{14,8},{1,11},{3,13... | collective-permute-start | bytes 98312 | tf_op jit(solution)/shard_map/ppermute | solution.py:46
  170.0 7.0 %collective-permute-start.26 = (f16[64,256]{1,0:T(8,128)(2,1)S(1)}, f16[64,256]{1,0:T(8,128)(2,1)S(1)}, u32[]{:S(2)}, u32[]{:S(2)}) collective-permute-start(f16[64,256]{1,0:T(8,128)(2,1)S(1)} %get-tuple-element.31), channel_id=1, source_target_pairs={{0,6},{2,8},{4,10},{6,12},{8,14},{10,0},{12,2},{14,4},{1,7},{3,9},... | collective-permute-start | bytes 98312 | tf_op jit(solution)/shard_map/ppermute | solution.py:46
  170.1 8.0 %collective-permute-start.25 = (f16[64,256]{1,0:T(8,128)(2,1)S(1)}, f16[64,256]{1,0:T(8,128)(2,1)S(1)}, u32[]{:S(2)}, u32[]{:S(2)}) collective-permute-start(f16[64,256]{1,0:T(8,128)(2,1)S(1)} %get-tuple-element.25), channel_id=1, source_target_pairs={{0,8},{2,10},{4,12},{6,14},{8,0},{10,2},{12,4},{14,6},{1,9},{3,11}... | collective-permute-start | bytes 98312 | tf_op jit(solution)/shard_map/ppermute | solution.py:46
  171.0 7.7 %collective-permute-start.18 = (f32[64,256]{1,0:T(8,128)S(1)}, f32[64,256]{1,0:T(8,128)S(1)}, u32[]{:S(2)}, u32[]{:S(2)}) collective-permute-start(f32[64,256]{1,0:T(8,128)S(1)} %get-tuple-element.18), channel_id=1, source_target_pairs={{0,1},{65,64},{64,0},{1,65},{2,3},{67,66},{66,2},{3,67},{4,5},{69,... | collective-permute-start | bytes 196616 | tf_op jit(solution)/shard_map/ppermute | solution.py:40
  172.5 6.2 %collective-permute-start.19 = (f32[64,256]{1,0:T(8,128)S(1)}, f32[64,256]{1,0:T(8,128)S(1)}, u32[]{:S(2)}, u32[]{:S(2)}) collective-permute-start(f32[64,256]{1,0:T(8,128)S(1)} %get-tuple-element.19), channel_id=1, source_target_pairs={{64,1},{1,64},{66,3},{3,66},{68,5},{5,68},{70,7},{7,70},{72,9},{9,... | collective-permute-start | bytes 196616 | tf_op jit(solution)/shard_map/ppermute | solution.py:41
